TPU v7x, 256 devices: a whole 4x4x8 slice. The times are simulated.
256 devices in a mesh: tok: 8 (over z), proto: 32 (over x, y, core).
Axes of the slice: x: 4, y: 4, z: 8, core: 2. Of those that a mesh axis runs over, the one named last changes fastest.
Arguments:
- teacher_hidden: bfloat16 [16384, 2048], P('tok'), may hold values from -6 to 6
- head_teacher: bfloat16 [2048, 256], P('proto'), may hold values from -0.125 to 0.125
- proto_teacher: bfloat16 [256, 65536], P('tok', 'proto'), may hold values from -1.25 to 1.25
- student_hidden: bfloat16 [2048, 2048], P('tok'), may hold values from -0.0625 to 0.8
- head_student: bfloat16 [2048, 256], P('proto'), may hold values from -0.0625 to 0.0625
- proto_student: bfloat16 [256, 65536], P('tok', 'proto'), may hold values from -0.25 to 0.25
- mask_index: int32 [2048], P('tok'), may hold values from 0 to 2047
- mask_count: int32 [8], replicated, may hold values from 32 to 256, as said below
Outputs:
- row_loss: float32 [2048], P('tok')
- hidden_grad: bfloat16 [2048, 2048], P('tok')
Inputs may be any that keep to these rules, and one draw needn't show every extreme that they name: `mask_index`: a row among the teacher tokens held by the same index of tok. `mask_count`: in every draw one index of tok has all 256 slots live.
All inputs are finite; a program needn't handle non-finite values.
Results may differ from a plain program's by a relative error of at most 0.0056.
Values may be sent and summed in bfloat16 or wider, within the bound.
No kernel may reach another device: no remote copies, remote signals or barrier semaphores. Data moves between devices by JAX's collectives and lax.ppermute only.
A program may use at most 128 MiB of HBM per device.

v0:
```python
import jax
import jax.numpy as jnp
from jax import lax
from jax.sharding import PartitionSpec as P

PROTOS = 65536
ITERS = 3


teacher_temp = 0.07
student_temp = 0.1
norm_eps = 1e-06


def unit_rows(values):
    scale = lax.rsqrt(jnp.sum(values * values, axis=1, keepdims=True) + norm_eps)
    return (values * scale, scale)


def proto_total(values):
    return lax.psum(values, "tok")


def token_total(values):
    return lax.psum(values, "proto")


def shards(
    teacher_hidden,
    head_teacher,
    proto_teacher,
    student_hidden,
    head_student,
    proto_student,
    mask_index,
    mask_count,
):
    tok_count = lax.axis_size("tok")
    tok_index = lax.axis_index("tok")
    tok_dev = teacher_hidden.shape[0]
    slot_dev = student_hidden.shape[0]
    all_tokens = tok_dev * tok_count
    whole_teacher, whole_student = (
        lax.all_gather(proto_teacher, "tok", axis=0, tiled=True),
        lax.all_gather(proto_student, "tok", axis=0, tiled=True),
    )
    full_teacher_head, full_student_head = (
        lax.all_gather(head_teacher, "proto", axis=0, tiled=True),
        lax.all_gather(head_student, "proto", axis=0, tiled=True),
    )
    teacher_neck = jnp.dot(teacher_hidden, full_teacher_head, preferred_element_type=jnp.float32)
    unit_teacher = unit_rows(teacher_neck)[0].astype(jnp.bfloat16)
    student_neck = jnp.dot(student_hidden, full_student_head, preferred_element_type=jnp.float32)
    unit_float, feat_scale = unit_rows(student_neck)
    raw_scores = jnp.dot(unit_teacher, whole_teacher, preferred_element_type=jnp.float32)
    exp_scores = jnp.exp(raw_scores / teacher_temp)
    assign = exp_scores
    for sweep in range(ITERS):
        proto_sums = proto_total(jnp.sum(assign, axis=0))
        assign = assign / (PROTOS * proto_sums[None, :])
        token_sums = token_total(jnp.sum(assign, axis=1))
        assign = assign / (all_tokens * token_sums[:, None])
    targets = jnp.take(assign, mask_index, axis=0) * all_tokens
    slot_ids = jnp.arange(slot_dev, dtype=jnp.int32)
    live_rows = (slot_ids < jnp.take(mask_count, tok_index)).astype(jnp.float32)
    unit_student = unit_float.astype(jnp.bfloat16)
    proto_scale = lax.rsqrt(
        jnp.sum(jnp.square(whole_student.astype(jnp.float32)), axis=0) + norm_eps
    )
    logits = (
        jnp.dot(unit_student, whole_student, preferred_element_type=jnp.float32)
        * proto_scale
        / student_temp
    )
    exp_logits = jnp.exp(logits)
    totals, target_dot = lax.psum(
        (jnp.sum(exp_logits, axis=1), jnp.sum(targets * logits, axis=1)), "proto"
    )
    row_loss = live_rows * (jnp.log(totals) - target_dot)
    logit_grad = (
        live_rows[:, None] * (exp_logits / totals[:, None] - targets) * proto_scale / student_temp
    ).astype(jnp.bfloat16)
    grad_terms = lax.dot_general(
        logit_grad, whole_student, (((1,), (1,)), ((), ())), preferred_element_type=jnp.float32
    )
    unit_grad = lax.psum(grad_terms, "proto")
    inner = jnp.sum(unit_float * unit_grad, axis=1, keepdims=True)
    neck_grad = (feat_scale * (unit_grad - unit_float * inner)).astype(jnp.bfloat16)
    hidden_grad = lax.dot_general(
        neck_grad, full_student_head, (((1,), (1,)), ((), ())), preferred_element_type=jnp.float32
    ).astype(jnp.bfloat16)
    return (row_loss, hidden_grad)


def solution(mesh):
    placed = (
        P("tok", None),
        P("proto", None),
        P("tok", "proto"),
        P("tok", None),
        P("proto", None),
        P("tok", "proto"),
        P("tok"),
        P(),
    )
    return jax.shard_map(
        shards, mesh=mesh, in_specs=placed, out_specs=(P("tok"), P("tok", None)), check_vma=False
    )
```

profile of v0, /device:TPU:1, one launch (start us, length us, event | category | flops | bytes accessed | tf_op | source)
XLA Modules:
  0.0 636.6 jit_solution(17234545089512721534)
XLA Ops:
  7.2 0.0 copy-start
  7.2 0.0 all-gather.7.cloned.1.call-start
  7.2 0.7 all-gather.7.cloned.1.call-update
  7.9 0.0 all-gather.9.cloned.1.call-start
  8.0 0.7 all-gather.9.cloned.1.call-update
  8.7 0.0 all-gather.11.cloned.1.call-start
  8.7 0.7 all-gather.11.cloned.1.call-update
  9.4 0.0 all-gather.5.cloned.1.call-start
  9.4 0.5 all-gather.5.cloned.1.call-update
  10.0 0.0 all-reduce.3.cloned.1.call-start
  10.0 0.7 compare_select_fusion
  10.7 0.7 compare_and_fusion
  11.4 1.2 dynamic-slice.2
  13.3 34.0 %all-gather.7.cloned.1.call-done = bf16[256,2048]{1,0:T(8,128)(2,1)} async-done(((bf16[32,2048]{1,0:T(8,128)(2,1)}), bf16[256,2048]{1,0:T(8,128)(2,1)}) %all-gather.7.cloned.1.call-update) | async-done | bytes 1048592 | tf_op jit(solution)/shard_map/all_gather | solution.py:45
  47.3 1.5 multiply_reduce_fusion.2
  48.7 52.9 %all-gather.9.cloned.1.call-done = bf16[2048,256]{1,0:T(8,128)(2,1)} async-done(((bf16[64,256]{1,0:T(8,128)(2,1)}), bf16[2048,256]{1,0:T(8,128)(2,1)}) %all-gather.9.cloned.1.call-update) | async-done | bytes 1048592 | tf_op jit(solution)/shard_map/all_gather | solution.py:48
  101.6 6.0 multiply_reduce_fusion.1
  107.7 28.4 %all-gather.11.cloned.1.call-done = bf16[256,2048]{1,0:T(8,128)(2,1)} async-done(((bf16[32,2048]{1,0:T(8,128)(2,1)}), bf16[256,2048]{1,0:T(8,128)(2,1)}) %all-gather.11.cloned.1.call-update) | async-done | bytes 1048592 | tf_op jit(solution)/shard_map/all_gather | solution.py:44
  136.1 8.4 %fusion.21 = (f32[2048]{0:T(1024)S(1)}, f32[2048,2048]{1,0:T(8,128)}) fusion(bf16[256,2048]{1,0:T(8,128)(2,1)} %all-gather.11.cloned.1.call-done, f32[2048,256]{0,1:T(8,128)S(1)} %get-tuple-element.20, f32[2048]{0:T(1024)S(1)} %add_rsqrt_fusion), kind=kOutput, calls=%fused_computation.53 | convolution fusion | flops 2156918784 | bytes 19939328 | tf_op jit(solution)/shard_map/dot_general | solution.py:55
  144.4 12.3 %psum.64 = f32[2048]{0:T(1024)S(1)} all-reduce(f32[2048]{0:T(1024)S(1)} %get-tuple-element.21), channel_id=1, replica_groups=mesh['tok'=8,'proto'=32] {'tok'}, use_global_device_ids=true, to_apply=%region_6.0 | all-reduce | flops 2048 | bytes 16384 | tf_op jit(solution)/shard_map/psum | solution.py:21
  156.8 7.0 %divide_reduce_fusion = f32[2048]{0:T(1024)S(1)} fusion(f32[2048,2048]{1,0:T(8,128)} %get-tuple-element.22, f32[2048]{0:T(1024)S(1)} %broadcast_multiply_fusion.5), kind=kLoop, calls=%fused_computation.11 | loop fusion | flops 8386560 | bytes 16793600 | tf_op jit(solution)/shard_map/reduce_sum | solution.py:61
  163.7 72.6 %psum.65 = f32[2048]{0:T(1024)S(1)} all-reduce(f32[2048]{0:T(1024)S(1)} %divide_reduce_fusion), channel_id=1, replica_groups=mesh['tok'=8,'proto'=32] {'proto'}, use_global_device_ids=true, to_apply=%region_8.0 | all-reduce | flops 2048 | bytes 16384 | tf_op jit(solution)/shard_map/psum | solution.py:25
  236.3 7.3 %fusion.7 = f32[2048]{0:T(1024)S(1)} fusion(f32[2048,2048]{1,0:T(8,128)} %get-tuple-element.22, f32[2048]{0:T(1024)S(1)} %broadcast_multiply_fusion.2, f32[2048]{0:T(1024)S(1)} %broadcast_multiply_fusion.5), kind=kLoop, calls=%fused_computation.12 | loop fusion | flops 12580864 | bytes 16801792 | tf_op jit(solution)/shard_map/reduce_sum | solution.py:59
  243.7 11.2 %psum.66 = f32[2048]{0:T(1024)S(1)} all-reduce(f32[2048]{0:T(1024)S(1)} %fusion.7), channel_id=1, replica_groups=mesh['tok'=8,'proto'=32] {'tok'}, use_global_device_ids=true, to_apply=%region_10.0 | all-reduce | flops 2048 | bytes 16384 | tf_op jit(solution)/shard_map/psum | solution.py:21
  254.8 7.7 %fusion.8 = f32[2048]{0:T(1024)S(1)} fusion(f32[2048,2048]{1,0:T(8,128)} %get-tuple-element.22, f32[2048]{0:T(1024)S(1)} %broadcast_multiply_fusion.4, f32[2048]{0:T(1024)S(1)} %broadcast_multiply_fusion.2, f32[2048]{0:T(1024)S(1)} %broadcast_multiply_fusion.5), kind=kLoop, calls=%fused_computation.13 | loop fusion | flops 16775168 | bytes 16809984 | tf_op jit(solution)/shard_map/reduce_sum | solution.py:61
  262.5 67.3 %psum.67 = f32[2048]{0:T(1024)S(1)} all-reduce(f32[2048]{0:T(1024)S(1)} %fusion.8), channel_id=1, replica_groups=mesh['tok'=8,'proto'=32] {'proto'}, use_global_device_ids=true, to_apply=%region_12.0 | all-reduce | flops 2048 | bytes 16384 | tf_op jit(solution)/shard_map/psum | solution.py:25
  329.8 7.9 %fusion.9 = f32[2048]{0:T(1024)S(1)} fusion(f32[2048,2048]{1,0:T(8,128)} %get-tuple-element.22, f32[2048]{0:T(1024)S(1)} %broadcast_multiply_fusion.1, f32[2048]{0:T(1024)S(1)} %broadcast_multiply_fusion.4, f32[2048]{0:T(1024)S(1)} %broadcast_multiply_fusion.2, f32[2048]{0:T(1024)S(1)} %broadcast_multiply_fusion.5), kind=kLoop, calls=%fused_computation.14 | loop fusion | flops 20969472 | bytes 16818176 | tf_op jit(solution)/shard_map/reduce_sum | solution.py:59
  337.8 12.5 %psum.68 = f32[2048]{0:T(1024)S(1)} all-reduce(f32[2048]{0:T(1024)S(1)} %fusion.9), channel_id=1, replica_groups=mesh['tok'=8,'proto'=32] {'tok'}, use_global_device_ids=true, to_apply=%region_14.15 | all-reduce | flops 2048 | bytes 16384 | tf_op jit(solution)/shard_map/psum | solution.py:21
  350.2 8.2 %fusion.10 = f32[2048]{0:T(1024)S(1)} fusion(f32[2048,2048]{1,0:T(8,128)} %get-tuple-element.22, f32[2048]{0:T(1024)S(1)} %broadcast_multiply_fusion.3, f32[2048]{0:T(1024)S(1)} %broadcast_multiply_fusion.1, f32[2048]{0:T(1024)S(1)} %broadcast_multiply_fusion.4, f32[2048]{0:T(1024)S(1)} %broadcast_multiply_fusion.2, f32[2048]{0:T(1024)S(1)} %broadcast_multiply_fusion.5), kind=kLoop, calls=%fused_computation.15 | loop fusion | flops 25163776 | bytes 16826368 | tf_op jit(solution)/shard_map/reduce_sum | solution.py:61
  358.5 67.6 %psum.69 = f32[2048]{0:T(1024)S(1)} all-reduce(f32[2048]{0:T(1024)S(1)} %fusion.10), channel_id=1, replica_groups=mesh['tok'=8,'proto'=32] {'proto'}, use_global_device_ids=true, to_apply=%region_16.17 | all-reduce | flops 2048 | bytes 16384 | tf_op jit(solution)/shard_map/psum | solution.py:25
  426.1 13.0 %fusion.6 = f32[2048,2048]{1,0:T(8,128)} fusion(f32[2048,2048]{1,0:T(8,128)} %get-tuple-element.22, f32[2048]{0:T(1024)S(1)} %broadcast_multiply_fusion, f32[2048]{0:T(1024)S(1)} %broadcast_multiply_fusion.3, f32[2048]{0:T(1024)S(1)} %broadcast_multiply_fusion.1, f32[2048]{0:T(1024)S(1)} %broadcast_multiply_fusion.4, f32[2048]{0:T(1024)S(1)} %broadcast_multiply_fusion.2, ...), kind=kLoop, calls=%fused_computation.9 | loop fusion | flops 25165824 | bytes 33603584 | tf_op jit(solution)/shard_map/div | solution.py:62
  439.1 0.0 copy-start.2
  439.1 0.0 all-gather.5.cloned.1.call-done
  439.1 0.0 copy-done
  439.1 1.9 multiply_reduce_fusion.4
  441.0 0.0 copy-start.1
  441.0 9.5 %gather_fusion = f32[256,2048]{1,0:T(8,128)} fusion(f32[2048,2048]{1,0:T(8,128)} %fusion.6, s32[1024]{0:T(1024)S(1)} %pad_clamp_fusion), kind=kCustom, calls=%fused_computation | custom fusion | bytes 4195328 | tf_op jit(solution)/shard_map/jit(_take)/gather | solution.py:63
  450.5 0.0 copy-done.2
  450.5 3.7 exponential_reduce_fusion
  454.2 62.7 %all-reduce = (f32[256]{0:T(256)S(1)}, f32[256]{0:T(256)S(1)}) all-reduce(f32[256]{0:T(256)S(1)} %get-tuple-element.14, f32[256]{0:T(256)S(1)} %get-tuple-element.13), channel_id=1, replica_groups=mesh['tok'=8,'proto'=32] {'proto'}, use_global_device_ids=true, to_apply=%region_18.19 | all-reduce | flops 512 | bytes 4096 | tf_op jit(solution)/shard_map/psum | solution.py:76
  516.9 3.9 fusion.13
  520.8 0.0 all-reduce.3.cloned.1.call-update
  520.9 0.6 subtract_select_fusion
  521.4 105.2 %all-reduce.3.cloned.1.call-done = f32[256,256]{0,1:T(8,128)} async-done(((f32[256,256]{0,1:T(8,128)}), f32[256,256]{0,1:T(8,128)}) %all-reduce.3.cloned.1.call-update) | async-done | bytes 262160 | tf_op jit(solution)/shard_map/psum | solution.py:86
  626.6 1.0 multiply_reduce_fusion.3
  627.6 0.0 copy-done.1
  627.6 2.4 convolution_convert_fusion
  (11 shorter events, 0.0 us)
Async XLA Ops:
  7.2 432.0 %copy-start = (bf16[256,2048]{1,0:T(8,128)(2,1)S(1)}, bf16[256,2048]{1,0:T(8,128)(2,1)}, u32[]{:S(2)}) copy-start(bf16[256,2048]{1,0:T(8,128)(2,1)} %param.11) | copy-start | bytes 3145732
  7.2 40.1 %all-gather.7.cloned.1.call-start = ((), (), s32[]{:S(2)}) async-start(), calls=%async_computation.1 | async-start | bytes 1179648 | tf_op jit(solution)/shard_map/all_gather | solution.py:45
  7.9 93.7 %all-gather.9.cloned.1.call-start = ((), (), s32[]{:S(2)}) async-start(), calls=%async_computation.2 | async-start | bytes 1081344 | tf_op jit(solution)/shard_map/all_gather | solution.py:48
  8.7 127.4 %all-gather.11.cloned.1.call-start = ((), (), s32[]{:S(2)}) async-start(), calls=%async_computation.3 | async-start | bytes 1179648 | tf_op jit(solution)/shard_map/all_gather | solution.py:44
  9.4 429.7 %all-gather.5.cloned.1.call-start = ((), (), s32[]{:S(2)}) async-start(), calls=%async_computation | async-start | bytes 1081344 | tf_op jit(solution)/shard_map/all_gather | solution.py:49
  10.0 616.6 %all-reduce.3.cloned.1.call-start = ((), (), s32[]{:S(2)}) async-start(), calls=%async_computation.4 | async-start | bytes 524288 | tf_op jit(solution)/shard_map/psum | solution.py:86
  439.1 11.4 %copy-start.2 = (bf16[256,2048]{1,0:T(8,128)(2,1)S(1)}, bf16[256,2048]{1,0:T(8,128)(2,1)}, u32[]{:S(2)}) copy-start(bf16[256,2048]{1,0:T(8,128)(2,1)} %all-gather.7.cloned.1.call-done) | copy-start | bytes 3145732
  441.0 186.6 %copy-start.1 = (bf16[2048,256]{1,0:T(8,128)(2,1)S(1)}, bf16[2048,256]{1,0:T(8,128)(2,1)}, u32[]{:S(2)}) copy-start(bf16[2048,256]{1,0:T(8,128)(2,1)} %all-gather.5.cloned.1.call-done) | copy-start | bytes 3145732
Sparse Core Ops, SparseCore 0:
  9.8 37.4 all-gather.6
  49.8 51.7 all-gather.8
  103.4 32.5 all-gather.10
  138.5 51.8 all-gather.4
  521.0 105.5 all-reduce.2
where the time goes:
time: 637 us
  blocking collectives  306 us (48%)
  waiting for transfers between devices  223 us (35%)
  other arithmetic  55.6 us (9%)
  matrix products  26.3 us (4%)
  between operations  14.6 us (2%)
  local copies, waits for them, and re-layouts  10.7 us (2%)
    psum x3, blocking collectives, token_total(): return lax.psum(values, 'proto')  208 us
    psum x1, waiting for transfers between devices, shards(): unit_grad = lax.psum(grad_terms, 'proto')  105 us
    psum x1, blocking collectives, shards(): lax.psum((jnp.sum(exp_logits, axis=1), jnp.sum(targets * logits, axis=1))...  62.7 us
    all_gather x1, waiting for transfers between devices, shards(): lax.all_gather(head_teacher, 'proto', axis=0, tiled=True)  52.9 us
    psum x3, blocking collectives, proto_total(): return lax.psum(values, 'tok')  35.9 us
    all_gather x1, waiting for transfers between devices, shards(): lax.all_gather(proto_student, 'tok', axis=0, tiled=True)  34 us
    all_gather x1, waiting for transfers between devices, shards(): lax.all_gather(proto_teacher, 'tok', axis=0, tiled=True)  28.4 us
    reduce_sum x3, other arithmetic, shards(): token_sums = token_total(jnp.sum(assign, axis=1))  22.9 us
  transfers between devices with their start and end apart: 5, of which 4 were waited for; matrix products, arithmetic and copies ran while one was open for 11% of the time, Pallas kernels for 0%

commit v1 on v0

v1 whole, which is shorter than its diff:
```python
import jax
import jax.numpy as jnp
from jax import lax
from jax.sharding import PartitionSpec as P

teacher_temp = 0.07
student_temp = 0.1
norm_eps = 1e-06
LOG2E = 1.4426950408889634
f32 = jnp.float32
bf16 = jnp.bfloat16


def unit_rows(values):
    scale = lax.rsqrt(jnp.sum(values * values, axis=1, keepdims=True) + norm_eps)
    return (values * scale, scale)


def exchange(blocks, axis, groups=None):
    return lax.all_to_all(blocks, axis, 0, 0, tiled=True, axis_index_groups=groups)


def copies(values, count):
    return jnp.broadcast_to(values[None], (count,) + values.shape)


def total(values, axis, count):
    return jnp.sum(exchange(copies(values, count), axis), axis=0)


def gather_heads(block, count):
    chips = count // 2
    groups = [[2 * k + c for k in range(chips)] for c in range(2)]
    mine = exchange(copies(block, chips), "proto", groups)
    other = lax.ppermute(mine, "proto", [(i, i ^ 1) for i in range(count)])
    first = lax.axis_index("proto") % 2 == 0
    both = jnp.stack([jnp.where(first, mine, other), jnp.where(first, other, mine)], axis=1)
    return both.reshape(count * block.shape[0], block.shape[1])


def split_dot(left, right):
    high = left.astype(bf16)
    low = (left - high.astype(f32)).astype(bf16)
    dims = (((1,), (1,)), ((), ()))
    return lax.dot_general(high, right, dims, preferred_element_type=f32) + lax.dot_general(
        low, right, dims, preferred_element_type=f32
    )


def shards(
    teacher_hidden,
    head_teacher,
    proto_teacher,
    student_hidden,
    head_student,
    proto_student,
    mask_index,
    mask_count,
):
    toks = lax.axis_size("tok")
    protos = lax.axis_size("proto")
    tok_dev = teacher_hidden.shape[0]
    slot_dev = student_hidden.shape[0]
    width = head_teacher.shape[1]
    whole_teacher = lax.all_gather(proto_teacher, "tok", axis=0, tiled=True)
    heads = gather_heads(jnp.concatenate([head_teacher, head_student], axis=1), protos)
    teacher_neck = jnp.dot(teacher_hidden, heads[:, :width], preferred_element_type=f32)
    unit_teacher = unit_rows(teacher_neck)[0].astype(bf16)
    student_neck = jnp.dot(student_hidden, heads[:, width:], preferred_element_type=f32)
    unit_float, feat_scale = unit_rows(student_neck)
    unit_student = unit_float.astype(bf16)
    chosen = (mask_index[:, None] == jnp.arange(tok_dev, dtype=jnp.int32)[None, :]).astype(bf16)
    unit_masked = jnp.dot(chosen, unit_teacher, preferred_element_type=f32).astype(bf16)

    whole_student = lax.all_gather(
        lax.optimization_barrier((proto_student, whole_teacher))[0], "tok", axis=0, tiled=True
    )

    fold = LOG2E / teacher_temp
    scores = jnp.exp2(jnp.dot(unit_teacher, whole_teacher, preferred_element_type=f32) * fold)
    masked = jnp.exp2(jnp.dot(unit_masked, whole_teacher, preferred_element_type=f32) * fold)
    column = jnp.sum(scores, axis=0)
    scores = scores.astype(bf16)
    for sweep in range(2):
        inverse = 1.0 / total(column, "tok", toks)
        row = jnp.sum(scores.astype(f32) * inverse[None, :], axis=1)
        weight = 1.0 / total(row, "proto", protos)
        column = jnp.sum(scores.astype(f32) * weight[:, None], axis=0)
    inverse = 1.0 / total(column, "tok", toks)

    proto_scale = lax.rsqrt(
        jnp.sum(jnp.square(whole_student.astype(f32)), axis=0) + norm_eps
    ) / student_temp
    logits = jnp.dot(unit_student, whole_student, preferred_element_type=f32) * proto_scale
    exp_logits = jnp.exp(logits)
    grad_soft = split_dot(exp_logits * proto_scale, whole_student)
    goal = masked * inverse[None, :]
    grad_goal = split_dot(goal * proto_scale, whole_student)
    stats = jnp.stack(
        [jnp.sum(exp_logits, axis=1), jnp.sum(goal, axis=1), jnp.sum(goal * logits, axis=1)], axis=1
    )
    stats = jnp.pad(stats, ((0, 0), (0, 125)))
    parts = jnp.concatenate([grad_soft, grad_goal, stats], axis=1)
    share = slot_dev // protos
    parts = parts.reshape(protos, share, 2 * width + 128)
    mine = jnp.sum(exchange(parts, "proto"), axis=0)
    soft_total = mine[:, 2 * width : 2 * width + 1]
    goal_total = mine[:, 2 * width + 1 : 2 * width + 2]
    goal_dot = mine[:, 2 * width + 2 : 2 * width + 3]
    first = lax.axis_index("proto") * share
    slot_ids = first + jnp.arange(share, dtype=jnp.int32)
    live = (slot_ids < jnp.take(mask_count, lax.axis_index("tok"))).astype(f32)[:, None]
    loss = live * (jnp.log(soft_total) - goal_dot / goal_total)
    unit_grad = live * (mine[:, :width] / soft_total - mine[:, width : 2 * width] / goal_total)
    my_unit = lax.dynamic_slice_in_dim(unit_float, first, share, 0)
    my_scale = lax.dynamic_slice_in_dim(feat_scale, first, share, 0)
    inner = jnp.sum(my_unit * unit_grad, axis=1, keepdims=True)
    neck_grad = (my_scale * (unit_grad - my_unit * inner)).astype(bf16)
    top = loss.astype(bf16)
    rest = loss - top.astype(f32)
    mid = rest.astype(bf16)
    low = (rest - mid.astype(f32)).astype(bf16)
    final = jnp.concatenate(
        [neck_grad, top, mid, low, jnp.zeros((share, 125), bf16)], axis=1
    )
    final = exchange(copies(final, protos), "proto").reshape(slot_dev, width + 128)
    tail = final[:, width : width + 3].astype(f32)
    row_loss = tail[:, 0] + tail[:, 1] + tail[:, 2]
    hidden_grad = lax.dot_general(
        final[:, :width], heads[:, width:], (((1,), (1,)), ((), ())), preferred_element_type=f32
    ).astype(bf16)
    return (row_loss, hidden_grad)


def solution(mesh):
    placed = (
        P("tok", None),
        P("proto", None),
        P("tok", "proto"),
        P("tok", None),
        P("proto", None),
        P("tok", "proto"),
        P("tok"),
        P(),
    )
    return jax.shard_map(
        shards, mesh=mesh, in_specs=placed, out_specs=(P("tok"), P("tok", None)), check_vma=False
    )
```

time: 637 us -> 227 us (0.36)
  blocking collectives: 306 us -> 68.8 us
  waiting for transfers between devices: 223 us -> 60.1 us
  other arithmetic: 55.6 us -> 31.9 us
  starting transfers between devices: 0.19 us -> 19.5 us
    psum x7 -> x0, blocking collectives: 306 us -> none  [the longest x3 208 us: token_total(): return lax.psum(values, 'proto')]
    psum x1 -> x0, waiting for transfers between devices: 105 us -> none  [shards(): unit_grad = lax.psum(grad_terms, 'proto')]
    all_gather x4 -> x2, waiting for transfers between devices: 115 us -> 24.2 us  [the longest x1 24.2 us: shards(): whole_teacher = lax.all_gather(proto_teacher, 'tok', axis=0, tiled=True)]
    all_to_all x0 -> x4, blocking collectives: none -> 68.8 us  [exchange(): lax.all_to_all(blocks, axis, 0, 0, tiled=True, axis_index_groups=groups)]
    all_to_all x0 -> x4, waiting for transfers between devices: none -> 32.9 us  [exchange(): lax.all_to_all(blocks, axis, 0, 0, tiled=True, axis_index_groups=groups)]
    all_to_all x0 -> x4, starting transfers between devices: none -> 17.5 us  [exchange(): lax.all_to_all(blocks, axis, 0, 0, tiled=True, axis_index_groups=groups)]
    div x1 -> x6, other arithmetic: 13 us -> 0.04 us  [the longest x3 0.02 us: shards(): inverse = 1.0 / total(column, 'tok', toks)]
    reduce_sum x7 -> x12, other arithmetic: 40.6 us -> 28.8 us  [the longest x2 15.3 us: shards(): row = jnp.sum(scores.astype(f32) * inverse[None, :], axis=1)]
  transfers between devices with their start and end apart: 5 -> 7, of which waited for: 4 -> 6; matrix products, arithmetic and copies ran while one was open for 11% -> 9% of each run, Pallas kernels for 0% -> 0%
where the time goes in v1:
time: 227 us; the launch traced here: 226 us
  blocking collectives  68.8 us (30%)
  waiting for transfers between devices  60.1 us (26%)
  other arithmetic  31.9 us (14%)
  matrix products  20.8 us (9%)
  starting transfers between devices  19.5 us (9%)
  between operations  15.1 us (7%)
  local copies, waits for them, and re-layouts  9.98 us (4%)
    all_to_all x4, blocking collectives, exchange(): lax.all_to_all(blocks, axis, 0, 0, tiled=True, axis_index_groups=groups)  68.8 us
    all_to_all x4, waiting for transfers between devices, exchange(): lax.all_to_all(blocks, axis, 0, 0, tiled=True, axis_index_groups=groups)  32.9 us
    all_gather x1, waiting for transfers between devices, shards(): whole_teacher = lax.all_gather(proto_teacher, 'tok', axis=0, tiled=True)  24.2 us
    all_to_all x4, starting transfers between devices, exchange(): lax.all_to_all(blocks, axis, 0, 0, tiled=True, axis_index_groups=groups)  17.5 us
    reduce_sum x2, other arithmetic, shards(): row = jnp.sum(scores.astype(f32) * inverse[None, :], axis=1)  15.3 us
    reduce_sum x2, other arithmetic, shards(): column = jnp.sum(scores.astype(f32) * weight[:, None], axis=0)  10.2 us
    dot_general x1, matrix products, shards(): jnp.dot(unit_teacher, whole_teacher, preferred_element_type=f32) * fold  8.36 us
  transfers between devices with their start and end apart: 7, of which 6 were waited for; matrix products, arithmetic and copies ran while one was open for 9% of the time, Pallas kernels for 0%

profile of v1, /device:TPU:1, one launch (start us, length us, event | category | flops | bytes accessed | tf_op | source)
XLA Modules:
  0.0 226.2 jit_solution(12386701098694458322)
XLA Ops:
  7.2 0.0 all-gather.3.cloned.1.call-start
  7.2 0.9 pad_maximum_fusion.2
  8.1 0.1 broadcast_in_dim.19
  8.2 23.3 %all_to_all.45 = bf16[16,64,512]{2,1,0:T(8,128)(2,1)S(1)} all-to-all(bf16[16,64,512]{2,1,0:T(8,128)(2,1)S(1)} %broadcast_in_dim.19), channel_id=1, replica_groups={{0,2,4,6,8,10,12,14,16,18,20,22,24,26,28,30},{1,3,5,7,9,11,13,15,17,19,..., dimensions={0} | all-to-all | bytes 2097152 | tf_op jit(solution)/shard_map/all_to_all | solution.py:20
  31.4 1.9 collective-permute-start
  33.4 2.2 collective-permute-done
  35.7 0.1 select_bitcast_fusion.1
  35.8 0.2 pad_maximum_fusion
  36.0 3.8 %copy-done.8 = bf16[2048,2048]{1,0:T(8,128)(2,1)S(1)} copy-done((bf16[2048,2048]{1,0:T(8,128)(2,1)S(1)}, bf16[2048,2048]{1,0:T(8,128)(2,1)}, u32[]{:S(2)}) %copy-start.8) | copy-done | bytes 8388632
  39.8 2.4 %multiply_reduce_fusion.1 = (f32[2048]{0:T(1024)S(1)}, f32[256,2048]{1,0:T(8,128)S(1)}) fusion(bf16[2048,2048]{1,0:T(8,128)(2,1)S(1)} %copy-done.8, bf16[2048,512]{1,0:T(8,128)(2,1)S(1)} %bitcast.36), kind=kOutput, calls=%fused_computation.20 | convolution fusion | flops 2148530176 | bytes 11542528 | tf_op jit(solution)/shard_map/dot_general | solution.py:67
  42.2 24.2 %all-gather.3.cloned.1.call-done = bf16[256,2048]{1,0:T(8,128)(2,1)} async-done(((bf16[32,2048]{1,0:T(8,128)(2,1)}), bf16[256,2048]{1,0:T(8,128)(2,1)}) %all-gather.3.cloned.1.call-update) | async-done | bytes 1048592 | tf_op jit(solution)/shard_map/all_gather | solution.py:65
  66.4 8.4 %fusion.4 = (f32[2048]{0:T(1024)S(1)}, f32[2048,2048]{1,0:T(8,128)}) fusion(bf16[256,2048]{1,0:T(8,128)(2,1)} %all-gather.3.cloned.1.call-done, f32[256,2048]{1,0:T(8,128)S(1)} %get-tuple-element.34, f32[2048]{0:T(1024)S(1)} %add_rsqrt_fusion), kind=kOutput, calls=%fused_computation.9 | convolution fusion | flops 2156918784 | bytes 19939328 | tf_op jit(solution)/shard_map/dot_general | solution.py:80
  74.8 11.6 %all_to_all.46 = f32[8,1,2048]{2,1,0:T(1,128)S(1)} all-to-all(f32[8,1,2048]{2,1,0:T(1,128)S(1)} %broadcast_in_dim.21), channel_id=1, replica_groups=mesh['tok'=8,'proto'=32] {'tok'}, dimensions={0} | all-to-all | bytes 131072 | tf_op jit(solution)/shard_map/all_to_all | solution.py:20
  86.5 0.1 reduce_sum.166
  86.5 10.0 %fusion = (f32[2048]{0:T(1024)S(1)}, bf16[2048,2048]{1,0:T(8,128)(2,1)}) fusion(f32[2048]{0:T(1024)S(1)} %broadcast_divide_fusion.4, f32[2048,2048]{1,0:T(8,128)} %get-tuple-element.36), kind=kLoop, calls=%fused_computation.4 | loop fusion | flops 20969472 | bytes 25182208 | tf_op jit(solution)/shard_map/reduce_sum | solution.py:86
  96.6 0.1 broadcast_in_dim.22
  96.7 22.2 %all_to_all.47 = f32[32,1,2048]{2,1,0:T(1,128)S(1)} all-to-all(f32[32,1,2048]{2,1,0:T(1,128)S(1)} %broadcast_in_dim.22), channel_id=1, replica_groups=mesh['tok'=8,'proto'=32] {'proto'}, dimensions={0} | all-to-all | bytes 524288 | tf_op jit(solution)/shard_map/all_to_all | solution.py:20
  118.9 0.2 reduce_sum.168
  119.1 5.1 %fusion.1 = f32[2048]{0:T(1024)S(1)} fusion(bf16[2048,2048]{1,0:T(8,128)(2,1)} %get-tuple-element.23, f32[2048]{0:T(1024)S(1)} %broadcast_divide_fusion.3), kind=kLoop, calls=%fused_computation.5 | loop fusion | flops 12580864 | bytes 8404992 | tf_op jit(solution)/shard_map/reduce_sum | solution.py:88
  124.2 0.7 broadcast_in_dim.23
  124.8 3.4 %all-to-all-start.3 = ((f32[8,1,2048]{2,1,0:T(1,128)}), f32[8,1,2048]{2,1,0:T(1,128)S(1)}, u32[]{:S(2)}, u32[]{:S(2)}) async-start(f32[8,1,2048]{2,1,0:T(1,128)} %broadcast_in_dim.23), calls=%async_computation.3 | async-start | bytes 131072 | tf_op jit(solution)/shard_map/all_to_all | solution.py:20
  128.2 0.0 all-gather.5.cloned.1.call-start
  128.2 0.7 all-gather.5.cloned.1.call-update
  128.9 6.3 %all-to-all-done.3 = f32[8,1,2048]{2,1,0:T(1,128)S(1)} async-done(((f32[8,1,2048]{2,1,0:T(1,128)}), f32[8,1,2048]{2,1,0:T(1,128)S(1)}, u32[]{:S(2)}, u32[]{:S(2)}) %all-to-all-start.3) | async-done | bytes 65568 | tf_op jit(solution)/shard_map/all_to_all | solution.py:20
  135.2 0.1 reduce_sum.170
  135.3 5.3 %fusion.2 = f32[2048]{0:T(1024)S(1)} fusion(bf16[2048,2048]{1,0:T(8,128)(2,1)} %get-tuple-element.23, f32[2048]{0:T(1024)S(1)} %broadcast_divide_fusion.2), kind=kLoop, calls=%fused_computation.6 | loop fusion | flops 12580864 | bytes 8404992 | tf_op jit(solution)/shard_map/reduce_sum | solution.py:86
  140.6 0.9 broadcast_in_dim.24
  141.4 5.0 %all-to-all-start.4 = ((f32[32,1,2048]{2,1,0:T(1,128)}), f32[32,1,2048]{2,1,0:T(1,128)S(1)}, u32[]{:S(2)}, u32[]{:S(2)}) async-start(f32[32,1,2048]{2,1,0:T(1,128)} %broadcast_in_dim.24), calls=%async_computation.4 | async-start | bytes 524288 | tf_op jit(solution)/shard_map/all_to_all | solution.py:20
  146.5 1.1 multiply_reduce_fusion.3
  147.6 7.9 %all-to-all-done.4 = f32[32,1,2048]{2,1,0:T(1,128)S(1)} async-done(((f32[32,1,2048]{2,1,0:T(1,128)}), f32[32,1,2048]{2,1,0:T(1,128)S(1)}, u32[]{:S(2)}, u32[]{:S(2)}) %all-to-all-start.4) | async-done | bytes 262176 | tf_op jit(solution)/shard_map/all_to_all | solution.py:20
  155.6 0.2 reduce_sum.172
  155.8 5.2 %fusion.3 = f32[2048]{0:T(1024)S(1)} fusion(bf16[2048,2048]{1,0:T(8,128)(2,1)} %get-tuple-element.23, f32[2048]{0:T(1024)S(1)} %broadcast_divide_fusion.1), kind=kLoop, calls=%fused_computation.7 | loop fusion | flops 12580864 | bytes 8404992 | tf_op jit(solution)/shard_map/reduce_sum | solution.py:88
  160.9 0.7 broadcast_in_dim.25
  161.6 3.3 %all-to-all-start.5 = ((f32[8,1,2048]{2,1,0:T(1,128)}), f32[8,1,2048]{2,1,0:T(1,128)S(1)}, u32[]{:S(2)}, u32[]{:S(2)}) async-start(f32[8,1,2048]{2,1,0:T(1,128)} %broadcast_in_dim.25), calls=%async_computation.5 | async-start | bytes 131072 | tf_op jit(solution)/shard_map/all_to_all | solution.py:20
  164.9 0.1 broadcast_multiply_fusion
  165.1 6.9 %all-to-all-done.5 = f32[8,1,2048]{2,1,0:T(1,128)S(1)} async-done(((f32[8,1,2048]{2,1,0:T(1,128)}), f32[8,1,2048]{2,1,0:T(1,128)S(1)}, u32[]{:S(2)}, u32[]{:S(2)}) %all-to-all-start.5) | async-done | bytes 65568 | tf_op jit(solution)/shard_map/all_to_all | solution.py:20
  172.0 0.1 reduce_sum.174
  172.1 3.2 %fusion.7 = f32[256,2048]{1,0:T(8,128)S(1)} fusion(bf16[256,2048]{1,0:T(8,128)(2,1)} %all-gather.3.cloned.1.call-done, f32[2048]{0:T(1024)S(1)} %broadcast_divide_fusion, s32[256]{0:T(256)S(1)} %copy-done.7, f32[256,2048]{1,0:T(8,128)} %copy-done.2, f32[2048]{0:T(1024)S(1)} %add_rsqrt_fusion), kind=kOutput, calls=%fused_computation.13 | convolution fusion | flops 539557888 | bytes 5260288 | tf_op jit(solution)/shard_map/dot_general | solution.py:81
  175.3 1.5 multiply_reduce_fusion.2
  176.8 2.1 exponential_reduce_fusion
  178.9 0.5 fusion.15
  179.5 0.6 fusion.14
  180.0 0.5 fusion.11
  180.5 0.5 fusion.12
  181.1 0.9 pad_maximum_fusion.1
  182.0 2.3 %copy.39 = f32[256,640]{1,0:T(8,128)} copy(f32[256,640]{0,1:T(8,128)} %pad_maximum_fusion.1) | data formatting | bytes 1310720 | tf_op jit(solution)/shard_map/concatenate | solution.py:103
  184.3 5.7 %all-to-all-start.6 = ((f32[32,8,640]{2,1,0:T(8,128)}), f32[32,8,640]{2,1,0:T(8,128)}, u32[]{:S(2)}, u32[]{:S(2)}) async-start(f32[32,8,640]{2,1,0:T(8,128)} %bitcast.39), calls=%async_computation.6 | async-start | bytes 1310720 | tf_op jit(solution)/shard_map/all_to_all | solution.py:20
  190.0 0.6 dynamic-slice.10
  191.3 0.1 dynamic-slice.6
  191.4 11.8 %all-to-all-done.6 = f32[32,8,640]{2,1,0:T(8,128)} async-done(((f32[32,8,640]{2,1,0:T(8,128)}), f32[32,8,640]{2,1,0:T(8,128)}, u32[]{:S(2)}, u32[]{:S(2)}) %all-to-all-start.6) | async-done | bytes 655392 | tf_op jit(solution)/shard_map/all_to_all | solution.py:20
  203.1 1.1 reduce_sum.178
  204.3 0.1 fusion.40
  204.3 0.1 copy.51
  204.4 0.1 copy.52
  204.5 0.1 copy.53
  204.6 0.1 copy.43
  204.7 0.1 copy.44
  204.8 0.1 copy.45
  204.9 0.2 fusion.33
  205.1 0.1 fusion.36
  205.2 0.1 concatenate.11
  205.3 11.8 %all_to_all.48 = bf16[32,8,384]{2,1,0:T(8,128)(2,1)S(1)} all-to-all(bf16[32,8,384]{2,1,0:T(8,128)(2,1)S(1)} %broadcast_in_dim.27), channel_id=1, replica_groups=mesh['tok'=8,'proto'=32] {'proto'}, dimensions={0} | all-to-all | bytes 393216 | tf_op jit(solution)/shard_map/all_to_all | solution.py:20
  217.1 1.4 convolution_convert_fusion
  218.5 0.8 fusion.29
  (37 shorter events, 0.3 us)
Async XLA Ops:
  7.2 139.3 %copy-start = (bf16[256,2048]{1,0:T(8,128)(2,1)S(1)}, bf16[256,2048]{1,0:T(8,128)(2,1)}, u32[]{:S(2)}) copy-start(bf16[256,2048]{1,0:T(8,128)(2,1)} %param.11) | copy-start | bytes 3145732
  7.2 59.3 %all-gather.3.cloned.1.call-start = ((), (), s32[]{:S(2)}) async-start(), calls=%async_computation.8 | async-start | bytes 1179648 | tf_op jit(solution)/shard_map/all_gather | solution.py:65
  31.4 4.2 %collective-permute-start = (bf16[16,64,512]{2,1,0:T(8,128)(2,1)S(1)}, bf16[16,64,512]{2,1,0:T(8,128)(2,1)S(1)}, u32[]{:S(2)}, u32[]{:S(2)}) collective-permute-start(bf16[16,64,512]{2,1,0:T(8,128)(2,1)S(1)} %all_to_all.45), channel_id=1, source_target_pairs={{0,1},{1,0},{2,3},{3,2},{4,5},{5,4},{6,7},{7,6},{8,9},{9,8},{10,11... | collective-permute-start | bytes 3145736 | tf_op jit(solution)/shard_map/ppermute | solution.py:35
  35.7 4.1 %copy-start.8 = (bf16[2048,2048]{1,0:T(8,128)(2,1)S(1)}, bf16[2048,2048]{1,0:T(8,128)(2,1)}, u32[]{:S(2)}) copy-start(bf16[2048,2048]{1,0:T(8,128)(2,1)} %param.8) | copy-start | bytes 25165828
  36.0 6.2 %copy-start.3 = (bf16[16,2,64,512]{3,2,1,0:T(8,128)(2,1)}, bf16[16,2,64,512]{3,2,1,0:T(8,128)(2,1)S(1)}, u32[]{:S(2)}) copy-start(bf16[16,2,64,512]{3,2,1,0:T(8,128)(2,1)S(1)} %pad_maximum_fusion) | copy-start | bytes 6291460
  42.2 32.6 %copy-start.2 = (f32[256,2048]{1,0:T(8,128)}, f32[256,2048]{1,0:T(8,128)S(1)}, u32[]{:S(2)}) copy-start(f32[256,2048]{1,0:T(8,128)S(1)} %get-tuple-element.34) | copy-start | bytes 6291460
  124.8 10.4 %all-to-all-start.3 = ((f32[8,1,2048]{2,1,0:T(1,128)}), f32[8,1,2048]{2,1,0:T(1,128)S(1)}, u32[]{:S(2)}, u32[]{:S(2)}) async-start(f32[8,1,2048]{2,1,0:T(1,128)} %broadcast_in_dim.23), calls=%async_computation.3 | async-start | bytes 131072 | tf_op jit(solution)/shard_map/all_to_all | solution.py:20
  128.2 47.1 %all-gather.5.cloned.1.call-start = ((), (), s32[]{:S(2)}) async-start(), calls=%async_computation.9 | async-start | bytes 1179648 | tf_op jit(solution)/shard_map/all_gather | solution.py:75
  135.3 11.2 %copy-start.4 = (bf16[16,2,64,512]{3,2,1,0:T(8,128)(2,1)S(1)}, bf16[16,2,64,512]{3,2,1,0:T(8,128)(2,1)}, u32[]{:S(2)}) copy-start(bf16[16,2,64,512]{3,2,1,0:T(8,128)(2,1)} %copy-done.3) | copy-start | bytes 6291460
  141.4 14.1 %all-to-all-start.4 = ((f32[32,1,2048]{2,1,0:T(1,128)}), f32[32,1,2048]{2,1,0:T(1,128)S(1)}, u32[]{:S(2)}, u32[]{:S(2)}) async-start(f32[32,1,2048]{2,1,0:T(1,128)} %broadcast_in_dim.24), calls=%async_computation.4 | async-start | bytes 524288 | tf_op jit(solution)/shard_map/all_to_all | solution.py:20
  155.7 9.2 %copy-start.6 = (f32[256,256]{0,1:T(8,128)S(1)}, f32[256,256]{0,1:T(8,128)}, u32[]{:S(2)}) copy-start(f32[256,256]{0,1:T(8,128)} %get-tuple-element.32) | copy-start | bytes 786436
  155.8 16.3 %copy-start.7 = (s32[256]{0:T(256)S(1)}, s32[256]{0:T(256)}, u32[]{:S(2)}) copy-start(s32[256]{0:T(256)} %param.14) | copy-start | bytes 3076
  161.6 10.4 %all-to-all-start.5 = ((f32[8,1,2048]{2,1,0:T(1,128)}), f32[8,1,2048]{2,1,0:T(1,128)S(1)}, u32[]{:S(2)}, u32[]{:S(2)}) async-start(f32[8,1,2048]{2,1,0:T(1,128)} %broadcast_in_dim.25), calls=%async_computation.5 | async-start | bytes 131072 | tf_op jit(solution)/shard_map/all_to_all | solution.py:20
  176.8 2.2 copy-start.1
  181.1 9.0 %copy-start.9 = (s32[8]{0:T(128)S(1)}, s32[8]{0:T(128)}, u32[]{:S(2)}) copy-start(s32[8]{0:T(128)} %param.15) | copy-start | bytes 100
  182.0 35.1 %copy-start.5 = (bf16[16,2,64,512]{3,2,1,0:T(8,128)(2,1)S(1)}, bf16[16,2,64,512]{3,2,1,0:T(8,128)(2,1)}, u32[]{:S(2)}) copy-start(bf16[16,2,64,512]{3,2,1,0:T(8,128)(2,1)} %copy-done.3) | copy-start | bytes 6291460
  184.3 18.8 %all-to-all-start.6 = ((f32[32,8,640]{2,1,0:T(8,128)}), f32[32,8,640]{2,1,0:T(8,128)}, u32[]{:S(2)}, u32[]{:S(2)}) async-start(f32[32,8,640]{2,1,0:T(8,128)} %bitcast.39), calls=%async_computation.6 | async-start | bytes 1310720 | tf_op jit(solution)/shard_map/all_to_all | solution.py:20
Sparse Core Ops, SparseCore 0:
  33.5 32.8 all-gather.2
  130.8 31.1 all-gather.4

commit v2 on v0

v2 whole, which is shorter than its diff:
```python
import jax
import jax.numpy as jnp
from jax import lax
from jax.experimental import pallas as pl
from jax.experimental.pallas import tpu as pltpu
from jax.sharding import PartitionSpec as P

teacher_temp = 0.07
student_temp = 0.1
norm_eps = 1e-06
LOG2E = 1.4426950408889634
MIB = 1024 * 1024
f32 = jnp.float32
bf16 = jnp.bfloat16
VM = pl.BlockSpec(memory_space=pltpu.VMEM)
SM = pl.BlockSpec(memory_space=pltpu.SMEM)
HB = pl.BlockSpec(memory_space=pltpu.HBM)
ANY = pl.BlockSpec(memory_space=pl.ANY)
NT = (((1,), (1,)), ((), ()))


def shaped(shape, dtype):
    return jax.ShapeDtypeStruct(shape, dtype)


def call(kernel, out_shape, in_specs, out_specs, cost, scratch=(), mib=40):
    return pl.pallas_call(
        kernel,
        out_shape=out_shape,
        in_specs=in_specs,
        out_specs=out_specs,
        scratch_shapes=list(scratch),
        cost_estimate=pl.CostEstimate(flops=cost[0], bytes_accessed=cost[1], transcendentals=0),
        compiler_params=pltpu.CompilerParams(vmem_limit_bytes=mib * MIB),
    )


def held(values):
    return pltpu.with_memory_space_constraint(values, pltpu.VMEM)


def dot(left, right, dims=(((1,), (0,)), ((), ()))):
    return lax.dot_general(left, right, dims, preferred_element_type=f32)


def split(values):
    high = values.astype(bf16)
    return high, (values - high.astype(f32)).astype(bf16)


def fetch(pairs, sems, first=0):
    copies = [
        pltpu.make_async_copy(source, target, sems.at[first + k])
        for k, (source, target) in enumerate(pairs)
    ]
    for copy in copies:
        copy.start()
    return copies


def settle(copies):
    for copy in copies:
        copy.wait()


def heads_kernel(teacher, student, first, second, copies, both, v_teacher, v_student, sems):
    rows, width = first.shape[0], teacher.shape[1]
    heads = fetch([(teacher, v_teacher), (student, v_student)], sems)
    rest = fetch(
        [(first, both.at[pl.ds(0, rows), :]), (second, both.at[pl.ds(rows, rows), :])], sems, 2
    )
    settle(heads)
    copies[:, :, :width] = jnp.broadcast_to(v_teacher[...][None], copies.shape[:2] + (width,))
    copies[:, :, width:] = jnp.broadcast_to(v_student[...][None], copies.shape[:2] + (width,))
    settle(rest)


def neck_kernel(core, hidden, mine, other, unit, kept, student, head, tokens, sems):
    chips, rows, double = mine.shape
    width = double // 2
    near, far = core[0] * rows, (1 - core[0]) * rows
    near, far = (pl.ds(pl.multiple_of(at, rows), rows) for at in (near, far))
    heads = fetch(
        [
            (mine.at[:, :, :width], head.at[:, near, :]),
            (other.at[:, :, :width], head.at[:, far, :]),
        ],
        sems,
    )
    count = tokens.shape[0]
    step = tokens.shape[1]
    blocks = fetch(
        [(hidden.at[pl.ds(k * step, step), :], tokens.at[k]) for k in range(count)], sems, 2
    )
    rest = fetch(
        [
            (mine.at[:, :, width:], student.at[:, near, :]),
            (other.at[:, :, width:], student.at[:, far, :]),
        ],
        sems,
        2 + count,
    )
    settle(heads)
    weights = head[...].reshape(chips * 2 * rows, width)
    for k in range(count):
        blocks[k].wait()
        neck = dot(tokens[k], weights)
        scale = lax.rsqrt(jnp.sum(neck * neck, axis=1, keepdims=True) + norm_eps)
        unit[k * step : (k + 1) * step, :] = (neck * scale).astype(bf16)
    settle(rest + fetch([(unit, kept)], sems, 4 + count))


def ring_pairs(tok, blocks, whole, which):
    rows = blocks[0].shape[0] // 2
    count = whole.shape[0] // rows
    pairs = []
    for k, block in enumerate(blocks):
        hop = (k + 1) // 2
        if 2 * hop < count:
            part = block.at[pl.ds(which * rows, rows), :]
        elif k % 2 != which:
            part = block
        else:
            continue
        origin = lax.rem(tok + (count - hop if k % 2 == 1 else hop), count) * rows
        pairs.append((part, whole.at[pl.ds(pl.multiple_of(origin, rows), rows), :]))
    return pairs


def scores_kernel(tok, unit, *refs):
    blocks, refs = refs[:-7], refs[-7:]
    scores, teacher, student, columns, whole, sums, sems = refs
    copies = fetch(ring_pairs(tok[0], blocks, whole, 0), sems)
    rest = fetch(ring_pairs(tok[0], blocks, student, 1), sems, len(copies))
    settle(copies)
    rest = rest + fetch([(whole, teacher)], sems, len(copies + rest))
    fold = LOG2E / teacher_temp
    step = 256
    count = step // 128

    def over_columns(c, _):
        at = pl.ds(pl.multiple_of(c * step, step), step)
        weights = whole[:, at]
        acc = jnp.zeros((8, step), f32)
        for r in range(unit.shape[0] // step):
            rows = slice(r * step, (r + 1) * step)
            value = jnp.exp2(dot(unit[rows, :], weights) * fold)
            scores[rows, at] = value.astype(bf16)
            acc = acc + jnp.sum(value.reshape(step // 8, 8, step), axis=0)
        acc = jnp.sum(acc, axis=0, keepdims=True)
        for k in range(count):
            sums[pl.ds(c * count + k, 1), :] = acc[:, k * 128 : (k + 1) * 128]
        return 0

    lax.fori_loop(0, whole.shape[1] // step, over_columns, 0)
    settle(rest)
    columns[...] = jnp.broadcast_to(sums[...][None], columns.shape)


def row_kernel(parts, scores, rows, sums):
    inverse = 1.0 / jnp.sum(parts[...], axis=0)
    group = 4

    def over_rows(i, _):
        for r in range(group):
            at = pl.ds(pl.multiple_of(i * (group * 128) + r * 128, 128), 128)
            acc = jnp.zeros((128, 128), f32)
            for c in range(scores.shape[1] // 128):
                block = scores[at, c * 128 : (c + 1) * 128].astype(f32)
                acc = acc + block * inverse[c : c + 1, :]
            sums[pl.ds(i * group + r, 1), :] = jnp.sum(acc.T, axis=0, keepdims=True)
        return 0

    lax.fori_loop(0, scores.shape[0] // (group * 128), over_rows, 0)
    rows[...] = jnp.broadcast_to(sums[...][None], rows.shape)


def column_kernel(parts, scores, columns, weight):
    turned = (1.0 / jnp.sum(parts[...], axis=0)).T
    for r in range(weight.shape[0] // 128):
        weight[r * 128 : (r + 1) * 128, :] = jnp.broadcast_to(turned[:, r : r + 1], (128, 128))
    step = 64
    tiles = scores.shape[1] // 128

    def over_rows(r, acc):
        at = pl.ds(pl.multiple_of(r * step, step), step)
        w = weight[at, :]
        out = []
        for c in range(tiles):
            block = scores[at, c * 128 : (c + 1) * 128].astype(f32) * w
            out.append(acc[c] + jnp.sum(block.reshape(step // 8, 8, 128), axis=0))
        return tuple(out)

    zeros = tuple(jnp.zeros((8, 128), f32) for _ in range(tiles))
    acc = lax.fori_loop(0, scores.shape[0] // step, over_rows, zeros, unroll=4)
    total = jnp.concatenate([jnp.sum(a, axis=0, keepdims=True) for a in acc], axis=0)
    columns[...] = jnp.broadcast_to(total[None], columns.shape)


def student_kernel(index, hidden, head, unit, teacher, student, *refs):
    masked, scale_out, unit_out, norm, grad, total = refs[:6]
    v_hidden, v_head, v_unit, v_teacher, whole, sems = refs[6:]
    copies = fetch(
        [
            (hidden, v_hidden),
            (head, v_head),
            (unit, v_unit),
            (teacher, v_teacher),
            (student, whole),
        ],
        sems,
    )
    slots, tokens = v_hidden.shape[0], v_unit.shape[0]
    settle(copies[:2])
    neck = dot(v_hidden[...], v_head[...])
    scale = lax.rsqrt(jnp.sum(neck * neck, axis=1, keepdims=True) + norm_eps)
    unit_float = neck * scale
    unit_out[...] = unit_float
    norm[...] = jnp.broadcast_to(scale, norm.shape)
    student = unit_float.astype(bf16)
    settle(copies[2:])
    wanted = jnp.broadcast_to(index[...].astype(f32), (128, slots)).T[:, 0:1]
    chosen = wanted == lax.broadcasted_iota(jnp.int32, (slots, tokens), 1).astype(f32)
    picked = dot(chosen.astype(f32).astype(bf16), v_unit[...]).astype(bf16)
    fold = LOG2E / teacher_temp
    step = 256
    grad_acc = jnp.zeros(grad.shape, f32)
    total_acc = jnp.zeros((slots, 1), f32)
    for c in range(whole.shape[1] // step):
        at = slice(c * step, (c + 1) * step)
        masked[:, at] = jnp.exp2(dot(picked, v_teacher[:, at]) * fold)
        weights = whole[:, at]
        wide = weights.astype(f32)
        scale_p = lax.rsqrt(jnp.sum(wide * wide, axis=0, keepdims=True) + norm_eps) / student_temp
        scale_out[:, at] = jnp.broadcast_to(scale_p, (8, step))
        soft = jnp.exp2(dot(student, weights) * (scale_p * LOG2E))
        total_acc = total_acc + jnp.sum(soft, axis=1, keepdims=True)
        high, low = split(soft * scale_p)
        grad_acc = grad_acc + dot(high, weights, NT) + dot(low, weights, NT)
    grad[...] = grad_acc
    total[...] = jnp.broadcast_to(total_acc, total.shape)


def goal_kernel(
    parts, masked, scale_p, whole, grad, total, out, v_masked, v_scale, v_whole, v_total, sems
):
    slots, width = grad.shape
    step = 512
    count = whole.shape[1] // step
    copies = fetch([(scale_p, v_scale), (total, v_total), (grad, out.at[:, :width])], sems)
    blocks = []
    for c in range(count):
        at = pl.ds(c * step, step)
        blocks.append(
            fetch(
                [(masked.at[:, at], v_masked.at[:, at]), (whole.at[:, at], v_whole.at[:, at])],
                sems,
                3 + 2 * c,
            )
        )
    inverse = 1.0 / jnp.sum(parts[...], axis=0)
    grad_acc = jnp.zeros((slots, width), f32)
    goal_acc = jnp.zeros((slots, 128), f32)
    settle(copies[:1])
    for c in range(count):
        settle(blocks[c])
        pieces = []
        for k in range(c * (step // 128), (c + 1) * (step // 128)):
            at = slice(k * 128, (k + 1) * 128)
            goal = v_masked[:, at] * inverse[k : k + 1, :]
            goal_acc = goal_acc + goal
            pieces.append(goal * v_scale[0:1, at])
        high, low = split(jnp.concatenate(pieces, axis=1))
        weights = v_whole[:, c * step : (c + 1) * step]
        grad_acc = grad_acc + dot(high, weights, NT) + dot(low, weights, NT)
    out[:, width : 2 * width] = grad_acc
    goal_total = jnp.sum(goal_acc, axis=1, keepdims=True)
    lane = lax.broadcasted_iota(jnp.int32, (slots, 128), 1)
    settle(copies[1:])
    out[:, 2 * width :] = jnp.where(lane == 0, v_total[...], goal_total)


def slots_kernel(place, parts, unit_float, norm, out, v_unit, v_norm, sems):
    share, width = parts.shape[1], unit_float.shape[1]
    at = pl.multiple_of(place[0] * share, share)
    copies = fetch(
        [(unit_float.at[pl.ds(at, share), :], v_unit), (norm.at[pl.ds(at, share), :], v_norm)], sems
    )
    mine = jnp.sum(parts[...], axis=0)
    settle(copies)
    unit = v_unit[...]
    scale = v_norm[:, 0:1]
    soft_total = mine[:, 2 * width : 2 * width + 1]
    goal_total = mine[:, 2 * width + 1 : 2 * width + 2]
    soft, goal = mine[:, :width] / soft_total, mine[:, width : 2 * width] / goal_total
    slot = at + lax.broadcasted_iota(jnp.int32, (share, 1), 0)
    live = jnp.where(slot < place[1], 1.0, 0.0)
    target_dot = jnp.sum(unit.astype(bf16).astype(f32) * goal, axis=1, keepdims=True)
    loss = live * (jnp.log(soft_total) - target_dot)
    unit_grad = live * (soft - goal)
    inner = jnp.sum(unit * unit_grad, axis=1, keepdims=True)
    neck_grad = scale * (unit_grad - unit * inner)
    top = loss.astype(bf16).astype(f32)
    mid = (loss - top).astype(bf16).astype(f32)
    low = loss - top - mid
    lane = lax.broadcasted_iota(jnp.int32, (share, width), 1)
    tail = jnp.where(lane == 0, top, jnp.where(lane == 1, mid, jnp.where(lane == 2, low, 0.0)))
    both = jnp.concatenate([neck_grad, tail], axis=0).astype(bf16)
    out[...] = jnp.broadcast_to(both[None], out.shape)


def hidden_kernel(parts, head, hidden, loss):
    count, double, width = parts.shape
    share = double // 2
    wide = parts[...].astype(f32)
    neck_grad = wide[:, :share, :].reshape(count * share, width).astype(bf16)
    tail = wide[:, share:, :128].reshape(count * share, 128).T
    loss[...] = tail[0:1, :] + tail[1:2, :] + tail[2:3, :]
    step = 512
    for c in range(head.shape[0] // step):
        at = slice(c * step, (c + 1) * step)
        hidden[:, at] = dot(neck_grad, head[at, :], NT).astype(bf16)


def exchange(blocks, axis, groups=None):
    return lax.all_to_all(blocks, axis, 0, 0, tiled=True, axis_index_groups=groups)


def shards(
    teacher_hidden,
    head_teacher,
    proto_teacher,
    student_hidden,
    head_student,
    proto_student,
    mask_index,
    mask_count,
):
    toks, protos = lax.axis_size("tok"), lax.axis_size("proto")
    tok, proto = lax.axis_index("tok"), lax.axis_index("proto")
    tok_dev, slots = teacher_hidden.shape[0], student_hidden.shape[0]
    depth = teacher_hidden.shape[1]
    width, local = head_teacher.shape[1], proto_teacher.shape[1]
    lines = local // 128
    share = slots // protos
    core, here = (proto % 2).reshape(1), tok.reshape(1)
    place = jnp.stack([proto, jnp.take(mask_count, tok)])
    dma = pltpu.SemaphoreType.DMA

    up = [(i, (i + 1) % toks) for i in range(toks)]
    down = [(i, (i - 1) % toks) for i in range(toks)]
    rows = proto_teacher.shape[0]

    def hop(pair):
        return lax.ppermute(pair[0], "tok", up), lax.ppermute(pair[1], "tok", down)

    def along(pair, values):
        first, second, values = lax.optimization_barrier((pair[0], pair[1], values))
        return (first, second), values

    chips = protos // 2
    groups = [[2 * k + c for k in range(chips)] for c in range(2)]
    copies, both = call(
        heads_kernel,
        (shaped((chips, depth // protos, 2 * width), bf16), shaped((2 * rows, local), bf16)),
        [HB] * 4,
        (VM, ANY),
        (0, MIB),
        [pltpu.VMEM((depth // protos, width), bf16)] * 2 + [dma((4,))],
    )(head_teacher, head_student, proto_teacher, proto_student)
    mine = exchange(copies, "proto", groups)
    blocks, pair = [both], (both, both)
    pair = hop(pair)
    blocks += list(pair)
    pair, mine = along(pair, mine)
    pair = hop(pair)
    blocks += list(pair)
    other = lax.ppermute(mine, "proto", [(i, i ^ 1) for i in range(protos)])
    pair = hop(pair)
    blocks += list(pair)
    step = 256
    unit_teacher, unit_kept, full_head = call(
        neck_kernel,
        (
            shaped((tok_dev, width), bf16),
            pltpu.HBM((tok_dev, width), bf16),
            pltpu.HBM((chips, depth // chips, width), bf16),
        ),
        [SM, HB, ANY, ANY],
        (VM, HB, HB),
        (2 * tok_dev * depth * width, 10 * MIB),
        [
            pltpu.VMEM((chips, depth // chips, width), bf16),
            pltpu.VMEM((tok_dev // step, step, depth), bf16),
            dma((tok_dev // step + 5,)),
        ],
    )(core, teacher_hidden, mine, other)
    full_head = full_head.reshape(depth, width)
    blocks += list(hop((pair[0][:rows], pair[1][rows:])))

    scores, whole_teacher, whole_student, columns = call(
        scores_kernel,
        (
            pltpu.VMEM((tok_dev, local), bf16),
            pltpu.HBM((toks * rows, local), bf16),
            pltpu.HBM((toks * rows, local), bf16),
            shaped((toks, lines, 128), f32),
        ),
        [SM, VM] + [ANY] * len(blocks),
        (VM, HB, HB, VM),
        (2 * tok_dev * local * width, 12 * MIB),
        [
            pltpu.VMEM((toks * rows, local), bf16),
            pltpu.VMEM((lines, 128), f32),
            dma((2 * len(blocks) + 1,)),
        ],
    )(here, unit_teacher, *blocks)

    row_call = call(
        row_kernel,
        shaped((protos, tok_dev // 128, 128), f32),
        [VM, VM],
        VM,
        (2 * tok_dev * local, 8 * MIB),
        [pltpu.VMEM((tok_dev // 128, 128), f32)],
    )
    column_call = call(
        column_kernel,
        shaped((toks, lines, 128), f32),
        [VM, VM],
        VM,
        (2 * tok_dev * local, 8 * MIB),
        [pltpu.VMEM((tok_dev, 128), f32)],
    )
    for _ in range(2):
        sums = row_call(exchange(columns, "tok"), held(scores))
        columns = column_call(exchange(sums, "proto"), held(scores))
    columns, whole_student = lax.optimization_barrier((columns, whole_student))

    rows = toks * rows
    masked, scale_p, unit_float, norm, grad, soft_total = call(
        student_kernel,
        (
            pltpu.HBM((slots, local), f32),
            pltpu.HBM((8, local), f32),
            pltpu.HBM((slots, width), f32),
            pltpu.HBM((slots, 128), f32),
            pltpu.HBM((slots, width), f32),
            pltpu.HBM((slots, 128), f32),
        ),
        [VM] + [HB] * 5,
        (VM,) * 6,
        (10 * slots * local * width, 8 * MIB),
        [
            pltpu.VMEM((slots, depth), bf16),
            pltpu.VMEM((depth, width), bf16),
            pltpu.VMEM((tok_dev, width), bf16),
            pltpu.VMEM((rows, local), bf16),
            pltpu.VMEM((rows, local), bf16),
            dma((5,)),
        ],
    )(
        mask_index.reshape(1, slots),
        student_hidden,
        full_head,
        unit_kept,
        whole_teacher,
        whole_student,
    )

    parts = call(
        goal_kernel,
        shaped((slots, 2 * width + 128), f32),
        [VM] + [HB] * 5,
        VM,
        (4 * slots * local * width, 4 * MIB),
        [
            pltpu.VMEM((slots, local), f32),
            pltpu.VMEM((8, local), f32),
            pltpu.VMEM((rows, local), bf16),
            pltpu.VMEM((slots, 128), f32),
            dma((3 + 2 * local // 512,)),
        ],
    )(exchange(columns, "tok"), masked, scale_p, whole_student, grad, soft_total)
    parts = exchange(parts.reshape(protos, share, 2 * width + 128), "proto")
    finals = call(
        slots_kernel,
        shaped((protos, 2 * share, width), bf16),
        [SM, VM, HB, HB],
        VM,
        (2 * slots * width, MIB),
        [pltpu.VMEM((share, width), f32), pltpu.VMEM((share, 128), f32), dma((2,))],
    )(place, parts, unit_float, norm)
    hidden_grad, row_loss = call(
        hidden_kernel,
        (shaped(student_hidden.shape, bf16), shaped((1, slots), f32)),
        [VM, VM],
        (VM, VM),
        (2 * slots * width * depth, 3 * MIB),
    )(exchange(finals, "proto"), full_head)
    return (row_loss.reshape(slots), hidden_grad)


def solution(mesh):
    placed = (
        P("tok", None),
        P("proto", None),
        P("tok", "proto"),
        P("tok", None),
        P("proto", None),
        P("tok", "proto"),
        P("tok"),
        P(),
    )
    return jax.shard_map(
        shards, mesh=mesh, in_specs=placed, out_specs=(P("tok"), P("tok", None)), check_vma=False
    )
```

time: 637 us -> 191 us (0.30)
  blocking collectives: 306 us -> 63.3 us
  waiting for transfers between devices: 223 us -> 34.4 us
  other arithmetic: 55.6 us -> 0.08 us
  Pallas kernels: 0 us -> 38.7 us
  starting transfers between devices: 0.19 us -> 35.9 us
  matrix products: 26.3 us -> 0 us
  between operations: 14.6 us -> 1.55 us
    psum x7 -> x0, blocking collectives: 306 us -> none  [the longest x3 208 us: token_total(): return lax.psum(values, 'proto')]
    all_gather x4 -> x0, waiting for transfers between devices: 115 us -> none  [the longest x1 52.9 us: shards(): lax.all_gather(head_teacher, 'proto', axis=0, tiled=True)]
    psum x1 -> x0, waiting for transfers between devices: 105 us -> none  [shards(): unit_grad = lax.psum(grad_terms, 'proto')]
    all_to_all x0 -> x5, blocking collectives: none -> 63.3 us  [exchange(): lax.all_to_all(blocks, axis, 0, 0, tiled=True, axis_index_groups=groups)]
    reduce_sum x7 -> x0, other arithmetic: 40.6 us -> none  [the longest x3 22.9 us: shards(): token_sums = token_total(jnp.sum(assign, axis=1))]
    pallas_call x0 -> x11, Pallas kernels: none -> 38.7 us  [the longest x1 10.3 us: shards(): call(scores_kernel, (pltpu.VMEM((tok_dev, local), bf16), pltpu.HBM((toks...]
    dot_general x6 -> x0, matrix products: 26.3 us -> none  [the longest x1 8.38 us: shards(): jnp.dot(unit_teacher, whole_teacher, preferred_element_type=jnp.float32)]
    ppermute x0 -> x9, waiting for transfers between devices: none -> 20.6 us  [the longest x4 15.9 us: hop(): lax.ppermute(pair[0], 'tok', up)]
  transfers between devices with their start and end apart: 5 -> 12, of which waited for: 4 -> 7; matrix products, arithmetic and copies ran while one was open for 11% -> 0% of each run, Pallas kernels for 0% -> 7%
where the time goes in v2:
time: 191 us; the launch traced here: 190 us
  blocking collectives  63.3 us (33%)
  Pallas kernels  38.7 us (20%)
  starting transfers between devices  35.9 us (19%)
  waiting for transfers between devices  34.4 us (18%)
  local copies, waits for them, and re-layouts  16 us (8%)
    all_to_all x5, blocking collectives, exchange(): lax.all_to_all(blocks, axis, 0, 0, tiled=True, axis_index_groups=groups)  63.3 us
    all_to_all x3, starting transfers between devices, exchange(): lax.all_to_all(blocks, axis, 0, 0, tiled=True, axis_index_groups=groups)  16 us
    ppermute x4, waiting for transfers between devices, hop(): lax.ppermute(pair[0], 'tok', up)  15.9 us
    unnamed x36, local copies, waits for them, and re-layouts  15.3 us
    ppermute x4, starting transfers between devices, hop(): lax.ppermute(pair[1], 'tok', down)  15 us
    all_to_all x3, waiting for transfers between devices, exchange(): lax.all_to_all(blocks, axis, 0, 0, tiled=True, axis_index_groups=groups)  13.8 us
    pallas_call x1, Pallas kernels, shards(): call(scores_kernel, (pltpu.VMEM((tok_dev, local), bf16), pltpu.HBM((toks...  10.3 us
    pallas_call x1, Pallas kernels, shards(): call(neck_kernel, (shaped((tok_dev, width), bf16), pltpu.HBM((tok_dev, wi...  7.98 us
  transfers between devices with their start and end apart: 12, of which 7 were waited for; matrix products, arithmetic and copies ran while one was open for 0% of the time, Pallas kernels for 7%

profile of v2, /device:TPU:1, one launch (start us, length us, event | category | flops | bytes accessed | tf_op | source)
XLA Modules:
  0.0 189.9 jit_solution(9079858558838177129)
XLA Ops:
  0.6 0.0 copy-start.11
  0.6 0.9 copy-done.11
  1.5 0.0 copy-start.12
  1.5 0.9 copy-done.12
  2.4 0.0 copy-start.14
  2.4 0.8 copy-done.14
  3.2 0.8 copy-done.15
  4.0 1.5 shard_map.95
  5.5 7.6 %all-to-all-start = ((bf16[16,64,512]{2,1,0:T(8,128)(2,1)}), bf16[16,64,512]{2,1,0:T(8,128)(2,1)S(1)}, u32[]{:S(2)}, u32[]{:S(2)}) async-start(bf16[16,64,512]{2,1,0:T(8,128)(2,1)} %get-tuple-element.25), calls=%async_computation | async-start | bytes 2097152 | tf_op jit(solution)/shard_map/all_to_all | solution.py:326
  13.1 5.7 %collective-permute-start.1 = (bf16[64,2048]{1,0:T(8,128)(2,1)S(1)}, bf16[64,2048]{1,0:T(8,128)(2,1)S(1)}, u32[]{:S(2)}, u32[]{:S(2)}) collective-permute-start(bf16[64,2048]{1,0:T(8,128)(2,1)S(1)} %get-tuple-element.24.refs_0_), channel_id=1, source_target_pairs={{0,224},{32,0},{64,32},{96,64},{128,96},{160,128},{192,160},{224,1... | collective-permute-start | bytes 786440 | tf_op jit(solution)/shard_map/ppermute | solution.py:355
  18.7 0.0 collective-permute-start
  18.7 4.7 %collective-permute-done.1.refs_2_ = bf16[64,2048]{1,0:T(8,128)(2,1)S(1)} collective-permute-done((bf16[64,2048]{1,0:T(8,128)(2,1)S(1)}, bf16[64,2048]{1,0:T(8,128)(2,1)S(1)}, u32[]{:S(2)}, u32[]{:S(2)}) %collective-permute-start.1) | collective-permute-done | bytes 262176 | tf_op jit(solution)/shard_map/ppermute | solution.py:355
  23.4 3.1 %collective-permute-done.refs_1_ = bf16[64,2048]{1,0:T(8,128)(2,1)S(1)} collective-permute-done((bf16[64,2048]{1,0:T(8,128)(2,1)S(1)}, bf16[64,2048]{1,0:T(8,128)(2,1)S(1)}, u32[]{:S(2)}, u32[]{:S(2)}) %collective-permute-start) | collective-permute-done | bytes 262176 | tf_op jit(solution)/shard_map/ppermute | solution.py:355
  26.5 2.1 %all-to-all-done.mine = bf16[16,64,512]{2,1,0:T(8,128)(2,1)S(1)} async-done(((bf16[16,64,512]{2,1,0:T(8,128)(2,1)}), bf16[16,64,512]{2,1,0:T(8,128)(2,1)S(1)}, u32[]{:S(2)}, u32[]{:S(2)}) %all-to-all-start) | async-done | bytes 1048608 | tf_op jit(solution)/shard_map/all_to_all | solution.py:326
  28.6 3.1 %collective-permute-start.2 = (bf16[16,64,512]{2,1,0:T(8,128)(2,1)S(1)}, bf16[16,64,512]{2,1,0:T(8,128)(2,1)S(1)}, u32[]{:S(2)}, u32[]{:S(2)}) collective-permute-start(bf16[16,64,512]{2,1,0:T(8,128)(2,1)S(1)} %all-to-all-done.mine), channel_id=1, source_target_pairs={{0,1},{1,0},{2,3},{3,2},{4,5},{5,4},{6,7},{7,6},{8,9},{9,8},{10,11... | collective-permute-start | bytes 3145736 | tf_op jit(solution)/shard_map/ppermute | solution.py:378
  31.7 1.6 collective-permute-start.3
  33.4 3.9 %collective-permute-start.4 = (bf16[64,2048]{1,0:T(8,128)(2,1)S(1)}, bf16[64,2048]{1,0:T(8,128)(2,1)}, u32[]{:S(2)}, u32[]{:S(2)}) collective-permute-start(bf16[64,2048]{1,0:T(8,128)(2,1)S(1)} %collective-permute-done.1.refs_2_), channel_id=1, source_target_pairs={{0,224},{32,0},{64,32},{96,64},{128,96},{160,128},{192,160},{224,1... | collective-permute-start | bytes 786440 | tf_op jit(solution)/shard_map/ppermute | solution.py:355
  37.3 6.8 %collective-permute-done.3.refs_3_ = bf16[64,2048]{1,0:T(8,128)(2,1)} collective-permute-done((bf16[64,2048]{1,0:T(8,128)(2,1)S(1)}, bf16[64,2048]{1,0:T(8,128)(2,1)}, u32[]{:S(2)}, u32[]{:S(2)}) %collective-permute-start.3) | collective-permute-done | bytes 262176 | tf_op jit(solution)/shard_map/ppermute | solution.py:355
  44.1 0.0 collective-permute-start.5
  44.1 0.0 collective-permute-done.4.refs_4_
  44.1 2.7 %collective-permute-start.6 = (bf16[64,2048]{1,0:T(8,128)(2,1)}, bf16[64,2048]{1,0:T(8,128)(2,1)S(1)}, u32[]{:S(2)}, u32[]{:S(2)}) collective-permute-start(bf16[64,2048]{1,0:T(8,128)(2,1)} %collective-permute-done.4.refs_4_), channel_id=1, source_target_pairs={{0,224},{32,0},{64,32},{96,64},{128,96},{160,128},{192,160},{224,1... | collective-permute-start | bytes 786440 | tf_op jit(solution)/shard_map/ppermute | solution.py:355
  46.8 6.0 %collective-permute-done.5.refs_5_ = bf16[64,2048]{1,0:T(8,128)(2,1)S(1)} collective-permute-done((bf16[64,2048]{1,0:T(8,128)(2,1)}, bf16[64,2048]{1,0:T(8,128)(2,1)S(1)}, u32[]{:S(2)}, u32[]{:S(2)}) %collective-permute-start.5) | collective-permute-done | bytes 262176 | tf_op jit(solution)/shard_map/ppermute | solution.py:355
  52.8 0.1 collective-permute-start.7
  52.9 0.0 collective-permute-done.6.refs_6_
  52.9 2.7 %collective-permute-start.8 = (bf16[32,2048]{1,0:T(8,128)(2,1)S(1)}, bf16[32,2048]{1,0:T(8,128)(2,1)S(1)}, u32[]{:S(2)}, u32[]{:S(2)}) collective-permute-start(bf16[32,2048]{1,0:T(8,128)(2,1)S(1)} %slice.14), channel_id=1, source_target_pairs={{0,224},{32,0},{64,32},{96,64},{128,96},{160,128},{192,160},{224,1... | collective-permute-start | bytes 393224 | tf_op jit(solution)/shard_map/ppermute | solution.py:355
  55.6 0.0 collective-permute-done.2.other
  55.7 3.4 %copy-done = bf16[2048,2048]{1,0:T(8,128)(2,1)S(1)} copy-done((bf16[2048,2048]{1,0:T(8,128)(2,1)S(1)}, bf16[2048,2048]{1,0:T(8,128)(2,1)}, u32[]{:S(2)}) %copy-start) | copy-done | bytes 8388632
  59.0 8.0 %shard_map.96 = (bf16[2048,256]{1,0:T(8,128)(2,1)S(1)}, bf16[2048,256]{1,0:T(8,128)(2,1)}, bf16[16,128,256]{2,1,0:T(8,128)(2,1)}) custom-call(s32[1]{0:T(128)} %bitcast.3.core, bf16[2048,2048]{1,0:T(8,128)(2,1)S(1)} %copy-done, bf16[16,64,512]{2,1,0:T(8,128)(2,1)S(1)} %all-to-all-done.mine, bf16[16,64,512]{2,1,0:T(8,128)(2,1)S(1)} %collective-permute-done.2.other), custom_call_target="tpu_custom_call" | custom-call | flops 2147483648 | bytes 10485760 | tf_op jit(solution)/shard_map/pallas_call | solution.py:382
  67.0 0.0 collective-permute-done.7.refs_7_
  67.0 0.0 collective-permute-done.8.refs_8_
  67.0 10.3 %shard_map.97 = (bf16[2048,2048]{1,0:T(8,128)(2,1)S(1)}, bf16[256,2048]{1,0:T(8,128)(2,1)}, bf16[256,2048]{1,0:T(8,128)(2,1)}, f32[8,16,128]{2,1,0:T(8,128)S(1)}) custom-call(s32[1]{0:T(128)} %bitcast.2.tok, bf16[2048,256]{1,0:T(8,128)(2,1)S(1)} %get-tuple-element.27.unit, bf16[64,2048]{1,0:T(8,128)(2,1)S(1)} %get-tuple-element.24.refs_0_, ...), custom_call_target="tpu_custom_call" | custom-call | flops 2147483648 | bytes 12582912 | tf_op jit(solution)/shard_map/pallas_call | solution.py:401
  77.4 11.9 %all_to_all.40.parts = f32[8,16,128]{2,1,0:T(8,128)S(1)} all-to-all(f32[8,16,128]{2,1,0:T(8,128)S(1)} %get-tuple-element.30), channel_id=1, replica_groups=mesh['tok'=8,'proto'=32] {'tok'}, dimensions={0} | all-to-all | bytes 131072 | tf_op jit(solution)/shard_map/all_to_all | solution.py:326
  89.2 2.0 %shard_map.98 = f32[32,16,128]{2,1,0:T(8,128)S(1)} custom-call(f32[8,16,128]{2,1,0:T(8,128)S(1)} %all_to_all.40.parts, bf16[2048,2048]{1,0:T(8,128)(2,1)S(1)} %get-tuple-element.31.scores), custom_call_target="tpu_custom_call" | custom-call | flops 8388608 | bytes 8388608 | tf_op jit(solution)/shard_map/pallas_call | solution.py:436
  91.2 15.8 %all_to_all.41.parts = f32[32,16,128]{2,1,0:T(8,128)S(1)} all-to-all(f32[32,16,128]{2,1,0:T(8,128)S(1)} %shard_map.98), channel_id=1, replica_groups=mesh['tok'=8,'proto'=32] {'proto'}, dimensions={0} | all-to-all | bytes 524288 | tf_op jit(solution)/shard_map/all_to_all | solution.py:326
  107.0 2.2 %shard_map.99 = f32[8,16,128]{2,1,0:T(8,128)S(1)} custom-call(f32[32,16,128]{2,1,0:T(8,128)S(1)} %all_to_all.41.parts, bf16[2048,2048]{1,0:T(8,128)(2,1)S(1)} %get-tuple-element.31.scores), custom_call_target="tpu_custom_call" | custom-call | flops 8388608 | bytes 8388608 | tf_op jit(solution)/shard_map/pallas_call | solution.py:437
  109.2 9.5 %all_to_all.42.parts = f32[8,16,128]{2,1,0:T(8,128)S(1)} all-to-all(f32[8,16,128]{2,1,0:T(8,128)S(1)} %shard_map.99), channel_id=1, replica_groups=mesh['tok'=8,'proto'=32] {'tok'}, dimensions={0} | all-to-all | bytes 131072 | tf_op jit(solution)/shard_map/all_to_all | solution.py:326
  118.8 2.0 %shard_map.100 = f32[32,16,128]{2,1,0:T(8,128)S(1)} custom-call(f32[8,16,128]{2,1,0:T(8,128)S(1)} %all_to_all.42.parts, bf16[2048,2048]{1,0:T(8,128)(2,1)S(1)} %get-tuple-element.31.scores), custom_call_target="tpu_custom_call" | custom-call | flops 8388608 | bytes 8388608 | tf_op jit(solution)/shard_map/pallas_call | solution.py:436
  120.7 13.7 %all_to_all.43.parts = f32[32,16,128]{2,1,0:T(8,128)S(1)} all-to-all(f32[32,16,128]{2,1,0:T(8,128)S(1)} %shard_map.100), channel_id=1, replica_groups=mesh['tok'=8,'proto'=32] {'proto'}, dimensions={0} | all-to-all | bytes 524288 | tf_op jit(solution)/shard_map/all_to_all | solution.py:326
  134.4 2.9 %shard_map.101 = f32[8,16,128]{2,1,0:T(8,128)} custom-call(f32[32,16,128]{2,1,0:T(8,128)S(1)} %all_to_all.43.parts, bf16[2048,2048]{1,0:T(8,128)(2,1)S(1)} %get-tuple-element.31.scores), custom_call_target="tpu_custom_call" | custom-call | flops 8388608 | bytes 8388608 | tf_op jit(solution)/shard_map/pallas_call | solution.py:437
  137.3 3.3 %all-to-all-start.5 = ((f32[8,16,128]{2,1,0:T(8,128)}), f32[8,16,128]{2,1,0:T(8,128)S(1)}, u32[]{:S(2)}, u32[]{:S(2)}) async-start(f32[8,16,128]{2,1,0:T(8,128)} %shard_map.101), calls=%async_computation.5 | async-start | bytes 131072 | tf_op jit(solution)/shard_map/all_to_all | solution.py:326
  140.6 0.0 copy-done.1
  140.7 0.0 copy-done.2
  140.7 0.0 copy-done.4
  140.7 0.0 copy-done.16
  140.7 0.0 copy-start.5
  140.7 1.2 copy-done.5
  141.9 1.2 copy-done.6
  143.1 4.5 %shard_map.102 = (f32[256,2048]{1,0:T(8,128)}, f32[8,2048]{1,0:T(8,128)}, f32[256,256]{1,0:T(8,128)}, f32[256,128]{1,0:T(8,128)}, f32[256,256]{1,0:T(8,128)}, /*index=5*/f32[256,128]{1,0:T(8,128)}) custom-call(s32[1,256]{1,0:T(1,128)S(1)} %bitcast.10, bf16[256,2048]{1,0:T(8,128)(2,1)S(1)} %copy-done.4, bf16[2048,256]{1,0:T(8,128)(2,1)S(1)} %bitcast.8, ...), custom_call_target="tpu_custom_call" | custom-call | flops 1342177280 | bytes 8388608 | tf_op jit(solution)/shard_map/pallas_call | solution.py:441
  147.6 0.1 all-to-all-done.5.parts
  147.7 1.6 copy-done.3
  149.3 0.9 copy-done.8
  150.2 0.9 copy-done.10
  151.1 0.8 copy-done.13
  152.0 3.1 %shard_map.103 = f32[256,640]{1,0:T(8,128)} custom-call(f32[8,16,128]{2,1,0:T(8,128)S(1)} %all-to-all-done.5.parts, f32[256,2048]{1,0:T(8,128)S(1)} %copy-done.3, f32[8,2048]{1,0:T(8,128)S(1)} %copy-done.13, bf16[256,2048]{1,0:T(8,128)(2,1)S(1)} %copy-done.2, f32[256,256]{1,0:T(8,128)S(1)} %copy-done.8, f32[256,128]{1,0:T(8,128)S(1)} %copy-done.10), custom_call_target="tpu_custom_call" | custom-call | flops 536870912 | bytes 4194304 | tf_op jit(solution)/shard_map/pallas_call | solution.py:471
  155.1 5.1 %all-to-all-start.6 = ((f32[32,8,640]{2,1,0:T(8,128)}), f32[32,8,640]{2,1,0:T(8,128)S(1)}, u32[]{:S(2)}, u32[]{:S(2)}) async-start(f32[32,8,640]{2,1,0:T(8,128)} %bitcast.6), calls=%async_computation.6 | async-start | bytes 1310720 | tf_op jit(solution)/shard_map/all_to_all | solution.py:326
  160.2 0.0 copy-done.17
  160.2 0.7 dynamic-slice.2
  161.6 0.1 pad_add_fusion.place
  161.6 11.6 %all-to-all-done.6.parts = f32[32,8,640]{2,1,0:T(8,128)S(1)} async-done(((f32[32,8,640]{2,1,0:T(8,128)}), f32[32,8,640]{2,1,0:T(8,128)S(1)}, u32[]{:S(2)}, u32[]{:S(2)}) %all-to-all-start.6) | async-done | bytes 655392 | tf_op jit(solution)/shard_map/all_to_all | solution.py:326
  173.2 0.9 copy-done.7
  174.2 0.9 copy-done.9
  175.1 0.9 shard_map.104
  176.0 12.5 %all_to_all.44.parts = bf16[32,16,256]{2,1,0:T(8,128)(2,1)S(1)} all-to-all(bf16[32,16,256]{2,1,0:T(8,128)(2,1)S(1)} %shard_map.104), channel_id=1, replica_groups=mesh['tok'=8,'proto'=32] {'proto'}, dimensions={0} | all-to-all | bytes 524288 | tf_op jit(solution)/shard_map/all_to_all | solution.py:326
  188.4 1.4 shard_map.105
  (16 shorter events, 0.0 us)
Async XLA Ops:
  0.6 0.9 copy-start.11
  1.5 0.9 copy-start.12
  2.4 0.8 copy-start.14
  3.2 0.8 copy-start.15
  5.5 23.1 %all-to-all-start = ((bf16[16,64,512]{2,1,0:T(8,128)(2,1)}), bf16[16,64,512]{2,1,0:T(8,128)(2,1)S(1)}, u32[]{:S(2)}, u32[]{:S(2)}) async-start(bf16[16,64,512]{2,1,0:T(8,128)(2,1)} %get-tuple-element.25), calls=%async_computation | async-start | bytes 2097152 | tf_op jit(solution)/shard_map/all_to_all | solution.py:326
  13.1 10.3 %collective-permute-start.1 = (bf16[64,2048]{1,0:T(8,128)(2,1)S(1)}, bf16[64,2048]{1,0:T(8,128)(2,1)S(1)}, u32[]{:S(2)}, u32[]{:S(2)}) collective-permute-start(bf16[64,2048]{1,0:T(8,128)(2,1)S(1)} %get-tuple-element.24.refs_0_), channel_id=1, source_target_pairs={{0,224},{32,0},{64,32},{96,64},{128,96},{160,128},{192,160},{224,1... | collective-permute-start | bytes 786440 | tf_op jit(solution)/shard_map/ppermute | solution.py:355
  18.7 7.8 %collective-permute-start = (bf16[64,2048]{1,0:T(8,128)(2,1)S(1)}, bf16[64,2048]{1,0:T(8,128)(2,1)S(1)}, u32[]{:S(2)}, u32[]{:S(2)}) collective-permute-start(bf16[64,2048]{1,0:T(8,128)(2,1)S(1)} %get-tuple-element.24.refs_0_), channel_id=1, source_target_pairs={{0,32},{32,64},{64,96},{96,128},{128,160},{160,192},{192,224},{224... | collective-permute-start | bytes 786440 | tf_op jit(solution)/shard_map/ppermute | solution.py:355
  28.6 27.1 %collective-permute-start.2 = (bf16[16,64,512]{2,1,0:T(8,128)(2,1)S(1)}, bf16[16,64,512]{2,1,0:T(8,128)(2,1)S(1)}, u32[]{:S(2)}, u32[]{:S(2)}) collective-permute-start(bf16[16,64,512]{2,1,0:T(8,128)(2,1)S(1)} %all-to-all-done.mine), channel_id=1, source_target_pairs={{0,1},{1,0},{2,3},{3,2},{4,5},{5,4},{6,7},{7,6},{8,9},{9,8},{10,11... | collective-permute-start | bytes 3145736 | tf_op jit(solution)/shard_map/ppermute | solution.py:378
  31.7 12.4 %collective-permute-start.3 = (bf16[64,2048]{1,0:T(8,128)(2,1)S(1)}, bf16[64,2048]{1,0:T(8,128)(2,1)}, u32[]{:S(2)}, u32[]{:S(2)}) collective-permute-start(bf16[64,2048]{1,0:T(8,128)(2,1)S(1)} %collective-permute-done.refs_1_), channel_id=1, source_target_pairs={{0,32},{32,64},{64,96},{96,128},{128,160},{160,192},{192,224},{224... | collective-permute-start | bytes 786440 | tf_op jit(solution)/shard_map/ppermute | solution.py:355
  33.4 10.7 %collective-permute-start.4 = (bf16[64,2048]{1,0:T(8,128)(2,1)S(1)}, bf16[64,2048]{1,0:T(8,128)(2,1)}, u32[]{:S(2)}, u32[]{:S(2)}) collective-permute-start(bf16[64,2048]{1,0:T(8,128)(2,1)S(1)} %collective-permute-done.1.refs_2_), channel_id=1, source_target_pairs={{0,224},{32,0},{64,32},{96,64},{128,96},{160,128},{192,160},{224,1... | collective-permute-start | bytes 786440 | tf_op jit(solution)/shard_map/ppermute | solution.py:355
  44.1 8.7 %collective-permute-start.5 = (bf16[64,2048]{1,0:T(8,128)(2,1)}, bf16[64,2048]{1,0:T(8,128)(2,1)S(1)}, u32[]{:S(2)}, u32[]{:S(2)}) collective-permute-start(bf16[64,2048]{1,0:T(8,128)(2,1)} %collective-permute-done.3.refs_3_), channel_id=1, source_target_pairs={{0,32},{32,64},{64,96},{96,128},{128,160},{160,192},{192,224},{224... | collective-permute-start | bytes 786440 | tf_op jit(solution)/shard_map/ppermute | solution.py:355
  44.1 8.8 %collective-permute-start.6 = (bf16[64,2048]{1,0:T(8,128)(2,1)}, bf16[64,2048]{1,0:T(8,128)(2,1)S(1)}, u32[]{:S(2)}, u32[]{:S(2)}) collective-permute-start(bf16[64,2048]{1,0:T(8,128)(2,1)} %collective-permute-done.4.refs_4_), channel_id=1, source_target_pairs={{0,224},{32,0},{64,32},{96,64},{128,96},{160,128},{192,160},{224,1... | collective-permute-start | bytes 786440 | tf_op jit(solution)/shard_map/ppermute | solution.py:355
  52.8 14.2 %collective-permute-start.7 = (bf16[32,2048]{1,0:T(8,128)(2,1)S(1)}, bf16[32,2048]{1,0:T(8,128)(2,1)S(1)}, u32[]{:S(2)}, u32[]{:S(2)}) collective-permute-start(bf16[32,2048]{1,0:T(8,128)(2,1)S(1)} %slice.13), channel_id=1, source_target_pairs={{0,32},{32,64},{64,96},{96,128},{128,160},{160,192},{192,224},{224... | collective-permute-start | bytes 393224 | tf_op jit(solution)/shard_map/ppermute | solution.py:355
  52.9 14.1 %collective-permute-start.8 = (bf16[32,2048]{1,0:T(8,128)(2,1)S(1)}, bf16[32,2048]{1,0:T(8,128)(2,1)S(1)}, u32[]{:S(2)}, u32[]{:S(2)}) collective-permute-start(bf16[32,2048]{1,0:T(8,128)(2,1)S(1)} %slice.14), channel_id=1, source_target_pairs={{0,224},{32,0},{64,32},{96,64},{128,96},{160,128},{192,160},{224,1... | collective-permute-start | bytes 393224 | tf_op jit(solution)/shard_map/ppermute | solution.py:355
  55.6 3.4 %copy-start = (bf16[2048,2048]{1,0:T(8,128)(2,1)S(1)}, bf16[2048,2048]{1,0:T(8,128)(2,1)}, u32[]{:S(2)}) copy-start(bf16[2048,2048]{1,0:T(8,128)(2,1)} %hidden.2) | copy-start | bytes 25165828
  118.7 21.9 %copy-start.1 = (bf16[16,128,256]{2,1,0:T(8,128)(2,1)S(1)}, bf16[16,128,256]{2,1,0:T(8,128)(2,1)}, u32[]{:S(2)}) copy-start(bf16[16,128,256]{2,1,0:T(8,128)(2,1)} %get-tuple-element.34) | copy-start | bytes 3145732
  118.7 21.9 %copy-start.2 = (bf16[256,2048]{1,0:T(8,128)(2,1)S(1)}, bf16[256,2048]{1,0:T(8,128)(2,1)}, u32[]{:S(2)}) copy-start(bf16[256,2048]{1,0:T(8,128)(2,1)} %get-tuple-element.37.student.whole) | copy-start | bytes 3145732
  118.7 21.9 %copy-start.4 = (bf16[256,2048]{1,0:T(8,128)(2,1)S(1)}, bf16[256,2048]{1,0:T(8,128)(2,1)}, u32[]{:S(2)}) copy-start(bf16[256,2048]{1,0:T(8,128)(2,1)} %hidden.3) | copy-start | bytes 3145732
  118.7 21.9 %copy-start.16 = (s32[256]{0:T(256)S(1)}, s32[256]{0:T(256)}, u32[]{:S(2)}) copy-start(s32[256]{0:T(256)} %param.14) | copy-start | bytes 3076
  134.4 25.8 %copy-start.17 = (s32[8]{0:T(128)S(1)}, s32[8]{0:T(128)}, u32[]{:S(2)}) copy-start(s32[8]{0:T(128)} %param.15) | copy-start | bytes 100
  137.3 10.4 %all-to-all-start.5 = ((f32[8,16,128]{2,1,0:T(8,128)}), f32[8,16,128]{2,1,0:T(8,128)S(1)}, u32[]{:S(2)}, u32[]{:S(2)}) async-start(f32[8,16,128]{2,1,0:T(8,128)} %shard_map.101), calls=%async_computation.5 | async-start | bytes 131072 | tf_op jit(solution)/shard_map/all_to_all | solution.py:326
  140.7 1.2 copy-start.5
  141.9 1.2 copy-start.6
  147.7 1.6 copy-start.3
  149.3 0.9 copy-start.8
  150.2 0.9 copy-start.10
  151.1 0.8 copy-start.13
  155.1 18.1 %all-to-all-start.6 = ((f32[32,8,640]{2,1,0:T(8,128)}), f32[32,8,640]{2,1,0:T(8,128)S(1)}, u32[]{:S(2)}, u32[]{:S(2)}) async-start(f32[32,8,640]{2,1,0:T(8,128)} %bitcast.6), calls=%async_computation.6 | async-start | bytes 1310720 | tf_op jit(solution)/shard_map/all_to_all | solution.py:326
  173.2 1.0 copy-start.7
  174.2 0.9 copy-start.9

commit v3 on v2

--- a/solution.py
+++ b/solution.py
@@ -39,6 +39,10 @@
     return pltpu.with_memory_space_constraint(values, pltpu.VMEM)
 
 
+def far(values):
+    return pltpu.with_memory_space_constraint(values, pltpu.HBM)
+
+
 def dot(left, right, dims=(((1,), (0,)), ((), ()))):
     return lax.dot_general(left, right, dims, preferred_element_type=f32)
 
@@ -75,65 +79,63 @@
     settle(rest)
 
 
-def neck_kernel(core, hidden, mine, other, unit, kept, student, head, tokens, sems):
+def stage_kernel(hidden, staged, sems):
+    step = hidden.shape[0] // 4
+    rows = [pl.ds(k * step, step) for k in range(4)]
+    settle(fetch([(hidden.at[at, :], staged.at[at, :]) for at in rows], sems))
+
+
+def neck_kernel(core, hidden, mine, other, unit, student, head, full, sems):
     chips, rows, double = mine.shape
     width = double // 2
-    near, far = core[0] * rows, (1 - core[0]) * rows
-    near, far = (pl.ds(pl.multiple_of(at, rows), rows) for at in (near, far))
-    heads = fetch(
-        [
-            (mine.at[:, :, :width], head.at[:, near, :]),
-            (other.at[:, :, :width], head.at[:, far, :]),
-        ],
-        sems,
-    )
-    count = tokens.shape[0]
-    step = tokens.shape[1]
-    blocks = fetch(
-        [(hidden.at[pl.ds(k * step, step), :], tokens.at[k]) for k in range(count)], sems, 2
-    )
-    rest = fetch(
-        [
-            (mine.at[:, :, width:], student.at[:, near, :]),
-            (other.at[:, :, width:], student.at[:, far, :]),
-        ],
-        sems,
-        2 + count,
-    )
-    settle(heads)
-    weights = head[...].reshape(chips * 2 * rows, width)
-    for k in range(count):
-        blocks[k].wait()
-        neck = dot(tokens[k], weights)
+    for chip in range(chips):
+        at = 2 * rows * chip
+        near = pl.ds(pl.multiple_of(at + core[0] * rows, rows), rows)
+        away = pl.ds(pl.multiple_of(at + (1 - core[0]) * rows, rows), rows)
+        head[near, :] = mine[chip, :, :width]
+        head[away, :] = other[chip, :, :width]
+        full[near, :] = mine[chip, :, width:]
+        full[away, :] = other[chip, :, width:]
+    copies = fetch([(full, student)], sems)
+    step = 256
+    for k in range(hidden.shape[0] // step):
+        at = slice(k * step, (k + 1) * step)
+        neck = dot(hidden[at, :], head[...])
         scale = lax.rsqrt(jnp.sum(neck * neck, axis=1, keepdims=True) + norm_eps)
-        unit[k * step : (k + 1) * step, :] = (neck * scale).astype(bf16)
-    settle(rest + fetch([(unit, kept)], sems, 4 + count))
-
-
-def ring_pairs(tok, blocks, whole, which):
-    rows = blocks[0].shape[0] // 2
+        unit[at, :] = (neck * scale).astype(bf16)
+    settle(copies)
+
+
+def join_kernel(mine, other, teacher, student):
+    rows = mine.shape[0] // 2
+    teacher[:rows, :] = mine[:rows, :]
+    teacher[rows:, :] = other[:rows, :]
+    student[:rows, :] = mine[rows:, :]
+    student[rows:, :] = other[rows:, :]
+
+
+def place_blocks(here, own, came, crossed, whole):
+    rows = own.shape[0]
     count = whole.shape[0] // rows
-    pairs = []
-    for k, block in enumerate(blocks):
-        hop = (k + 1) // 2
-        if 2 * hop < count:
-            part = block.at[pl.ds(which * rows, rows), :]
-        elif k % 2 != which:
-            part = block
-        else:
-            continue
-        origin = lax.rem(tok + (count - hop if k % 2 == 1 else hop), count) * rows
-        pairs.append((part, whole.at[pl.ds(pl.multiple_of(origin, rows), rows), :]))
-    return pairs
-
-
-def scores_kernel(tok, unit, *refs):
+    way = 1 - 2 * here[1]
+
+    def put(steps, block):
+        origin = lax.rem(here[0] + way * steps + count, count) * rows
+        whole[pl.ds(pl.multiple_of(origin, rows), rows), :] = block[:rows, :]
+
+    put(0, own)
+    for k, block in enumerate(came):
+        put(-(k + 1), block)
+    for k, block in enumerate(crossed):
+        put(k + 1, block)
+
+
+def scores_kernel(here, unit, own, *refs):
     blocks, refs = refs[:-7], refs[-7:]
-    scores, teacher, student, columns, whole, sums, sems = refs
-    copies = fetch(ring_pairs(tok[0], blocks, whole, 0), sems)
-    rest = fetch(ring_pairs(tok[0], blocks, student, 1), sems, len(copies))
-    settle(copies)
-    rest = rest + fetch([(whole, teacher)], sems, len(copies + rest))
+    scores, teacher, kept, columns, whole, sums, sems = refs
+    hops = (len(blocks) + 1) // 2
+    place_blocks(here, own[: own.shape[0] // 2, :], blocks[:hops], blocks[hops:], whole)
+    rest = fetch([(whole, teacher), (unit, kept)], sems)
     fold = LOG2E / teacher_temp
     step = 256
     count = step // 128
@@ -172,11 +174,11 @@
         return 0
 
     lax.fori_loop(0, scores.shape[0] // (group * 128), over_rows, 0)
-    rows[...] = jnp.broadcast_to(sums[...][None], rows.shape)
+    rows[...] = jnp.broadcast_to(sums[...].astype(rows.dtype)[None], rows.shape)
 
 
 def column_kernel(parts, scores, columns, weight):
-    turned = (1.0 / jnp.sum(parts[...], axis=0)).T
+    turned = (1.0 / jnp.sum(parts[...].astype(f32), axis=0)).T
     for r in range(weight.shape[0] // 128):
         weight[r * 128 : (r + 1) * 128, :] = jnp.broadcast_to(turned[:, r : r + 1], (128, 128))
     step = 64
@@ -195,6 +197,15 @@
     acc = lax.fori_loop(0, scores.shape[0] // step, over_rows, zeros, unroll=4)
     total = jnp.concatenate([jnp.sum(a, axis=0, keepdims=True) for a in acc], axis=0)
     columns[...] = jnp.broadcast_to(total[None], columns.shape)
+
+
+def last_column_kernel(here, parts, scores, own, *refs):
+    blocks, (columns, student, whole, weight, sems) = refs[:-5], refs[-5:]
+    hops = (len(blocks) + 1) // 2
+    place_blocks(here, own[own.shape[0] // 2 :, :], blocks[:hops], blocks[hops:], whole)
+    copies = fetch([(whole, student)], sems)
+    column_kernel(parts, scores, columns, weight)
+    settle(copies)
 
 
 def student_kernel(index, hidden, head, unit, teacher, student, *refs):
@@ -343,20 +354,17 @@
     width, local = head_teacher.shape[1], proto_teacher.shape[1]
     lines = local // 128
     share = slots // protos
-    core, here = (proto % 2).reshape(1), tok.reshape(1)
+    core, here = (proto % 2).reshape(1), jnp.stack([tok, proto % 2])
     place = jnp.stack([proto, jnp.take(mask_count, tok)])
     dma = pltpu.SemaphoreType.DMA
 
-    up = [(i, (i + 1) % toks) for i in range(toks)]
-    down = [(i, (i - 1) % toks) for i in range(toks)]
+    swap = [(i, i ^ 1) for i in range(protos)]
+    along = []
+    for t in range(toks):
+        for p in range(protos):
+            to = (t + (1 if p % 2 == 0 else -1)) % toks
+            along.append((t * protos + p, to * protos + p))
     rows = proto_teacher.shape[0]
-
-    def hop(pair):
-        return lax.ppermute(pair[0], "tok", up), lax.ppermute(pair[1], "tok", down)
-
-    def along(pair, values):
-        first, second, values = lax.optimization_barrier((pair[0], pair[1], values))
-        return (first, second), values
 
     chips = protos // 2
     groups = [[2 * k + c for k in range(chips)] for c in range(2)]
@@ -364,61 +372,73 @@
         heads_kernel,
         (shaped((chips, depth // protos, 2 * width), bf16), shaped((2 * rows, local), bf16)),
         [HB] * 4,
-        (VM, ANY),
+        (VM, VM),
         (0, MIB),
         [pltpu.VMEM((depth // protos, width), bf16)] * 2 + [dma((4,))],
-    )(head_teacher, head_student, proto_teacher, proto_student)
+    )(far(head_teacher), far(head_student), far(proto_teacher), far(proto_student))
     mine = exchange(copies, "proto", groups)
-    blocks, pair = [both], (both, both)
-    pair = hop(pair)
-    blocks += list(pair)
-    pair, mine = along(pair, mine)
-    pair = hop(pair)
-    blocks += list(pair)
-    other = lax.ppermute(mine, "proto", [(i, i ^ 1) for i in range(protos)])
-    pair = hop(pair)
-    blocks += list(pair)
-    step = 256
-    unit_teacher, unit_kept, full_head = call(
+    sibling = lax.ppermute(both, "proto", swap)
+    chains = call(
+        join_kernel,
+        (shaped((2 * rows, local), bf16),) * 2,
+        [VM, VM],
+        (VM, VM),
+        (0, MIB),
+    )(both, sibling)
+    teacher_own, student_own = chains
+    hops = toks // 2
+    hidden = teacher_hidden
+    came, crossed = [], []
+    for hop in range(hops):
+        sent = came[-1] if hop else teacher_own
+        came.append(lax.ppermute(sent if hop < hops - 1 else sent[:rows], ("tok", "proto"), along))
+        if hop < hops - 1:
+            crossed.append(lax.ppermute(came[-1][rows:], "proto", swap))
+        if hop == 1:
+            hidden, mine, _ = lax.optimization_barrier((hidden, mine, came[-1]))
+            other = lax.ppermute(mine, "proto", swap)
+        if hop == hops - 2:
+            student_own, _ = lax.optimization_barrier((student_own, came[-1]))
+    late, late_crossed = [lax.ppermute(student_own, ("tok", "proto"), along)], []
+    staged = call(
+        stage_kernel,
+        pltpu.VMEM(hidden.shape, bf16),
+        [HB],
+        VM,
+        (0, 16 * MIB),
+        [dma((4,))],
+    )(far(hidden))
+    unit_teacher, full_head = call(
         neck_kernel,
-        (
-            shaped((tok_dev, width), bf16),
-            pltpu.HBM((tok_dev, width), bf16),
-            pltpu.HBM((chips, depth // chips, width), bf16),
-        ),
-        [SM, HB, ANY, ANY],
-        (VM, HB, HB),
+        (shaped((tok_dev, width), bf16), pltpu.HBM((depth, width), bf16)),
+        [SM, VM, VM, VM],
+        (VM, HB),
         (2 * tok_dev * depth * width, 10 * MIB),
-        [
-            pltpu.VMEM((chips, depth // chips, width), bf16),
-            pltpu.VMEM((tok_dev // step, step, depth), bf16),
-            dma((tok_dev // step + 5,)),
-        ],
-    )(core, teacher_hidden, mine, other)
-    full_head = full_head.reshape(depth, width)
-    blocks += list(hop((pair[0][:rows], pair[1][rows:])))
-
-    scores, whole_teacher, whole_student, columns = call(
+        [pltpu.VMEM((depth, width), bf16), pltpu.VMEM((depth, width), bf16), dma((1,))],
+    )(core, held(staged), mine, other)
+
+    blocks = came + crossed
+    scores, whole_teacher, unit_kept, columns = call(
         scores_kernel,
         (
             pltpu.VMEM((tok_dev, local), bf16),
             pltpu.HBM((toks * rows, local), bf16),
-            pltpu.HBM((toks * rows, local), bf16),
+            pltpu.HBM((tok_dev, width), bf16),
             shaped((toks, lines, 128), f32),
         ),
-        [SM, VM] + [ANY] * len(blocks),
+        [SM] + [VM] * (2 + len(blocks)),
         (VM, HB, HB, VM),
         (2 * tok_dev * local * width, 12 * MIB),
         [
             pltpu.VMEM((toks * rows, local), bf16),
             pltpu.VMEM((lines, 128), f32),
-            dma((2 * len(blocks) + 1,)),
+            dma((2,)),
         ],
-    )(here, unit_teacher, *blocks)
+    )(here, unit_teacher, both, *blocks)
 
     row_call = call(
         row_kernel,
-        shaped((protos, tok_dev // 128, 128), f32),
+        shaped((protos, tok_dev // 128, 128), bf16),
         [VM, VM],
         VM,
         (2 * tok_dev * local, 8 * MIB),
@@ -432,9 +452,39 @@
         (2 * tok_dev * local, 8 * MIB),
         [pltpu.VMEM((tok_dev, 128), f32)],
     )
-    for _ in range(2):
-        sums = row_call(exchange(columns, "tok"), held(scores))
-        columns = column_call(exchange(sums, "proto"), held(scores))
+    last_column_call = call(
+        last_column_kernel,
+        (shaped((toks, lines, 128), f32), pltpu.HBM((toks * rows, local), bf16)),
+        [SM] + [VM] * (2 + 2 * hops),
+        (VM, HB),
+        (2 * tok_dev * local, 8 * MIB),
+        [
+            pltpu.VMEM((toks * rows, local), bf16),
+            pltpu.VMEM((tok_dev, 128), f32),
+            dma((1,)),
+        ],
+    )
+
+    def onward(values):
+        values, late[-1], *late_crossed[:] = lax.optimization_barrier(
+            (values, late[-1], *late_crossed)
+        )
+        if len(late) < hops:
+            late_crossed.append(lax.ppermute(late[-1][rows:], "proto", swap))
+            sent = late[-1] if len(late) < hops - 1 else late[-1][:rows]
+            late.append(lax.ppermute(sent, ("tok", "proto"), along))
+        return values
+
+    columns = onward(columns)
+    sums = row_call(exchange(columns, "tok"), held(scores))
+    sums = onward(sums)
+    columns = column_call(exchange(sums, "proto"), held(scores))
+    columns = onward(columns)
+    sums = row_call(exchange(columns, "tok"), held(scores))
+    sums = onward(sums)
+    columns, whole_student = last_column_call(
+        here, exchange(sums, "proto"), held(scores), both, *late, *late_crossed
+    )
     columns, whole_student = lax.optimization_barrier((columns, whole_student))
 
     rows = toks * rows
@@ -461,11 +511,11 @@
         ],
     )(
         mask_index.reshape(1, slots),
-        student_hidden,
-        full_head,
-        unit_kept,
-        whole_teacher,
-        whole_student,
+        far(student_hidden),
+        far(full_head),
+        far(unit_kept),
+        far(whole_teacher),
+        far(whole_student),
     )
 
     parts = call(
@@ -481,7 +531,14 @@
             pltpu.VMEM((slots, 128), f32),
             dma((3 + 2 * local // 512,)),
         ],
-    )(exchange(columns, "tok"), masked, scale_p, whole_student, grad, soft_total)
+    )(
+        exchange(columns, "tok"),
+        far(masked),
+        far(scale_p),
+        far(whole_student),
+        far(grad),
+        far(soft_total),
+    )
     parts = exchange(parts.reshape(protos, share, 2 * width + 128), "proto")
     finals = call(
         slots_kernel,
@@ -490,7 +547,7 @@
         VM,
         (2 * slots * width, MIB),
         [pltpu.VMEM((share, width), f32), pltpu.VMEM((share, 128), f32), dma((2,))],
-    )(place, parts, unit_float, norm)
+    )(place, parts, far(unit_float), far(norm))
     hidden_grad, row_loss = call(
         hidden_kernel,
         (shaped(student_hidden.shape, bf16), shaped((1, slots), f32)),

time: 191 us -> 163 us (0.85)
  local copies, waits for them, and re-layouts: 16 us -> 0.67 us
  waiting for transfers between devices: 34.4 us -> 20.8 us
  starting transfers between devices: 35.9 us -> 42.8 us
  Pallas kernels: 38.7 us -> 35.3 us
  blocking collectives: 63.3 us -> 61 us
    unnamed x36 -> x6, local copies, waits for them, and re-layouts: 15.3 us -> 0.01 us
    ppermute x9 -> x16, waiting for transfers between devices: 20.6 us -> 7.83 us  [the longest x4 6.64 us: shards(): lax.ppermute(sent if hop < hops - 1 else sent[:rows], ('tok', 'proto'), a...]
    ppermute x9 -> x16, starting transfers between devices: 19.9 us -> 26.6 us  [the longest x4 14.7 us: shards(): lax.ppermute(sent if hop < hops - 1 else sent[:rows], ('tok', 'proto'), a...]
    pallas_call x1, Pallas kernels: 10.3 us -> 4.34 us  [shards(): call(scores_kernel, (pltpu.VMEM((tok_dev, local), bf16), pltpu.HBM((toks...]
    pallas_call x2 -> x1, Pallas kernels: 5.1 us -> 2.24 us  [shards(): columns = column_call(exchange(sums, 'proto'), held(scores))]
    all_to_all x5, blocking collectives: 63.3 us -> 61 us  [exchange(): lax.all_to_all(blocks, axis, 0, 0, tiled=True, axis_index_groups=groups)]
    pallas_call x1 -> x4, Pallas kernels: 7.98 us -> 10.2 us  [the longest x1 3.5 us: shards(): call(stage_kernel, pltpu.VMEM(hidden.shape, bf16), [HB], VM, (0, 16 * MIB...]
  transfers between devices with their start and end apart: 12 -> 19, of which waited for: 7 -> 5; matrix products, arithmetic and copies ran while one was open for 0% -> 0% of each run, Pallas kernels for 7% -> 14%
where the time goes in v3:
time: 163 us; the launch traced here: 162 us
  blocking collectives  61 us (37%)
  starting transfers between devices  42.8 us (26%)
  Pallas kernels  35.3 us (22%)
  waiting for transfers between devices  20.8 us (13%)
    all_to_all x5, blocking collectives, exchange(): lax.all_to_all(blocks, axis, 0, 0, tiled=True, axis_index_groups=groups)  61 us
    all_to_all x3, starting transfers between devices, exchange(): lax.all_to_all(blocks, axis, 0, 0, tiled=True, axis_index_groups=groups)  16.3 us
    ppermute x4, starting transfers between devices, shards(): lax.ppermute(sent if hop < hops - 1 else sent[:rows], ('tok', 'proto'), a...  14.7 us
    all_to_all x3, waiting for transfers between devices, exchange(): lax.all_to_all(blocks, axis, 0, 0, tiled=True, axis_index_groups=groups)  13 us
    ppermute x4, waiting for transfers between devices, shards(): lax.ppermute(sent if hop < hops - 1 else sent[:rows], ('tok', 'proto'), a...  6.64 us
    pallas_call x1, Pallas kernels, shards(): call(student_kernel, (pltpu.HBM((slots, local), f32), pltpu.HBM((8, local...  5.87 us
    pallas_call x1, Pallas kernels, shards(): call(scores_kernel, (pltpu.VMEM((tok_dev, local), bf16), pltpu.HBM((toks...  4.34 us
    ppermute x3, starting transfers between devices, onward(): late.append(lax.ppermute(sent, ('tok', 'proto'), along))  3.92 us
  transfers between devices with their start and end apart: 19, of which 5 were waited for; matrix products, arithmetic and copies ran while one was open for 0% of the time, Pallas kernels for 14%

profile of v3, /device:TPU:1, one launch (start us, length us, event | category | flops | bytes accessed | tf_op | source)
XLA Modules:
  0.0 162.3 jit_solution(9355963888252354223)
XLA Ops:
  0.6 2.0 %shard_map.95 = (bf16[16,64,512]{2,1,0:T(8,128)(2,1)}, bf16[64,2048]{1,0:T(8,128)(2,1)S(1)}) custom-call(bf16[64,256]{1,0:T(8,128)(2,1)} %teacher.1, bf16[64,256]{1,0:T(8,128)(2,1)} %student.1, bf16[32,2048]{1,0:T(8,128)(2,1)} %first.1, bf16[32,2048]{1,0:T(8,128)(2,1)} %second.1), custom_call_target="tpu_custom_call" | custom-call | bytes 1048576 | tf_op jit(solution)/shard_map/pallas_call | solution.py:371
  2.6 7.6 %all-to-all-start = ((bf16[16,64,512]{2,1,0:T(8,128)(2,1)}), bf16[16,64,512]{2,1,0:T(8,128)(2,1)S(1)}, u32[]{:S(2)}, u32[]{:S(2)}) async-start(bf16[16,64,512]{2,1,0:T(8,128)(2,1)} %get-tuple-element.39), calls=%async_computation | async-start | bytes 2097152 | tf_op jit(solution)/shard_map/all_to_all | solution.py:337
  10.3 1.0 collective-permute-start
  11.3 1.2 collective-permute-done.other
  12.5 5.7 %collective-permute-start.1 = (bf16[64,2048]{1,0:T(8,128)(2,1)S(1)}, bf16[64,2048]{1,0:T(8,128)(2,1)S(1)}, u32[]{:S(2)}, u32[]{:S(2)}) collective-permute-start(bf16[64,2048]{1,0:T(8,128)(2,1)S(1)} %get-tuple-element.41), channel_id=1, source_target_pairs={{0,32},{1,225},{2,34},{3,227},{4,36},{5,229},{6,38},{7,231},{8,40}... | collective-permute-start | bytes 786440 | tf_op jit(solution)/shard_map/ppermute | solution.py:394
  18.1 3.3 %collective-permute-done.1.refs_0_ = bf16[64,2048]{1,0:T(8,128)(2,1)S(1)} collective-permute-done((bf16[64,2048]{1,0:T(8,128)(2,1)S(1)}, bf16[64,2048]{1,0:T(8,128)(2,1)S(1)}, u32[]{:S(2)}, u32[]{:S(2)}) %collective-permute-start.1) | collective-permute-done | bytes 262176 | tf_op jit(solution)/shard_map/ppermute | solution.py:394
  21.5 3.4 %collective-permute-start.2 = (bf16[64,2048]{1,0:T(8,128)(2,1)S(1)}, bf16[64,2048]{1,0:T(8,128)(2,1)S(1)}, u32[]{:S(2)}, u32[]{:S(2)}) collective-permute-start(bf16[64,2048]{1,0:T(8,128)(2,1)S(1)} %collective-permute-done.1.refs_0_), channel_id=1, source_target_pairs={{0,32},{1,225},{2,34},{3,227},{4,36},{5,229},{6,38},{7,231},{8,40}... | collective-permute-start | bytes 786440 | tf_op jit(solution)/shard_map/ppermute | solution.py:394
  24.9 3.3 %collective-permute-done.2.refs_1_ = bf16[64,2048]{1,0:T(8,128)(2,1)S(1)} collective-permute-done((bf16[64,2048]{1,0:T(8,128)(2,1)S(1)}, bf16[64,2048]{1,0:T(8,128)(2,1)S(1)}, u32[]{:S(2)}, u32[]{:S(2)}) %collective-permute-start.2) | collective-permute-done | bytes 262176 | tf_op jit(solution)/shard_map/ppermute | solution.py:394
  28.2 0.0 all-to-all-done.mine
  28.2 2.5 %collective-permute-start.3 = (bf16[16,64,512]{2,1,0:T(8,128)(2,1)S(1)}, bf16[16,64,512]{2,1,0:T(8,128)(2,1)S(1)}, u32[]{:S(2)}, u32[]{:S(2)}) collective-permute-start(bf16[16,64,512]{2,1,0:T(8,128)(2,1)S(1)} %all-to-all-done.mine), channel_id=1, source_target_pairs={{0,1},{1,0},{2,3},{3,2},{4,5},{5,4},{6,7},{7,6},{8,9},{9,8},{10,11... | collective-permute-start | bytes 3145736 | tf_op jit(solution)/shard_map/ppermute | solution.py:399
  30.7 3.7 %collective-permute-start.4 = (bf16[64,2048]{1,0:T(8,128)(2,1)S(1)}, bf16[64,2048]{1,0:T(8,128)(2,1)S(1)}, u32[]{:S(2)}, u32[]{:S(2)}) collective-permute-start(bf16[64,2048]{1,0:T(8,128)(2,1)S(1)} %collective-permute-done.2.refs_1_), channel_id=1, source_target_pairs={{0,32},{1,225},{2,34},{3,227},{4,36},{5,229},{6,38},{7,231},{8,40}... | collective-permute-start | bytes 786440 | tf_op jit(solution)/shard_map/ppermute | solution.py:394
  34.5 0.1 pad_add_fusion.1.here
  34.6 0.1 collective-permute-start.6
  34.7 0.6 collective-permute-start.7
  35.3 3.5 %shard_map.97.hidden = bf16[2048,2048]{1,0:T(8,128)(2,1)S(1)} custom-call(bf16[2048,2048]{1,0:T(8,128)(2,1)} %hidden.1), custom_call_target="tpu_custom_call" | custom-call | bytes 16777216 | tf_op jit(solution)/shard_map/pallas_call | solution.py:403
  38.8 0.0 collective-permute-done.4.refs_2_
  38.8 0.4 collective-permute-start.8
  39.2 1.9 %collective-permute-start.5 = (bf16[32,2048]{1,0:T(8,128)(2,1)S(1)}, bf16[32,2048]{1,0:T(8,128)(2,1)S(1)}, u32[]{:S(2)}, u32[]{:S(2)}) collective-permute-start(bf16[32,2048]{1,0:T(8,128)(2,1)S(1)} %get-tuple-element.90), channel_id=1, source_target_pairs={{0,32},{1,225},{2,34},{3,227},{4,36},{5,229},{6,38},{7,231},{8,40}... | collective-permute-start | bytes 393224 | tf_op jit(solution)/shard_map/ppermute | solution.py:394
  41.1 0.0 collective-permute-done.3.other
  41.1 0.6 collective-permute-start.9
  41.7 3.3 %shard_map.98 = (bf16[2048,256]{1,0:T(8,128)(2,1)S(1)}, bf16[2048,256]{1,0:T(8,128)(2,1)}) custom-call(s32[1]{0:T(128)} %bitcast.3.core, bf16[2048,2048]{1,0:T(8,128)(2,1)S(1)} %shard_map.97.hidden, bf16[16,64,512]{2,1,0:T(8,128)(2,1)S(1)} %all-to-all-done.mine, bf16[16,64,512]{2,1,0:T(8,128)(2,1)S(1)} %collective-permute-done.3.other), custom_call_target="tpu_custom_call" | custom-call | flops 2147483648 | bytes 10485760 | tf_op jit(solution)/shard_map/pallas_call | solution.py:411
  45.0 0.0 collective-permute-done.6.refs_4_
  45.0 0.0 collective-permute-done.7.refs_5_
  45.0 0.0 collective-permute-done.8.refs_6_
  45.0 0.0 collective-permute-done.5.refs_3_
  45.0 4.3 %shard_map.99 = (bf16[2048,2048]{1,0:T(8,128)(2,1)S(1)}, bf16[256,2048]{1,0:T(8,128)(2,1)}, bf16[2048,256]{1,0:T(8,128)(2,1)}, f32[8,16,128]{2,1,0:T(8,128)S(1)}) custom-call(s32[2]{0:T(128)S(1)} %pad_add_fusion.1.here, bf16[2048,256]{1,0:T(8,128)(2,1)S(1)} %get-tuple-element.44.unit, bf16[64,2048]{1,0:T(8,128)(2,1)S(1)} %get-tuple-element.40.mine.own, ...), custom_call_target="tpu_custom_call" | custom-call | flops 2147483648 | bytes 12582912 | tf_op jit(solution)/shard_map/pallas_call | solution.py:421
  49.4 0.0 collective-permute-done.9.refs_0_
  49.4 1.2 collective-permute-start.10
  50.6 0.1 collective-permute-start.11
  50.7 12.4 %all_to_all.40.parts = f32[8,16,128]{2,1,0:T(8,128)S(1)} all-to-all(f32[8,16,128]{2,1,0:T(8,128)S(1)} %get-tuple-element.48), channel_id=1, replica_groups=mesh['tok'=8,'proto'=32] {'tok'}, dimensions={0} | all-to-all | bytes 131072 | tf_op jit(solution)/shard_map/all_to_all | solution.py:337
  63.1 2.0 %shard_map.100 = bf16[32,16,128]{2,1,0:T(8,128)(2,1)S(1)} custom-call(f32[8,16,128]{2,1,0:T(8,128)S(1)} %all_to_all.40.parts, bf16[2048,2048]{1,0:T(8,128)(2,1)S(1)} %get-tuple-element.49.scores), custom_call_target="tpu_custom_call" | custom-call | flops 8388608 | bytes 8388608 | tf_op jit(solution)/shard_map/pallas_call | solution.py:479
  65.0 0.0 collective-permute-done.11.refs_4_
  65.0 0.0 collective-permute-done.10.refs_1_
  65.1 0.3 collective-permute-start.12
  65.4 2.1 %collective-permute-start.13 = (bf16[32,2048]{1,0:T(8,128)(2,1)S(1)}, bf16[32,2048]{1,0:T(8,128)(2,1)S(1)}, u32[]{:S(2)}, u32[]{:S(2)}) collective-permute-start(bf16[32,2048]{1,0:T(8,128)(2,1)S(1)} %slice.29), channel_id=1, source_target_pairs={{0,1},{1,0},{2,3},{3,2},{4,5},{5,4},{6,7},{7,6},{8,9},{9,8},{10,11... | collective-permute-start | bytes 393224 | tf_op jit(solution)/shard_map/ppermute | solution.py:473
  67.5 14.0 %all_to_all.41.parts = bf16[32,16,128]{2,1,0:T(8,128)(2,1)S(1)} all-to-all(bf16[32,16,128]{2,1,0:T(8,128)(2,1)S(1)} %shard_map.100), channel_id=1, replica_groups=mesh['tok'=8,'proto'=32] {'proto'}, dimensions={0} | all-to-all | bytes 262144 | tf_op jit(solution)/shard_map/all_to_all | solution.py:337
  81.5 2.2 %shard_map.101 = f32[8,16,128]{2,1,0:T(8,128)S(1)} custom-call(bf16[32,16,128]{2,1,0:T(8,128)(2,1)S(1)} %all_to_all.41.parts, bf16[2048,2048]{1,0:T(8,128)(2,1)S(1)} %get-tuple-element.49.scores), custom_call_target="tpu_custom_call" | custom-call | flops 8388608 | bytes 8388608 | tf_op jit(solution)/shard_map/pallas_call | solution.py:481
  83.8 0.0 collective-permute-done.13.refs_5_
  83.8 0.0 collective-permute-done.12.refs_2_
  83.8 0.5 collective-permute-start.15
  84.3 2.4 %collective-permute-start.14 = (bf16[32,2048]{1,0:T(8,128)(2,1)S(1)}, bf16[32,2048]{1,0:T(8,128)(2,1)S(1)}, u32[]{:S(2)}, u32[]{:S(2)}) collective-permute-start(bf16[32,2048]{1,0:T(8,128)(2,1)S(1)} %get-tuple-element.88), channel_id=1, source_target_pairs={{0,32},{1,225},{2,34},{3,227},{4,36},{5,229},{6,38},{7,231},{8,40}... | collective-permute-start | bytes 393224 | tf_op jit(solution)/shard_map/ppermute | solution.py:475
  86.7 9.6 %all_to_all.42.parts = f32[8,16,128]{2,1,0:T(8,128)S(1)} all-to-all(f32[8,16,128]{2,1,0:T(8,128)S(1)} %shard_map.101), channel_id=1, replica_groups=mesh['tok'=8,'proto'=32] {'tok'}, dimensions={0} | all-to-all | bytes 131072 | tf_op jit(solution)/shard_map/all_to_all | solution.py:337
  96.3 0.0 copy-start.1
  96.3 2.0 %shard_map.102 = bf16[32,16,128]{2,1,0:T(8,128)(2,1)S(1)} custom-call(f32[8,16,128]{2,1,0:T(8,128)S(1)} %all_to_all.42.parts, bf16[2048,2048]{1,0:T(8,128)(2,1)S(1)} %get-tuple-element.49.scores), custom_call_target="tpu_custom_call" | custom-call | flops 8388608 | bytes 8388608 | tf_op jit(solution)/shard_map/pallas_call | solution.py:483
  98.2 0.0 collective-permute-done.15.refs_6_
  98.3 0.0 collective-permute-done.14.refs_3_
  98.3 12.6 %all_to_all.43.parts = bf16[32,16,128]{2,1,0:T(8,128)(2,1)S(1)} all-to-all(bf16[32,16,128]{2,1,0:T(8,128)(2,1)S(1)} %shard_map.102), channel_id=1, replica_groups=mesh['tok'=8,'proto'=32] {'proto'}, dimensions={0} | all-to-all | bytes 262144 | tf_op jit(solution)/shard_map/all_to_all | solution.py:337
  110.8 0.0 copy-start.2
  110.8 3.4 %shard_map.103 = (f32[8,16,128]{2,1,0:T(8,128)}, bf16[256,2048]{1,0:T(8,128)(2,1)}) custom-call(s32[2]{0:T(128)S(1)} %pad_add_fusion.1.here, bf16[32,16,128]{2,1,0:T(8,128)(2,1)S(1)} %all_to_all.43.parts, bf16[2048,2048]{1,0:T(8,128)(2,1)S(1)} %get-tuple-element.49.scores, bf16[64,2048]{1,0:T(8,128)(2,1)S(1)} %get-tuple-element.40.mine.own, ...), custom_call_target="tpu_custom_call" | custom-call | flops 8388608 | bytes 8388608 | tf_op jit(solution)/shard_map/pallas_call | solution.py:485
  114.3 0.0 copy-start
  114.3 3.5 %all-to-all-start.5 = ((f32[8,16,128]{2,1,0:T(8,128)}), f32[8,16,128]{2,1,0:T(8,128)S(1)}, u32[]{:S(2)}, u32[]{:S(2)}) async-start(f32[8,16,128]{2,1,0:T(8,128)} %get-tuple-element.63), calls=%async_computation.5 | async-start | bytes 131072 | tf_op jit(solution)/shard_map/all_to_all | solution.py:337
  117.8 0.0 copy-done.1
  117.8 5.9 %shard_map.104 = (f32[256,2048]{1,0:T(8,128)}, f32[8,2048]{1,0:T(8,128)}, f32[256,256]{1,0:T(8,128)}, f32[256,128]{1,0:T(8,128)}, f32[256,256]{1,0:T(8,128)}, /*index=5*/f32[256,128]{1,0:T(8,128)}) custom-call(s32[1,256]{1,0:T(1,128)S(1)} %bitcast.7, bf16[256,2048]{1,0:T(8,128)(2,1)} %hidden.2, bf16[2048,256]{1,0:T(8,128)(2,1)} %get-tuple-element.64.head, ...), custom_call_target="tpu_custom_call" | custom-call | flops 1342177280 | bytes 8388608 | tf_op jit(solution)/shard_map/pallas_call | solution.py:491
  123.7 1.2 all-to-all-done.5.parts
  124.8 3.8 %shard_map.105 = f32[256,640]{1,0:T(8,128)} custom-call(f32[8,16,128]{2,1,0:T(8,128)S(1)} %all-to-all-done.5.parts, f32[256,2048]{1,0:T(8,128)} %get-tuple-element.68.masked, f32[8,2048]{1,0:T(8,128)} %get-tuple-element.69.scale_p, bf16[256,2048]{1,0:T(8,128)(2,1)} %get-tuple-element.67.student.whole, f32[256,256]{1,0:T(8,128)} %get-tuple-element.70.grad, ...), custom_call_target="tpu_custom_call" | custom-call | flops 536870912 | bytes 4194304 | tf_op jit(solution)/shard_map/pallas_call | solution.py:521
  128.7 5.2 %all-to-all-start.6 = ((f32[32,8,640]{2,1,0:T(8,128)}), f32[32,8,640]{2,1,0:T(8,128)S(1)}, u32[]{:S(2)}, u32[]{:S(2)}) async-start(f32[32,8,640]{2,1,0:T(8,128)} %bitcast.5), calls=%async_computation.6 | async-start | bytes 1310720 | tf_op jit(solution)/shard_map/all_to_all | solution.py:337
  133.9 0.0 copy-done.2
  133.9 0.6 dynamic-slice.2
  135.0 0.1 pad_add_fusion.place
  135.1 11.8 %all-to-all-done.6.parts = f32[32,8,640]{2,1,0:T(8,128)S(1)} async-done(((f32[32,8,640]{2,1,0:T(8,128)}), f32[32,8,640]{2,1,0:T(8,128)S(1)}, u32[]{:S(2)}, u32[]{:S(2)}) %all-to-all-start.6) | async-done | bytes 655392 | tf_op jit(solution)/shard_map/all_to_all | solution.py:337
  146.9 1.5 shard_map.106
  148.4 12.5 %all_to_all.44.parts = bf16[32,16,256]{2,1,0:T(8,128)(2,1)S(1)} all-to-all(bf16[32,16,256]{2,1,0:T(8,128)(2,1)S(1)} %shard_map.106), channel_id=1, replica_groups=mesh['tok'=8,'proto'=32] {'proto'}, dimensions={0} | all-to-all | bytes 524288 | tf_op jit(solution)/shard_map/all_to_all | solution.py:337
  160.9 0.0 copy-done
  160.9 1.4 shard_map.107
  (7 shorter events, 0.1 us)
Async XLA Ops:
  2.6 25.5 %all-to-all-start = ((bf16[16,64,512]{2,1,0:T(8,128)(2,1)}), bf16[16,64,512]{2,1,0:T(8,128)(2,1)S(1)}, u32[]{:S(2)}, u32[]{:S(2)}) async-start(bf16[16,64,512]{2,1,0:T(8,128)(2,1)} %get-tuple-element.39), calls=%async_computation | async-start | bytes 2097152 | tf_op jit(solution)/shard_map/all_to_all | solution.py:337
  10.3 2.2 %collective-permute-start = (bf16[64,2048]{1,0:T(8,128)(2,1)S(1)}, bf16[64,2048]{1,0:T(8,128)(2,1)S(1)}, u32[]{:S(2)}, u32[]{:S(2)}) collective-permute-start(bf16[64,2048]{1,0:T(8,128)(2,1)S(1)} %get-tuple-element.40.mine.own), channel_id=1, source_target_pairs={{0,1},{1,0},{2,3},{3,2},{4,5},{5,4},{6,7},{7,6},{8,9},{9,8},{10,11... | collective-permute-start | bytes 786440 | tf_op jit(solution)/shard_map/ppermute | solution.py:380
  12.5 9.0 %collective-permute-start.1 = (bf16[64,2048]{1,0:T(8,128)(2,1)S(1)}, bf16[64,2048]{1,0:T(8,128)(2,1)S(1)}, u32[]{:S(2)}, u32[]{:S(2)}) collective-permute-start(bf16[64,2048]{1,0:T(8,128)(2,1)S(1)} %get-tuple-element.41), channel_id=1, source_target_pairs={{0,32},{1,225},{2,34},{3,227},{4,36},{5,229},{6,38},{7,231},{8,40}... | collective-permute-start | bytes 786440 | tf_op jit(solution)/shard_map/ppermute | solution.py:394
  21.5 6.7 %collective-permute-start.2 = (bf16[64,2048]{1,0:T(8,128)(2,1)S(1)}, bf16[64,2048]{1,0:T(8,128)(2,1)S(1)}, u32[]{:S(2)}, u32[]{:S(2)}) collective-permute-start(bf16[64,2048]{1,0:T(8,128)(2,1)S(1)} %collective-permute-done.1.refs_0_), channel_id=1, source_target_pairs={{0,32},{1,225},{2,34},{3,227},{4,36},{5,229},{6,38},{7,231},{8,40}... | collective-permute-start | bytes 786440 | tf_op jit(solution)/shard_map/ppermute | solution.py:394
  28.2 12.9 %collective-permute-start.3 = (bf16[16,64,512]{2,1,0:T(8,128)(2,1)S(1)}, bf16[16,64,512]{2,1,0:T(8,128)(2,1)S(1)}, u32[]{:S(2)}, u32[]{:S(2)}) collective-permute-start(bf16[16,64,512]{2,1,0:T(8,128)(2,1)S(1)} %all-to-all-done.mine), channel_id=1, source_target_pairs={{0,1},{1,0},{2,3},{3,2},{4,5},{5,4},{6,7},{7,6},{8,9},{9,8},{10,11... | collective-permute-start | bytes 3145736 | tf_op jit(solution)/shard_map/ppermute | solution.py:399
  30.7 8.0 %collective-permute-start.4 = (bf16[64,2048]{1,0:T(8,128)(2,1)S(1)}, bf16[64,2048]{1,0:T(8,128)(2,1)S(1)}, u32[]{:S(2)}, u32[]{:S(2)}) collective-permute-start(bf16[64,2048]{1,0:T(8,128)(2,1)S(1)} %collective-permute-done.2.refs_1_), channel_id=1, source_target_pairs={{0,32},{1,225},{2,34},{3,227},{4,36},{5,229},{6,38},{7,231},{8,40}... | collective-permute-start | bytes 786440 | tf_op jit(solution)/shard_map/ppermute | solution.py:394
  34.6 10.4 %collective-permute-start.6 = (bf16[32,2048]{1,0:T(8,128)(2,1)S(1)}, bf16[32,2048]{1,0:T(8,128)(2,1)S(1)}, u32[]{:S(2)}, u32[]{:S(2)}) collective-permute-start(bf16[32,2048]{1,0:T(8,128)(2,1)S(1)} %slice.38), channel_id=1, source_target_pairs={{0,1},{1,0},{2,3},{3,2},{4,5},{5,4},{6,7},{7,6},{8,9},{9,8},{10,11... | collective-permute-start | bytes 393224 | tf_op jit(solution)/shard_map/ppermute | solution.py:396
  34.7 10.3 %collective-permute-start.7 = (bf16[32,2048]{1,0:T(8,128)(2,1)S(1)}, bf16[32,2048]{1,0:T(8,128)(2,1)S(1)}, u32[]{:S(2)}, u32[]{:S(2)}) collective-permute-start(bf16[32,2048]{1,0:T(8,128)(2,1)S(1)} %slice.39), channel_id=1, source_target_pairs={{0,1},{1,0},{2,3},{3,2},{4,5},{5,4},{6,7},{7,6},{8,9},{9,8},{10,11... | collective-permute-start | bytes 393224 | tf_op jit(solution)/shard_map/ppermute | solution.py:396
  38.8 6.2 %collective-permute-start.8 = (bf16[32,2048]{1,0:T(8,128)(2,1)S(1)}, bf16[32,2048]{1,0:T(8,128)(2,1)S(1)}, u32[]{:S(2)}, u32[]{:S(2)}) collective-permute-start(bf16[32,2048]{1,0:T(8,128)(2,1)S(1)} %get-tuple-element.89), channel_id=1, source_target_pairs={{0,1},{1,0},{2,3},{3,2},{4,5},{5,4},{6,7},{7,6},{8,9},{9,8},{10,11... | collective-permute-start | bytes 393224 | tf_op jit(solution)/shard_map/ppermute | solution.py:396
  39.2 5.8 %collective-permute-start.5 = (bf16[32,2048]{1,0:T(8,128)(2,1)S(1)}, bf16[32,2048]{1,0:T(8,128)(2,1)S(1)}, u32[]{:S(2)}, u32[]{:S(2)}) collective-permute-start(bf16[32,2048]{1,0:T(8,128)(2,1)S(1)} %get-tuple-element.90), channel_id=1, source_target_pairs={{0,32},{1,225},{2,34},{3,227},{4,36},{5,229},{6,38},{7,231},{8,40}... | collective-permute-start | bytes 393224 | tf_op jit(solution)/shard_map/ppermute | solution.py:394
  41.1 8.2 %collective-permute-start.9 = (bf16[64,2048]{1,0:T(8,128)(2,1)S(1)}, bf16[64,2048]{1,0:T(8,128)(2,1)S(1)}, u32[]{:S(2)}, u32[]{:S(2)}) collective-permute-start(bf16[64,2048]{1,0:T(8,128)(2,1)S(1)} %get-tuple-element.47), channel_id=1, source_target_pairs={{0,32},{1,225},{2,34},{3,227},{4,36},{5,229},{6,38},{7,231},{8,40}... | collective-permute-start | bytes 786440 | tf_op jit(solution)/shard_map/ppermute | solution.py:402
  49.4 15.7 %collective-permute-start.10 = (bf16[64,2048]{1,0:T(8,128)(2,1)S(1)}, bf16[64,2048]{1,0:T(8,128)(2,1)S(1)}, u32[]{:S(2)}, u32[]{:S(2)}) collective-permute-start(bf16[64,2048]{1,0:T(8,128)(2,1)S(1)} %collective-permute-done.9.refs_0_), channel_id=1, source_target_pairs={{0,32},{1,225},{2,34},{3,227},{4,36},{5,229},{6,38},{7,231},{8,40}... | collective-permute-start | bytes 786440 | tf_op jit(solution)/shard_map/ppermute | solution.py:475
  50.6 14.5 %collective-permute-start.11 = (bf16[32,2048]{1,0:T(8,128)(2,1)S(1)}, bf16[32,2048]{1,0:T(8,128)(2,1)S(1)}, u32[]{:S(2)}, u32[]{:S(2)}) collective-permute-start(bf16[32,2048]{1,0:T(8,128)(2,1)S(1)} %slice.28), channel_id=1, source_target_pairs={{0,1},{1,0},{2,3},{3,2},{4,5},{5,4},{6,7},{7,6},{8,9},{9,8},{10,11... | collective-permute-start | bytes 393224 | tf_op jit(solution)/shard_map/ppermute | solution.py:473
  65.1 18.7 %collective-permute-start.12 = (bf16[64,2048]{1,0:T(8,128)(2,1)S(1)}, bf16[64,2048]{1,0:T(8,128)(2,1)S(1)}, u32[]{:S(2)}, u32[]{:S(2)}) collective-permute-start(bf16[64,2048]{1,0:T(8,128)(2,1)S(1)} %collective-permute-done.10.refs_1_), channel_id=1, source_target_pairs={{0,32},{1,225},{2,34},{3,227},{4,36},{5,229},{6,38},{7,231},{8,40}... | collective-permute-start | bytes 786440 | tf_op jit(solution)/shard_map/ppermute | solution.py:475
  65.4 18.4 %collective-permute-start.13 = (bf16[32,2048]{1,0:T(8,128)(2,1)S(1)}, bf16[32,2048]{1,0:T(8,128)(2,1)S(1)}, u32[]{:S(2)}, u32[]{:S(2)}) collective-permute-start(bf16[32,2048]{1,0:T(8,128)(2,1)S(1)} %slice.29), channel_id=1, source_target_pairs={{0,1},{1,0},{2,3},{3,2},{4,5},{5,4},{6,7},{7,6},{8,9},{9,8},{10,11... | collective-permute-start | bytes 393224 | tf_op jit(solution)/shard_map/ppermute | solution.py:473
  83.8 14.4 %collective-permute-start.15 = (bf16[32,2048]{1,0:T(8,128)(2,1)S(1)}, bf16[32,2048]{1,0:T(8,128)(2,1)S(1)}, u32[]{:S(2)}, u32[]{:S(2)}) collective-permute-start(bf16[32,2048]{1,0:T(8,128)(2,1)S(1)} %get-tuple-element.87), channel_id=1, source_target_pairs={{0,1},{1,0},{2,3},{3,2},{4,5},{5,4},{6,7},{7,6},{8,9},{9,8},{10,11... | collective-permute-start | bytes 393224 | tf_op jit(solution)/shard_map/ppermute | solution.py:473
  84.3 14.0 %collective-permute-start.14 = (bf16[32,2048]{1,0:T(8,128)(2,1)S(1)}, bf16[32,2048]{1,0:T(8,128)(2,1)S(1)}, u32[]{:S(2)}, u32[]{:S(2)}) collective-permute-start(bf16[32,2048]{1,0:T(8,128)(2,1)S(1)} %get-tuple-element.88), channel_id=1, source_target_pairs={{0,32},{1,225},{2,34},{3,227},{4,36},{5,229},{6,38},{7,231},{8,40}... | collective-permute-start | bytes 393224 | tf_op jit(solution)/shard_map/ppermute | solution.py:475
  96.3 21.5 %copy-start.1 = (s32[256]{0:T(256)S(1)}, s32[256]{0:T(256)}, u32[]{:S(2)}) copy-start(s32[256]{0:T(256)} %param.14) | copy-start | bytes 3076
  110.8 23.0 %copy-start.2 = (s32[8]{0:T(128)S(1)}, s32[8]{0:T(128)}, u32[]{:S(2)}) copy-start(s32[8]{0:T(128)} %param.15) | copy-start | bytes 100
  114.3 46.6 %copy-start = (bf16[2048,256]{1,0:T(8,128)(2,1)S(1)}, bf16[2048,256]{1,0:T(8,128)(2,1)}, u32[]{:S(2)}) copy-start(bf16[2048,256]{1,0:T(8,128)(2,1)} %get-tuple-element.64.head) | copy-start | bytes 3145732
  114.3 10.6 %all-to-all-start.5 = ((f32[8,16,128]{2,1,0:T(8,128)}), f32[8,16,128]{2,1,0:T(8,128)S(1)}, u32[]{:S(2)}, u32[]{:S(2)}) async-start(f32[8,16,128]{2,1,0:T(8,128)} %get-tuple-element.63), calls=%async_computation.5 | async-start | bytes 131072 | tf_op jit(solution)/shard_map/all_to_all | solution.py:337
  128.7 18.3 %all-to-all-start.6 = ((f32[32,8,640]{2,1,0:T(8,128)}), f32[32,8,640]{2,1,0:T(8,128)S(1)}, u32[]{:S(2)}, u32[]{:S(2)}) async-start(f32[32,8,640]{2,1,0:T(8,128)} %bitcast.5), calls=%async_computation.6 | async-start | bytes 1310720 | tf_op jit(solution)/shard_map/all_to_all | solution.py:337

commit v4 on v3

--- a/solution.py
+++ b/solution.py
@@ -85,13 +85,13 @@
     settle(fetch([(hidden.at[at, :], staged.at[at, :]) for at in rows], sems))
 
 
-def neck_kernel(core, hidden, mine, other, unit, student, head, full, sems):
+def neck_kernel(here, hidden, mine, other, unit, student, head, full, sems):
     chips, rows, double = mine.shape
     width = double // 2
     for chip in range(chips):
         at = 2 * rows * chip
-        near = pl.ds(pl.multiple_of(at + core[0] * rows, rows), rows)
-        away = pl.ds(pl.multiple_of(at + (1 - core[0]) * rows, rows), rows)
+        near = pl.ds(pl.multiple_of(at + here[1] * rows, rows), rows)
+        away = pl.ds(pl.multiple_of(at + (1 - here[1]) * rows, rows), rows)
         head[near, :] = mine[chip, :, :width]
         head[away, :] = other[chip, :, :width]
         full[near, :] = mine[chip, :, width:]
@@ -209,8 +209,8 @@
 
 
 def student_kernel(index, hidden, head, unit, teacher, student, *refs):
-    masked, scale_out, unit_out, norm, grad, total = refs[:6]
-    v_hidden, v_head, v_unit, v_teacher, whole, sems = refs[6:]
+    masked, scale_out, unit_out, grad, total = refs[:5]
+    v_hidden, v_head, v_unit, v_teacher, whole, sems = refs[5:]
     copies = fetch(
         [
             (hidden, v_hidden),
@@ -226,8 +226,9 @@
     neck = dot(v_hidden[...], v_head[...])
     scale = lax.rsqrt(jnp.sum(neck * neck, axis=1, keepdims=True) + norm_eps)
     unit_float = neck * scale
-    unit_out[...] = unit_float
-    norm[...] = jnp.broadcast_to(scale, norm.shape)
+    width = v_head.shape[1]
+    unit_out[:, :width] = unit_float
+    unit_out[:, width:] = jnp.broadcast_to(scale, (unit_float.shape[0], 128))
     student = unit_float.astype(bf16)
     settle(copies[2:])
     wanted = jnp.broadcast_to(index[...].astype(f32), (128, slots)).T[:, 0:1]
@@ -252,81 +253,80 @@
     total[...] = jnp.broadcast_to(total_acc, total.shape)
 
 
-def goal_kernel(
-    parts, masked, scale_p, whole, grad, total, out, v_masked, v_scale, v_whole, v_total, sems
-):
+def goal_kernel(parts, masked, unit, scale_p, whole, grad, total, out, v_scale, v_whole, v_total, sems):
     slots, width = grad.shape
     step = 512
     count = whole.shape[1] // step
     copies = fetch([(scale_p, v_scale), (total, v_total), (grad, out.at[:, :width])], sems)
-    blocks = []
-    for c in range(count):
-        at = pl.ds(c * step, step)
-        blocks.append(
-            fetch(
-                [(masked.at[:, at], v_masked.at[:, at]), (whole.at[:, at], v_whole.at[:, at])],
-                sems,
-                3 + 2 * c,
-            )
-        )
+    blocks = [pl.ds(c * step, step) for c in range(count)]
+    blocks = fetch([(whole.at[:, at], v_whole.at[:, at]) for at in blocks], sems, 3)
     inverse = 1.0 / jnp.sum(parts[...], axis=0)
     grad_acc = jnp.zeros((slots, width), f32)
     goal_acc = jnp.zeros((slots, 128), f32)
     settle(copies[:1])
     for c in range(count):
-        settle(blocks[c])
         pieces = []
         for k in range(c * (step // 128), (c + 1) * (step // 128)):
             at = slice(k * 128, (k + 1) * 128)
-            goal = v_masked[:, at] * inverse[k : k + 1, :]
+            goal = masked[:, at] * inverse[k : k + 1, :]
             goal_acc = goal_acc + goal
             pieces.append(goal * v_scale[0:1, at])
         high, low = split(jnp.concatenate(pieces, axis=1))
+        blocks[c].wait()
         weights = v_whole[:, c * step : (c + 1) * step]
         grad_acc = grad_acc + dot(high, weights, NT) + dot(low, weights, NT)
     out[:, width : 2 * width] = grad_acc
     goal_total = jnp.sum(goal_acc, axis=1, keepdims=True)
+    rounded = unit[:, :width].astype(bf16).astype(f32)
+    goal_dot = jnp.sum(rounded * grad_acc, axis=1, keepdims=True)
     lane = lax.broadcasted_iota(jnp.int32, (slots, 128), 1)
     settle(copies[1:])
-    out[:, 2 * width :] = jnp.where(lane == 0, v_total[...], goal_total)
-
-
-def slots_kernel(place, parts, unit_float, norm, out, v_unit, v_norm, sems):
-    share, width = parts.shape[1], unit_float.shape[1]
-    at = pl.multiple_of(place[0] * share, share)
-    copies = fetch(
-        [(unit_float.at[pl.ds(at, share), :], v_unit), (norm.at[pl.ds(at, share), :], v_norm)], sems
-    )
+    sums = jnp.where(lane == 0, v_total[...], jnp.where(lane == 1, goal_total, goal_dot)).T
+    rows = [sums[k : k + 1, c : c + 128] for k in range(3) for c in range(0, slots, 128)]
+    tile = jnp.concatenate(rows + [jnp.zeros((8 - len(rows), 128), f32)], axis=0)
+    out[:, 2 * width :] = jnp.broadcast_to(tile[None], (slots // 8, 8, 128)).reshape(slots, 128)
+
+
+def slots_kernel(here, counts, parts, unit_float, out, loss):
+    count = counts[here[0]]
+    share, width = parts.shape[1], unit_float.shape[1] - 128
     mine = jnp.sum(parts[...], axis=0)
-    settle(copies)
-    unit = v_unit[...]
-    scale = v_norm[:, 0:1]
-    soft_total = mine[:, 2 * width : 2 * width + 1]
-    goal_total = mine[:, 2 * width + 1 : 2 * width + 2]
+    sums = mine[:, 2 * width :]
+    slot = 128 * lax.broadcasted_iota(jnp.int32, (2, 128), 0)
+    slot = slot + lax.broadcasted_iota(jnp.int32, (2, 128), 1)
+    live = jnp.where(slot < count, 1.0, 0.0)
+    loss[...] = live * (jnp.log(sums[0:2, :]) - sums[4:6, :] / sums[2:4, :])
+    at = pl.multiple_of(here[2] * share, share)
+    row = lax.div(at, 128)
+    pick = lax.broadcasted_iota(jnp.int32, (share, 128), 1) == (
+        lax.rem(at, 128) + lax.broadcasted_iota(jnp.int32, (share, 128), 0)
+    )
+
+    def column(first, second):
+        line = jnp.where(row == 0, first, second)
+        return jnp.sum(jnp.where(pick, line, 0.0), axis=1, keepdims=True)
+
+    soft_total = column(sums[0:1, :], sums[1:2, :])
+    goal_total = column(sums[2:3, :], sums[3:4, :])
+    unit = unit_float[pl.ds(at, share), :width]
+    scale = unit_float[pl.ds(at, share), width : width + 1]
     soft, goal = mine[:, :width] / soft_total, mine[:, width : 2 * width] / goal_total
     slot = at + lax.broadcasted_iota(jnp.int32, (share, 1), 0)
-    live = jnp.where(slot < place[1], 1.0, 0.0)
-    target_dot = jnp.sum(unit.astype(bf16).astype(f32) * goal, axis=1, keepdims=True)
-    loss = live * (jnp.log(soft_total) - target_dot)
-    unit_grad = live * (soft - goal)
+    unit_grad = jnp.where(slot < count, soft - goal, 0.0)
     inner = jnp.sum(unit * unit_grad, axis=1, keepdims=True)
     neck_grad = scale * (unit_grad - unit * inner)
-    top = loss.astype(bf16).astype(f32)
-    mid = (loss - top).astype(bf16).astype(f32)
-    low = loss - top - mid
-    lane = lax.broadcasted_iota(jnp.int32, (share, width), 1)
-    tail = jnp.where(lane == 0, top, jnp.where(lane == 1, mid, jnp.where(lane == 2, low, 0.0)))
-    both = jnp.concatenate([neck_grad, tail], axis=0).astype(bf16)
-    out[...] = jnp.broadcast_to(both[None], out.shape)
-
-
-def hidden_kernel(parts, head, hidden, loss):
-    count, double, width = parts.shape
+    halves = jnp.concatenate([neck_grad[:, : width // 2], neck_grad[:, width // 2 :]], axis=0)
+    out[...] = jnp.broadcast_to(halves.astype(bf16)[None], out.shape)
+
+
+def hidden_kernel(parts, head, hidden):
+    count, double, half = parts.shape
     share = double // 2
     wide = parts[...].astype(f32)
-    neck_grad = wide[:, :share, :].reshape(count * share, width).astype(bf16)
-    tail = wide[:, share:, :128].reshape(count * share, 128).T
-    loss[...] = tail[0:1, :] + tail[1:2, :] + tail[2:3, :]
+    halves = [
+        wide[:, k * share : (k + 1) * share, :].reshape(count * share, half) for k in range(2)
+    ]
+    neck_grad = jnp.concatenate(halves, axis=1).astype(bf16)
     step = 512
     for c in range(head.shape[0] // step):
         at = slice(c * step, (c + 1) * step)
@@ -354,8 +354,7 @@
     width, local = head_teacher.shape[1], proto_teacher.shape[1]
     lines = local // 128
     share = slots // protos
-    core, here = (proto % 2).reshape(1), jnp.stack([tok, proto % 2])
-    place = jnp.stack([proto, jnp.take(mask_count, tok)])
+    here = jnp.stack([tok, proto % 2, proto])
     dma = pltpu.SemaphoreType.DMA
 
     swap = [(i, i ^ 1) for i in range(protos)]
@@ -415,7 +414,7 @@
         (VM, HB),
         (2 * tok_dev * depth * width, 10 * MIB),
         [pltpu.VMEM((depth, width), bf16), pltpu.VMEM((depth, width), bf16), dma((1,))],
-    )(core, held(staged), mine, other)
+    )(here, held(staged), mine, other)
 
     blocks = came + crossed
     scores, whole_teacher, unit_kept, columns = call(
@@ -488,18 +487,17 @@
     columns, whole_student = lax.optimization_barrier((columns, whole_student))
 
     rows = toks * rows
-    masked, scale_p, unit_float, norm, grad, soft_total = call(
+    masked, scale_p, unit_float, grad, soft_total = call(
         student_kernel,
         (
-            pltpu.HBM((slots, local), f32),
+            pltpu.VMEM((slots, local), f32),
             pltpu.HBM((8, local), f32),
-            pltpu.HBM((slots, width), f32),
-            pltpu.HBM((slots, 128), f32),
+            pltpu.VMEM((slots, width + 128), f32),
             pltpu.HBM((slots, width), f32),
             pltpu.HBM((slots, 128), f32),
         ),
         [VM] + [HB] * 5,
-        (VM,) * 6,
+        (VM,) * 5,
         (10 * slots * local * width, 8 * MIB),
         [
             pltpu.VMEM((slots, depth), bf16),
@@ -521,38 +519,37 @@
     parts = call(
         goal_kernel,
         shaped((slots, 2 * width + 128), f32),
-        [VM] + [HB] * 5,
+        [VM] * 3 + [HB] * 4,
         VM,
         (4 * slots * local * width, 4 * MIB),
         [
-            pltpu.VMEM((slots, local), f32),
             pltpu.VMEM((8, local), f32),
             pltpu.VMEM((rows, local), bf16),
             pltpu.VMEM((slots, 128), f32),
-            dma((3 + 2 * local // 512,)),
+            dma((3 + local // 512,)),
         ],
     )(
         exchange(columns, "tok"),
-        far(masked),
+        held(masked),
+        held(unit_float),
         far(scale_p),
         far(whole_student),
         far(grad),
         far(soft_total),
     )
     parts = exchange(parts.reshape(protos, share, 2 * width + 128), "proto")
-    finals = call(
+    finals, row_loss = call(
         slots_kernel,
-        shaped((protos, 2 * share, width), bf16),
-        [SM, VM, HB, HB],
+        (shaped((protos, 2 * share, width // 2), bf16), shaped((slots // 128, 128), f32)),
+        [SM, SM, VM, VM],
+        (VM, VM),
+        (2 * slots * width, MIB),
+    )(here, mask_count, parts, held(unit_float))
+    hidden_grad = call(
+        hidden_kernel,
+        shaped(student_hidden.shape, bf16),
+        [VM, VM],
         VM,
-        (2 * slots * width, MIB),
-        [pltpu.VMEM((share, width), f32), pltpu.VMEM((share, 128), f32), dma((2,))],
-    )(place, parts, far(unit_float), far(norm))
-    hidden_grad, row_loss = call(
-        hidden_kernel,
-        (shaped(student_hidden.shape, bf16), shaped((1, slots), f32)),
-        [VM, VM],
-        (VM, VM),
         (2 * slots * width * depth, 3 * MIB),
     )(exchange(finals, "proto"), full_head)
     return (row_loss.reshape(slots), hidden_grad)

time: 163 us -> 162 us (level)
  blocking collectives: 61 us -> 77.1 us
  waiting for transfers between devices: 20.8 us -> 9.58 us
  starting transfers between devices: 42.8 us -> 37.9 us
    all_to_all x5 -> x6, blocking collectives: 61 us -> 77.1 us  [exchange(): lax.all_to_all(blocks, axis, 0, 0, tiled=True, axis_index_groups=groups)]
    all_to_all x3 -> x2, waiting for transfers between devices: 13 us -> 1.75 us  [exchange(): lax.all_to_all(blocks, axis, 0, 0, tiled=True, axis_index_groups=groups)]
    all_to_all x3 -> x2, starting transfers between devices: 16.3 us -> 11.7 us  [exchange(): lax.all_to_all(blocks, axis, 0, 0, tiled=True, axis_index_groups=groups)]
  transfers between devices with their start and end apart: 19 -> 18, of which waited for: 5 -> 4; matrix products, arithmetic and copies ran while one was open for 0% -> 0% of each run, Pallas kernels for 14% -> 14%
where the time goes in v4:
time: 162 us; the launch traced here: 161 us
  blocking collectives  77.1 us (48%)
  starting transfers between devices  37.9 us (23%)
  Pallas kernels  35.7 us (22%)
  waiting for transfers between devices  9.58 us (6%)
    all_to_all x6, blocking collectives, exchange(): lax.all_to_all(blocks, axis, 0, 0, tiled=True, axis_index_groups=groups)  77.1 us
    ppermute x4, starting transfers between devices, shards(): lax.ppermute(sent if hop < hops - 1 else sent[:rows], ('tok', 'proto'), a...  14.7 us
    all_to_all x2, starting transfers between devices, exchange(): lax.all_to_all(blocks, axis, 0, 0, tiled=True, axis_index_groups=groups)  11.7 us
    ppermute x4, waiting for transfers between devices, shards(): lax.ppermute(sent if hop < hops - 1 else sent[:rows], ('tok', 'proto'), a...  6.64 us
    pallas_call x1, Pallas kernels, shards(): call(student_kernel, (pltpu.VMEM((slots, local), f32), pltpu.HBM((8, loca...  5.38 us
    pallas_call x1, Pallas kernels, shards(): call(scores_kernel, (pltpu.VMEM((tok_dev, local), bf16), pltpu.HBM((toks...  4.34 us
    pallas_call x1, Pallas kernels, shards(): call(goal_kernel, shaped((slots, 2 * width + 128), f32), [VM] * 3 + [HB]...  4.25 us
    pallas_call x1, Pallas kernels, shards(): call(neck_kernel, (shaped((tok_dev, width), bf16), pltpu.HBM((depth, widt...  4.01 us
  transfers between devices with their start and end apart: 18, of which 4 were waited for; matrix products, arithmetic and copies ran while one was open for 0% of the time, Pallas kernels for 14%

profile of v4, /device:TPU:1, one launch (start us, length us, event | category | flops | bytes accessed | tf_op | source)
XLA Modules:
  0.0 161.4 jit_solution(5640768819810694099)
XLA Ops:
  0.6 2.0 %shard_map.95 = (bf16[16,64,512]{2,1,0:T(8,128)(2,1)}, bf16[64,2048]{1,0:T(8,128)(2,1)S(1)}) custom-call(bf16[64,256]{1,0:T(8,128)(2,1)} %teacher.1, bf16[64,256]{1,0:T(8,128)(2,1)} %student.1, bf16[32,2048]{1,0:T(8,128)(2,1)} %first.1, bf16[32,2048]{1,0:T(8,128)(2,1)} %second.1), custom_call_target="tpu_custom_call" | custom-call | bytes 1048576 | tf_op jit(solution)/shard_map/pallas_call | solution.py:370
  2.6 7.6 %all-to-all-start = ((bf16[16,64,512]{2,1,0:T(8,128)(2,1)}), bf16[16,64,512]{2,1,0:T(8,128)(2,1)S(1)}, u32[]{:S(2)}, u32[]{:S(2)}) async-start(bf16[16,64,512]{2,1,0:T(8,128)(2,1)} %get-tuple-element.38), calls=%async_computation | async-start | bytes 2097152 | tf_op jit(solution)/shard_map/all_to_all | solution.py:337
  10.3 1.0 collective-permute-start
  11.3 1.2 collective-permute-done.other
  12.5 5.7 %collective-permute-start.1 = (bf16[64,2048]{1,0:T(8,128)(2,1)S(1)}, bf16[64,2048]{1,0:T(8,128)(2,1)S(1)}, u32[]{:S(2)}, u32[]{:S(2)}) collective-permute-start(bf16[64,2048]{1,0:T(8,128)(2,1)S(1)} %get-tuple-element.40), channel_id=1, source_target_pairs={{0,32},{1,225},{2,34},{3,227},{4,36},{5,229},{6,38},{7,231},{8,40}... | collective-permute-start | bytes 786440 | tf_op jit(solution)/shard_map/ppermute | solution.py:393
  18.1 3.3 %collective-permute-done.1.refs_0_ = bf16[64,2048]{1,0:T(8,128)(2,1)S(1)} collective-permute-done((bf16[64,2048]{1,0:T(8,128)(2,1)S(1)}, bf16[64,2048]{1,0:T(8,128)(2,1)S(1)}, u32[]{:S(2)}, u32[]{:S(2)}) %collective-permute-start.1) | collective-permute-done | bytes 262176 | tf_op jit(solution)/shard_map/ppermute | solution.py:393
  21.5 3.4 %collective-permute-start.2 = (bf16[64,2048]{1,0:T(8,128)(2,1)S(1)}, bf16[64,2048]{1,0:T(8,128)(2,1)S(1)}, u32[]{:S(2)}, u32[]{:S(2)}) collective-permute-start(bf16[64,2048]{1,0:T(8,128)(2,1)S(1)} %collective-permute-done.1.refs_0_), channel_id=1, source_target_pairs={{0,32},{1,225},{2,34},{3,227},{4,36},{5,229},{6,38},{7,231},{8,40}... | collective-permute-start | bytes 786440 | tf_op jit(solution)/shard_map/ppermute | solution.py:393
  24.9 3.3 %collective-permute-done.2.refs_1_ = bf16[64,2048]{1,0:T(8,128)(2,1)S(1)} collective-permute-done((bf16[64,2048]{1,0:T(8,128)(2,1)S(1)}, bf16[64,2048]{1,0:T(8,128)(2,1)S(1)}, u32[]{:S(2)}, u32[]{:S(2)}) %collective-permute-start.2) | collective-permute-done | bytes 262176 | tf_op jit(solution)/shard_map/ppermute | solution.py:393
  28.2 0.0 all-to-all-done.mine
  28.2 2.5 %collective-permute-start.3 = (bf16[16,64,512]{2,1,0:T(8,128)(2,1)S(1)}, bf16[16,64,512]{2,1,0:T(8,128)(2,1)S(1)}, u32[]{:S(2)}, u32[]{:S(2)}) collective-permute-start(bf16[16,64,512]{2,1,0:T(8,128)(2,1)S(1)} %all-to-all-done.mine), channel_id=1, source_target_pairs={{0,1},{1,0},{2,3},{3,2},{4,5},{5,4},{6,7},{7,6},{8,9},{9,8},{10,11... | collective-permute-start | bytes 3145736 | tf_op jit(solution)/shard_map/ppermute | solution.py:398
  30.7 3.7 %collective-permute-start.4 = (bf16[64,2048]{1,0:T(8,128)(2,1)S(1)}, bf16[64,2048]{1,0:T(8,128)(2,1)S(1)}, u32[]{:S(2)}, u32[]{:S(2)}) collective-permute-start(bf16[64,2048]{1,0:T(8,128)(2,1)S(1)} %collective-permute-done.2.refs_1_), channel_id=1, source_target_pairs={{0,32},{1,225},{2,34},{3,227},{4,36},{5,229},{6,38},{7,231},{8,40}... | collective-permute-start | bytes 786440 | tf_op jit(solution)/shard_map/ppermute | solution.py:393
  34.5 0.1 pad_add_fusion.here
  34.6 0.1 collective-permute-start.6
  34.7 0.6 collective-permute-start.7
  35.3 3.5 %shard_map.97.hidden = bf16[2048,2048]{1,0:T(8,128)(2,1)S(1)} custom-call(bf16[2048,2048]{1,0:T(8,128)(2,1)} %hidden.1), custom_call_target="tpu_custom_call" | custom-call | bytes 16777216 | tf_op jit(solution)/shard_map/pallas_call | solution.py:402
  38.8 0.0 collective-permute-done.4.refs_2_
  38.8 0.4 collective-permute-start.8
  39.2 1.9 %collective-permute-start.5 = (bf16[32,2048]{1,0:T(8,128)(2,1)S(1)}, bf16[32,2048]{1,0:T(8,128)(2,1)S(1)}, u32[]{:S(2)}, u32[]{:S(2)}) collective-permute-start(bf16[32,2048]{1,0:T(8,128)(2,1)S(1)} %get-tuple-element.77), channel_id=1, source_target_pairs={{0,32},{1,225},{2,34},{3,227},{4,36},{5,229},{6,38},{7,231},{8,40}... | collective-permute-start | bytes 393224 | tf_op jit(solution)/shard_map/ppermute | solution.py:393
  41.1 0.0 collective-permute-done.3.other
  41.1 0.6 collective-permute-start.9
  41.7 4.0 %shard_map.98 = (bf16[2048,256]{1,0:T(8,128)(2,1)S(1)}, bf16[2048,256]{1,0:T(8,128)(2,1)}) custom-call(s32[3]{0:T(128)S(1)} %pad_add_fusion.here, bf16[2048,2048]{1,0:T(8,128)(2,1)S(1)} %shard_map.97.hidden, bf16[16,64,512]{2,1,0:T(8,128)(2,1)S(1)} %all-to-all-done.mine, bf16[16,64,512]{2,1,0:T(8,128)(2,1)S(1)} %collective-permute-done.3.other), custom_call_target="tpu_custom_call" | custom-call | flops 2147483648 | bytes 10485760 | tf_op jit(solution)/shard_map/pallas_call | solution.py:410
  45.7 0.0 collective-permute-done.6.refs_4_
  45.7 0.0 collective-permute-done.7.refs_5_
  45.7 0.0 collective-permute-done.8.refs_6_
  45.7 0.0 collective-permute-done.5.refs_3_
  45.8 4.3 %shard_map.99 = (bf16[2048,2048]{1,0:T(8,128)(2,1)S(1)}, bf16[256,2048]{1,0:T(8,128)(2,1)}, bf16[2048,256]{1,0:T(8,128)(2,1)}, f32[8,16,128]{2,1,0:T(8,128)S(1)}) custom-call(s32[3]{0:T(128)S(1)} %pad_add_fusion.here, bf16[2048,256]{1,0:T(8,128)(2,1)S(1)} %get-tuple-element.43.unit, bf16[64,2048]{1,0:T(8,128)(2,1)S(1)} %get-tuple-element.39.mine.own, ...), custom_call_target="tpu_custom_call" | custom-call | flops 2147483648 | bytes 12582912 | tf_op jit(solution)/shard_map/pallas_call | solution.py:420
  50.1 0.0 collective-permute-done.9.refs_0_
  50.1 0.8 collective-permute-start.10
  50.9 0.1 collective-permute-start.11
  51.0 12.0 %all_to_all.40.parts = f32[8,16,128]{2,1,0:T(8,128)S(1)} all-to-all(f32[8,16,128]{2,1,0:T(8,128)S(1)} %get-tuple-element.47), channel_id=1, replica_groups=mesh['tok'=8,'proto'=32] {'tok'}, dimensions={0} | all-to-all | bytes 131072 | tf_op jit(solution)/shard_map/all_to_all | solution.py:337
  63.1 2.0 %shard_map.100 = bf16[32,16,128]{2,1,0:T(8,128)(2,1)S(1)} custom-call(f32[8,16,128]{2,1,0:T(8,128)S(1)} %all_to_all.40.parts, bf16[2048,2048]{1,0:T(8,128)(2,1)S(1)} %get-tuple-element.48.scores), custom_call_target="tpu_custom_call" | custom-call | flops 8388608 | bytes 8388608 | tf_op jit(solution)/shard_map/pallas_call | solution.py:478
  65.0 0.0 collective-permute-done.11.refs_4_
  65.0 0.0 collective-permute-done.10.refs_1_
  65.1 0.3 collective-permute-start.12
  65.4 2.1 %collective-permute-start.13 = (bf16[32,2048]{1,0:T(8,128)(2,1)S(1)}, bf16[32,2048]{1,0:T(8,128)(2,1)S(1)}, u32[]{:S(2)}, u32[]{:S(2)}) collective-permute-start(bf16[32,2048]{1,0:T(8,128)(2,1)S(1)} %slice.29), channel_id=1, source_target_pairs={{0,1},{1,0},{2,3},{3,2},{4,5},{5,4},{6,7},{7,6},{8,9},{9,8},{10,11... | collective-permute-start | bytes 393224 | tf_op jit(solution)/shard_map/ppermute | solution.py:472
  67.5 14.0 %all_to_all.41.parts = bf16[32,16,128]{2,1,0:T(8,128)(2,1)S(1)} all-to-all(bf16[32,16,128]{2,1,0:T(8,128)(2,1)S(1)} %shard_map.100), channel_id=1, replica_groups=mesh['tok'=8,'proto'=32] {'proto'}, dimensions={0} | all-to-all | bytes 262144 | tf_op jit(solution)/shard_map/all_to_all | solution.py:337
  81.5 2.2 %shard_map.101 = f32[8,16,128]{2,1,0:T(8,128)S(1)} custom-call(bf16[32,16,128]{2,1,0:T(8,128)(2,1)S(1)} %all_to_all.41.parts, bf16[2048,2048]{1,0:T(8,128)(2,1)S(1)} %get-tuple-element.48.scores), custom_call_target="tpu_custom_call" | custom-call | flops 8388608 | bytes 8388608 | tf_op jit(solution)/shard_map/pallas_call | solution.py:480
  83.8 0.0 collective-permute-done.13.refs_5_
  83.8 0.0 collective-permute-done.12.refs_2_
  83.8 0.5 collective-permute-start.15
  84.3 2.4 %collective-permute-start.14 = (bf16[32,2048]{1,0:T(8,128)(2,1)S(1)}, bf16[32,2048]{1,0:T(8,128)(2,1)S(1)}, u32[]{:S(2)}, u32[]{:S(2)}) collective-permute-start(bf16[32,2048]{1,0:T(8,128)(2,1)S(1)} %get-tuple-element.75), channel_id=1, source_target_pairs={{0,32},{1,225},{2,34},{3,227},{4,36},{5,229},{6,38},{7,231},{8,40}... | collective-permute-start | bytes 393224 | tf_op jit(solution)/shard_map/ppermute | solution.py:474
  86.7 9.6 %all_to_all.42.parts = f32[8,16,128]{2,1,0:T(8,128)S(1)} all-to-all(f32[8,16,128]{2,1,0:T(8,128)S(1)} %shard_map.101), channel_id=1, replica_groups=mesh['tok'=8,'proto'=32] {'tok'}, dimensions={0} | all-to-all | bytes 131072 | tf_op jit(solution)/shard_map/all_to_all | solution.py:337
  96.3 0.0 copy-start.1
  96.3 2.0 %shard_map.102 = bf16[32,16,128]{2,1,0:T(8,128)(2,1)S(1)} custom-call(f32[8,16,128]{2,1,0:T(8,128)S(1)} %all_to_all.42.parts, bf16[2048,2048]{1,0:T(8,128)(2,1)S(1)} %get-tuple-element.48.scores), custom_call_target="tpu_custom_call" | custom-call | flops 8388608 | bytes 8388608 | tf_op jit(solution)/shard_map/pallas_call | solution.py:482
  98.2 0.0 collective-permute-done.15.refs_6_
  98.3 0.0 collective-permute-done.14.refs_3_
  98.3 12.6 %all_to_all.43.parts = bf16[32,16,128]{2,1,0:T(8,128)(2,1)S(1)} all-to-all(bf16[32,16,128]{2,1,0:T(8,128)(2,1)S(1)} %shard_map.102), channel_id=1, replica_groups=mesh['tok'=8,'proto'=32] {'proto'}, dimensions={0} | all-to-all | bytes 262144 | tf_op jit(solution)/shard_map/all_to_all | solution.py:337
  110.8 0.0 copy-start.2
  110.8 3.4 %shard_map.103 = (f32[8,16,128]{2,1,0:T(8,128)}, bf16[256,2048]{1,0:T(8,128)(2,1)}) custom-call(s32[3]{0:T(128)S(1)} %pad_add_fusion.here, bf16[32,16,128]{2,1,0:T(8,128)(2,1)S(1)} %all_to_all.43.parts, bf16[2048,2048]{1,0:T(8,128)(2,1)S(1)} %get-tuple-element.48.scores, bf16[64,2048]{1,0:T(8,128)(2,1)S(1)} %get-tuple-element.39.mine.own, ...), custom_call_target="tpu_custom_call" | custom-call | flops 8388608 | bytes 8388608 | tf_op jit(solution)/shard_map/pallas_call | solution.py:484
  114.3 0.0 copy-start
  114.3 4.1 %all-to-all-start.5 = ((f32[8,16,128]{2,1,0:T(8,128)}), f32[8,16,128]{2,1,0:T(8,128)}, u32[]{:S(2)}, u32[]{:S(2)}) async-start(f32[8,16,128]{2,1,0:T(8,128)} %get-tuple-element.62), calls=%async_computation.5 | async-start | bytes 131072 | tf_op jit(solution)/shard_map/all_to_all | solution.py:337
  118.4 0.0 copy-done.1
  118.4 5.4 %shard_map.104 = (f32[256,2048]{1,0:T(8,128)S(1)}, f32[8,2048]{1,0:T(8,128)}, f32[256,384]{1,0:T(8,128)S(1)}, f32[256,256]{1,0:T(8,128)}, f32[256,128]{1,0:T(8,128)}) custom-call(s32[1,256]{1,0:T(1,128)S(1)} %bitcast.7, bf16[256,2048]{1,0:T(8,128)(2,1)} %hidden.2, bf16[2048,256]{1,0:T(8,128)(2,1)} %get-tuple-element.63.head, ...), custom_call_target="tpu_custom_call" | custom-call | flops 1342177280 | bytes 8388608 | tf_op jit(solution)/shard_map/pallas_call | solution.py:490
  123.8 1.8 %all-to-all-done.5.parts = f32[8,16,128]{2,1,0:T(8,128)} async-done(((f32[8,16,128]{2,1,0:T(8,128)}), f32[8,16,128]{2,1,0:T(8,128)}, u32[]{:S(2)}, u32[]{:S(2)}) %all-to-all-start.5) | async-done | bytes 65568 | tf_op jit(solution)/shard_map/all_to_all | solution.py:337
  125.5 4.2 %shard_map.105 = f32[256,640]{1,0:T(8,128)S(1)} custom-call(f32[8,16,128]{2,1,0:T(8,128)} %all-to-all-done.5.parts, f32[256,2048]{1,0:T(8,128)S(1)} %get-tuple-element.67.masked, f32[256,384]{1,0:T(8,128)S(1)} %get-tuple-element.68.unit.unit_float, f32[8,2048]{1,0:T(8,128)} %get-tuple-element.69.scale_p, bf16[256,2048]{1,0:T(8,128)(2,1)} %get-tuple-element.66.student.whole, ...), custom_call_target="tpu_custom_call" | custom-call | flops 536870912 | bytes 4194304 | tf_op jit(solution)/shard_map/pallas_call | solution.py:519
  129.8 17.7 %all_to_all.44.parts = f32[32,8,640]{2,1,0:T(8,128)S(1)} all-to-all(f32[32,8,640]{2,1,0:T(8,128)S(1)} %bitcast.6), channel_id=1, replica_groups=mesh['tok'=8,'proto'=32] {'proto'}, dimensions={0} | all-to-all | bytes 1310720 | tf_op jit(solution)/shard_map/all_to_all | solution.py:337
  147.5 0.0 copy-done.2
  147.5 1.2 shard_map.106
  148.8 11.2 %all_to_all.45.parts = bf16[32,16,128]{2,1,0:T(8,128)(2,1)S(1)} all-to-all(bf16[32,16,128]{2,1,0:T(8,128)(2,1)S(1)} %get-tuple-element.73), channel_id=1, replica_groups=mesh['tok'=8,'proto'=32] {'proto'}, dimensions={0} | all-to-all | bytes 262144 | tf_op jit(solution)/shard_map/all_to_all | solution.py:337
  160.0 0.0 copy-done
  160.0 1.4 shard_map.107
  (7 shorter events, 0.1 us)
Async XLA Ops:
  2.6 25.5 %all-to-all-start = ((bf16[16,64,512]{2,1,0:T(8,128)(2,1)}), bf16[16,64,512]{2,1,0:T(8,128)(2,1)S(1)}, u32[]{:S(2)}, u32[]{:S(2)}) async-start(bf16[16,64,512]{2,1,0:T(8,128)(2,1)} %get-tuple-element.38), calls=%async_computation | async-start | bytes 2097152 | tf_op jit(solution)/shard_map/all_to_all | solution.py:337
  10.3 2.2 %collective-permute-start = (bf16[64,2048]{1,0:T(8,128)(2,1)S(1)}, bf16[64,2048]{1,0:T(8,128)(2,1)S(1)}, u32[]{:S(2)}, u32[]{:S(2)}) collective-permute-start(bf16[64,2048]{1,0:T(8,128)(2,1)S(1)} %get-tuple-element.39.mine.own), channel_id=1, source_target_pairs={{0,1},{1,0},{2,3},{3,2},{4,5},{5,4},{6,7},{7,6},{8,9},{9,8},{10,11... | collective-permute-start | bytes 786440 | tf_op jit(solution)/shard_map/ppermute | solution.py:379
  12.5 9.0 %collective-permute-start.1 = (bf16[64,2048]{1,0:T(8,128)(2,1)S(1)}, bf16[64,2048]{1,0:T(8,128)(2,1)S(1)}, u32[]{:S(2)}, u32[]{:S(2)}) collective-permute-start(bf16[64,2048]{1,0:T(8,128)(2,1)S(1)} %get-tuple-element.40), channel_id=1, source_target_pairs={{0,32},{1,225},{2,34},{3,227},{4,36},{5,229},{6,38},{7,231},{8,40}... | collective-permute-start | bytes 786440 | tf_op jit(solution)/shard_map/ppermute | solution.py:393
  21.5 6.7 %collective-permute-start.2 = (bf16[64,2048]{1,0:T(8,128)(2,1)S(1)}, bf16[64,2048]{1,0:T(8,128)(2,1)S(1)}, u32[]{:S(2)}, u32[]{:S(2)}) collective-permute-start(bf16[64,2048]{1,0:T(8,128)(2,1)S(1)} %collective-permute-done.1.refs_0_), channel_id=1, source_target_pairs={{0,32},{1,225},{2,34},{3,227},{4,36},{5,229},{6,38},{7,231},{8,40}... | collective-permute-start | bytes 786440 | tf_op jit(solution)/shard_map/ppermute | solution.py:393
  28.2 12.9 %collective-permute-start.3 = (bf16[16,64,512]{2,1,0:T(8,128)(2,1)S(1)}, bf16[16,64,512]{2,1,0:T(8,128)(2,1)S(1)}, u32[]{:S(2)}, u32[]{:S(2)}) collective-permute-start(bf16[16,64,512]{2,1,0:T(8,128)(2,1)S(1)} %all-to-all-done.mine), channel_id=1, source_target_pairs={{0,1},{1,0},{2,3},{3,2},{4,5},{5,4},{6,7},{7,6},{8,9},{9,8},{10,11... | collective-permute-start | bytes 3145736 | tf_op jit(solution)/shard_map/ppermute | solution.py:398
  30.7 8.0 %collective-permute-start.4 = (bf16[64,2048]{1,0:T(8,128)(2,1)S(1)}, bf16[64,2048]{1,0:T(8,128)(2,1)S(1)}, u32[]{:S(2)}, u32[]{:S(2)}) collective-permute-start(bf16[64,2048]{1,0:T(8,128)(2,1)S(1)} %collective-permute-done.2.refs_1_), channel_id=1, source_target_pairs={{0,32},{1,225},{2,34},{3,227},{4,36},{5,229},{6,38},{7,231},{8,40}... | collective-permute-start | bytes 786440 | tf_op jit(solution)/shard_map/ppermute | solution.py:393
  34.6 11.1 %collective-permute-start.6 = (bf16[32,2048]{1,0:T(8,128)(2,1)S(1)}, bf16[32,2048]{1,0:T(8,128)(2,1)S(1)}, u32[]{:S(2)}, u32[]{:S(2)}) collective-permute-start(bf16[32,2048]{1,0:T(8,128)(2,1)S(1)} %slice.33), channel_id=1, source_target_pairs={{0,1},{1,0},{2,3},{3,2},{4,5},{5,4},{6,7},{7,6},{8,9},{9,8},{10,11... | collective-permute-start | bytes 393224 | tf_op jit(solution)/shard_map/ppermute | solution.py:395
  34.7 11.0 %collective-permute-start.7 = (bf16[32,2048]{1,0:T(8,128)(2,1)S(1)}, bf16[32,2048]{1,0:T(8,128)(2,1)S(1)}, u32[]{:S(2)}, u32[]{:S(2)}) collective-permute-start(bf16[32,2048]{1,0:T(8,128)(2,1)S(1)} %slice.34), channel_id=1, source_target_pairs={{0,1},{1,0},{2,3},{3,2},{4,5},{5,4},{6,7},{7,6},{8,9},{9,8},{10,11... | collective-permute-start | bytes 393224 | tf_op jit(solution)/shard_map/ppermute | solution.py:395
  38.8 6.9 %collective-permute-start.8 = (bf16[32,2048]{1,0:T(8,128)(2,1)S(1)}, bf16[32,2048]{1,0:T(8,128)(2,1)S(1)}, u32[]{:S(2)}, u32[]{:S(2)}) collective-permute-start(bf16[32,2048]{1,0:T(8,128)(2,1)S(1)} %get-tuple-element.76), channel_id=1, source_target_pairs={{0,1},{1,0},{2,3},{3,2},{4,5},{5,4},{6,7},{7,6},{8,9},{9,8},{10,11... | collective-permute-start | bytes 393224 | tf_op jit(solution)/shard_map/ppermute | solution.py:395
  39.2 6.5 %collective-permute-start.5 = (bf16[32,2048]{1,0:T(8,128)(2,1)S(1)}, bf16[32,2048]{1,0:T(8,128)(2,1)S(1)}, u32[]{:S(2)}, u32[]{:S(2)}) collective-permute-start(bf16[32,2048]{1,0:T(8,128)(2,1)S(1)} %get-tuple-element.77), channel_id=1, source_target_pairs={{0,32},{1,225},{2,34},{3,227},{4,36},{5,229},{6,38},{7,231},{8,40}... | collective-permute-start | bytes 393224 | tf_op jit(solution)/shard_map/ppermute | solution.py:393
  41.1 9.0 %collective-permute-start.9 = (bf16[64,2048]{1,0:T(8,128)(2,1)S(1)}, bf16[64,2048]{1,0:T(8,128)(2,1)S(1)}, u32[]{:S(2)}, u32[]{:S(2)}) collective-permute-start(bf16[64,2048]{1,0:T(8,128)(2,1)S(1)} %get-tuple-element.46), channel_id=1, source_target_pairs={{0,32},{1,225},{2,34},{3,227},{4,36},{5,229},{6,38},{7,231},{8,40}... | collective-permute-start | bytes 786440 | tf_op jit(solution)/shard_map/ppermute | solution.py:401
  50.1 14.9 %collective-permute-start.10 = (bf16[64,2048]{1,0:T(8,128)(2,1)S(1)}, bf16[64,2048]{1,0:T(8,128)(2,1)S(1)}, u32[]{:S(2)}, u32[]{:S(2)}) collective-permute-start(bf16[64,2048]{1,0:T(8,128)(2,1)S(1)} %collective-permute-done.9.refs_0_), channel_id=1, source_target_pairs={{0,32},{1,225},{2,34},{3,227},{4,36},{5,229},{6,38},{7,231},{8,40}... | collective-permute-start | bytes 786440 | tf_op jit(solution)/shard_map/ppermute | solution.py:474
  50.9 14.1 %collective-permute-start.11 = (bf16[32,2048]{1,0:T(8,128)(2,1)S(1)}, bf16[32,2048]{1,0:T(8,128)(2,1)S(1)}, u32[]{:S(2)}, u32[]{:S(2)}) collective-permute-start(bf16[32,2048]{1,0:T(8,128)(2,1)S(1)} %slice.28), channel_id=1, source_target_pairs={{0,1},{1,0},{2,3},{3,2},{4,5},{5,4},{6,7},{7,6},{8,9},{9,8},{10,11... | collective-permute-start | bytes 393224 | tf_op jit(solution)/shard_map/ppermute | solution.py:472
  65.1 18.7 %collective-permute-start.12 = (bf16[64,2048]{1,0:T(8,128)(2,1)S(1)}, bf16[64,2048]{1,0:T(8,128)(2,1)S(1)}, u32[]{:S(2)}, u32[]{:S(2)}) collective-permute-start(bf16[64,2048]{1,0:T(8,128)(2,1)S(1)} %collective-permute-done.10.refs_1_), channel_id=1, source_target_pairs={{0,32},{1,225},{2,34},{3,227},{4,36},{5,229},{6,38},{7,231},{8,40}... | collective-permute-start | bytes 786440 | tf_op jit(solution)/shard_map/ppermute | solution.py:474
  65.4 18.4 %collective-permute-start.13 = (bf16[32,2048]{1,0:T(8,128)(2,1)S(1)}, bf16[32,2048]{1,0:T(8,128)(2,1)S(1)}, u32[]{:S(2)}, u32[]{:S(2)}) collective-permute-start(bf16[32,2048]{1,0:T(8,128)(2,1)S(1)} %slice.29), channel_id=1, source_target_pairs={{0,1},{1,0},{2,3},{3,2},{4,5},{5,4},{6,7},{7,6},{8,9},{9,8},{10,11... | collective-permute-start | bytes 393224 | tf_op jit(solution)/shard_map/ppermute | solution.py:472
  83.8 14.4 %collective-permute-start.15 = (bf16[32,2048]{1,0:T(8,128)(2,1)S(1)}, bf16[32,2048]{1,0:T(8,128)(2,1)S(1)}, u32[]{:S(2)}, u32[]{:S(2)}) collective-permute-start(bf16[32,2048]{1,0:T(8,128)(2,1)S(1)} %get-tuple-element.74), channel_id=1, source_target_pairs={{0,1},{1,0},{2,3},{3,2},{4,5},{5,4},{6,7},{7,6},{8,9},{9,8},{10,11... | collective-permute-start | bytes 393224 | tf_op jit(solution)/shard_map/ppermute | solution.py:472
  84.3 14.0 %collective-permute-start.14 = (bf16[32,2048]{1,0:T(8,128)(2,1)S(1)}, bf16[32,2048]{1,0:T(8,128)(2,1)S(1)}, u32[]{:S(2)}, u32[]{:S(2)}) collective-permute-start(bf16[32,2048]{1,0:T(8,128)(2,1)S(1)} %get-tuple-element.75), channel_id=1, source_target_pairs={{0,32},{1,225},{2,34},{3,227},{4,36},{5,229},{6,38},{7,231},{8,40}... | collective-permute-start | bytes 393224 | tf_op jit(solution)/shard_map/ppermute | solution.py:474
  96.3 22.1 %copy-start.1 = (s32[256]{0:T(256)S(1)}, s32[256]{0:T(256)}, u32[]{:S(2)}) copy-start(s32[256]{0:T(256)} %param.14) | copy-start | bytes 3076
  110.8 36.7 %copy-start.2 = (s32[8]{0:T(128)S(1)}, s32[8]{0:T(128)}, u32[]{:S(2)}) copy-start(s32[8]{0:T(128)} %counts.1) | copy-start | bytes 100
  114.3 45.7 %copy-start = (bf16[2048,256]{1,0:T(8,128)(2,1)S(1)}, bf16[2048,256]{1,0:T(8,128)(2,1)}, u32[]{:S(2)}) copy-start(bf16[2048,256]{1,0:T(8,128)(2,1)} %get-tuple-element.63.head) | copy-start | bytes 3145732
  114.3 11.3 %all-to-all-start.5 = ((f32[8,16,128]{2,1,0:T(8,128)}), f32[8,16,128]{2,1,0:T(8,128)}, u32[]{:S(2)}, u32[]{:S(2)}) async-start(f32[8,16,128]{2,1,0:T(8,128)} %get-tuple-element.62), calls=%async_computation.5 | async-start | bytes 131072 | tf_op jit(solution)/shard_map/all_to_all | solution.py:337

commit v5 on v4

--- a/solution.py
+++ b/solution.py
@@ -85,18 +85,22 @@
     settle(fetch([(hidden.at[at, :], staged.at[at, :]) for at in rows], sems))
 
 
-def neck_kernel(here, hidden, mine, other, unit, student, head, full, sems):
+def neck_kernel(here, hidden, mine, other, unit, student, head, sems):
     chips, rows, double = mine.shape
     width = double // 2
+    near, away = here[1] * rows, (1 - here[1]) * rows
+    near, away = (pl.multiple_of(at, rows) for at in (near, away))
+    copies = fetch(
+        [
+            (mine.at[:, :, width:], student.at[:, pl.ds(near, rows), :]),
+            (other.at[:, :, width:], student.at[:, pl.ds(away, rows), :]),
+        ],
+        sems,
+    )
     for chip in range(chips):
         at = 2 * rows * chip
-        near = pl.ds(pl.multiple_of(at + here[1] * rows, rows), rows)
-        away = pl.ds(pl.multiple_of(at + (1 - here[1]) * rows, rows), rows)
-        head[near, :] = mine[chip, :, :width]
-        head[away, :] = other[chip, :, :width]
-        full[near, :] = mine[chip, :, width:]
-        full[away, :] = other[chip, :, width:]
-    copies = fetch([(full, student)], sems)
+        head[pl.ds(pl.multiple_of(at + near, rows), rows), :] = mine[chip, :, :width]
+        head[pl.ds(pl.multiple_of(at + away, rows), rows), :] = other[chip, :, :width]
     step = 256
     for k in range(hidden.shape[0] // step):
         at = slice(k * step, (k + 1) * step)
@@ -154,7 +158,7 @@
             sums[pl.ds(c * count + k, 1), :] = acc[:, k * 128 : (k + 1) * 128]
         return 0
 
-    lax.fori_loop(0, whole.shape[1] // step, over_columns, 0)
+    lax.fori_loop(0, whole.shape[1] // step, over_columns, 0, unroll=4)
     settle(rest)
     columns[...] = jnp.broadcast_to(sums[...][None], columns.shape)
 
@@ -173,7 +177,7 @@
             sums[pl.ds(i * group + r, 1), :] = jnp.sum(acc.T, axis=0, keepdims=True)
         return 0
 
-    lax.fori_loop(0, scores.shape[0] // (group * 128), over_rows, 0)
+    lax.fori_loop(0, scores.shape[0] // (group * 128), over_rows, 0, unroll=2)
     rows[...] = jnp.broadcast_to(sums[...].astype(rows.dtype)[None], rows.shape)
 
 
@@ -194,7 +198,7 @@
         return tuple(out)
 
     zeros = tuple(jnp.zeros((8, 128), f32) for _ in range(tiles))
-    acc = lax.fori_loop(0, scores.shape[0] // step, over_rows, zeros, unroll=4)
+    acc = lax.fori_loop(0, scores.shape[0] // step, over_rows, zeros, unroll=8)
     total = jnp.concatenate([jnp.sum(a, axis=0, keepdims=True) for a in acc], axis=0)
     columns[...] = jnp.broadcast_to(total[None], columns.shape)
 
@@ -210,7 +214,7 @@
 
 def student_kernel(index, hidden, head, unit, teacher, student, *refs):
     masked, scale_out, unit_out, grad, total = refs[:5]
-    v_hidden, v_head, v_unit, v_teacher, whole, sems = refs[5:]
+    v_hidden, v_head, v_unit, v_teacher, whole, halves, sems = refs[5:]
     copies = fetch(
         [
             (hidden, v_hidden),
@@ -236,7 +240,6 @@
     picked = dot(chosen.astype(f32).astype(bf16), v_unit[...]).astype(bf16)
     fold = LOG2E / teacher_temp
     step = 256
-    grad_acc = jnp.zeros(grad.shape, f32)
     total_acc = jnp.zeros((slots, 1), f32)
     for c in range(whole.shape[1] // step):
         at = slice(c * step, (c + 1) * step)
@@ -247,21 +250,21 @@
         scale_out[:, at] = jnp.broadcast_to(scale_p, (8, step))
         soft = jnp.exp2(dot(student, weights) * (scale_p * LOG2E))
         total_acc = total_acc + jnp.sum(soft, axis=1, keepdims=True)
-        high, low = split(soft * scale_p)
-        grad_acc = grad_acc + dot(high, weights, NT) + dot(low, weights, NT)
-    grad[...] = grad_acc
+        halves[:slots, at], halves[slots:, at] = split(soft * scale_p)
+    both = dot(halves[...], whole[...], NT)
+    grad[...] = both[:slots] + both[slots:]
     total[...] = jnp.broadcast_to(total_acc, total.shape)
 
 
-def goal_kernel(parts, masked, unit, scale_p, whole, grad, total, out, v_scale, v_whole, v_total, sems):
+def goal_kernel(
+    parts, masked, unit, scale_p, whole, grad, total, out, v_scale, v_whole, v_total, halves, sems
+):
     slots, width = grad.shape
     step = 512
     count = whole.shape[1] // step
     copies = fetch([(scale_p, v_scale), (total, v_total), (grad, out.at[:, :width])], sems)
-    blocks = [pl.ds(c * step, step) for c in range(count)]
-    blocks = fetch([(whole.at[:, at], v_whole.at[:, at]) for at in blocks], sems, 3)
+    weights = fetch([(whole, v_whole)], sems, 3)
     inverse = 1.0 / jnp.sum(parts[...], axis=0)
-    grad_acc = jnp.zeros((slots, width), f32)
     goal_acc = jnp.zeros((slots, 128), f32)
     settle(copies[:1])
     for c in range(count):
@@ -271,10 +274,11 @@
             goal = masked[:, at] * inverse[k : k + 1, :]
             goal_acc = goal_acc + goal
             pieces.append(goal * v_scale[0:1, at])
-        high, low = split(jnp.concatenate(pieces, axis=1))
-        blocks[c].wait()
-        weights = v_whole[:, c * step : (c + 1) * step]
-        grad_acc = grad_acc + dot(high, weights, NT) + dot(low, weights, NT)
+        at = slice(c * step, (c + 1) * step)
+        halves[:slots, at], halves[slots:, at] = split(jnp.concatenate(pieces, axis=1))
+    settle(weights)
+    both = dot(halves[...], v_whole[...], NT)
+    grad_acc = both[:slots] + both[slots:]
     out[:, width : 2 * width] = grad_acc
     goal_total = jnp.sum(goal_acc, axis=1, keepdims=True)
     rounded = unit[:, :width].astype(bf16).astype(f32)
@@ -409,12 +413,16 @@
     )(far(hidden))
     unit_teacher, full_head = call(
         neck_kernel,
-        (shaped((tok_dev, width), bf16), pltpu.HBM((depth, width), bf16)),
+        (
+            shaped((tok_dev, width), bf16),
+            pltpu.HBM((chips, depth // chips, width), bf16),
+        ),
         [SM, VM, VM, VM],
         (VM, HB),
         (2 * tok_dev * depth * width, 10 * MIB),
-        [pltpu.VMEM((depth, width), bf16), pltpu.VMEM((depth, width), bf16), dma((1,))],
+        [pltpu.VMEM((depth, width), bf16), dma((2,))],
     )(here, held(staged), mine, other)
+    full_head = full_head.reshape(depth, width)
 
     blocks = came + crossed
     scores, whole_teacher, unit_kept, columns = call(
@@ -505,6 +513,7 @@
             pltpu.VMEM((tok_dev, width), bf16),
             pltpu.VMEM((rows, local), bf16),
             pltpu.VMEM((rows, local), bf16),
+            pltpu.VMEM((2 * slots, local), bf16),
             dma((5,)),
         ],
     )(
@@ -526,7 +535,8 @@
             pltpu.VMEM((8, local), f32),
             pltpu.VMEM((rows, local), bf16),
             pltpu.VMEM((slots, 128), f32),
-            dma((3 + local // 512,)),
+            pltpu.VMEM((2 * slots, local), bf16),
+            dma((4,)),
         ],
     )(
         exchange(columns, "tok"),

time: 162 us -> 159 us (0.981)
  Pallas kernels: 35.7 us -> 32.3 us
  transfers between devices with their start and end apart: 18 -> 18, of which waited for: 4 -> 4; matrix products, arithmetic and copies ran while one was open for 0% -> 0% of each run, Pallas kernels for 14% -> 13%
where the time goes in v5:
time: 159 us
  blocking collectives  77.5 us (49%)
  starting transfers between devices  38.3 us (24%)
  Pallas kernels  32.3 us (20%)
  waiting for transfers between devices  9.55 us (6%)
    all_to_all x6, blocking collectives, exchange(): lax.all_to_all(blocks, axis, 0, 0, tiled=True, axis_index_groups=groups)  77.5 us
    ppermute x4, starting transfers between devices, shards(): lax.ppermute(sent if hop < hops - 1 else sent[:rows], ('tok', 'proto'), a...  14.7 us
    all_to_all x2, starting transfers between devices, exchange(): lax.all_to_all(blocks, axis, 0, 0, tiled=True, axis_index_groups=groups)  11.7 us
    ppermute x4, waiting for transfers between devices, shards(): lax.ppermute(sent if hop < hops - 1 else sent[:rows], ('tok', 'proto'), a...  6.64 us
    pallas_call x1, Pallas kernels, shards(): call(student_kernel, (pltpu.VMEM((slots, local), f32), pltpu.HBM((8, loca...  5.41 us
    ppermute x3, starting transfers between devices, onward(): late.append(lax.ppermute(sent, ('tok', 'proto'), along))  3.94 us
    pallas_call x2, Pallas kernels, shards(): sums = row_call(exchange(columns, 'tok'), held(scores))  3.6 us
    pallas_call x1, Pallas kernels, shards(): call(stage_kernel, pltpu.VMEM(hidden.shape, bf16), [HB], VM, (0, 16 * MIB...  3.5 us
  transfers between devices with their start and end apart: 18, of which 4 were waited for; matrix products, arithmetic and copies ran while one was open for 0% of the time, Pallas kernels for 13%

profile of v5, /device:TPU:1, one launch (start us, length us, event | category | flops | bytes accessed | tf_op | source)
XLA Modules:
  0.0 158.7 jit_solution(10930855352889927494)
XLA Ops:
  0.6 2.0 %shard_map.95 = (bf16[16,64,512]{2,1,0:T(8,128)(2,1)}, bf16[64,2048]{1,0:T(8,128)(2,1)S(1)}) custom-call(bf16[64,256]{1,0:T(8,128)(2,1)} %teacher.1, bf16[64,256]{1,0:T(8,128)(2,1)} %student.1, bf16[32,2048]{1,0:T(8,128)(2,1)} %first.1, bf16[32,2048]{1,0:T(8,128)(2,1)} %second.1), custom_call_target="tpu_custom_call" | custom-call | bytes 1048576 | tf_op jit(solution)/shard_map/pallas_call | solution.py:374
  2.6 7.6 %all-to-all-start = ((bf16[16,64,512]{2,1,0:T(8,128)(2,1)}), bf16[16,64,512]{2,1,0:T(8,128)(2,1)S(1)}, u32[]{:S(2)}, u32[]{:S(2)}) async-start(bf16[16,64,512]{2,1,0:T(8,128)(2,1)} %get-tuple-element.38), calls=%async_computation | async-start | bytes 2097152 | tf_op jit(solution)/shard_map/all_to_all | solution.py:341
  10.3 1.0 collective-permute-start
  11.3 1.2 collective-permute-done.other
  12.5 5.7 %collective-permute-start.1 = (bf16[64,2048]{1,0:T(8,128)(2,1)S(1)}, bf16[64,2048]{1,0:T(8,128)(2,1)S(1)}, u32[]{:S(2)}, u32[]{:S(2)}) collective-permute-start(bf16[64,2048]{1,0:T(8,128)(2,1)S(1)} %get-tuple-element.40), channel_id=1, source_target_pairs={{0,32},{1,225},{2,34},{3,227},{4,36},{5,229},{6,38},{7,231},{8,40}... | collective-permute-start | bytes 786440 | tf_op jit(solution)/shard_map/ppermute | solution.py:397
  18.1 3.3 %collective-permute-done.1.refs_0_ = bf16[64,2048]{1,0:T(8,128)(2,1)S(1)} collective-permute-done((bf16[64,2048]{1,0:T(8,128)(2,1)S(1)}, bf16[64,2048]{1,0:T(8,128)(2,1)S(1)}, u32[]{:S(2)}, u32[]{:S(2)}) %collective-permute-start.1) | collective-permute-done | bytes 262176 | tf_op jit(solution)/shard_map/ppermute | solution.py:397
  21.5 3.4 %collective-permute-start.2 = (bf16[64,2048]{1,0:T(8,128)(2,1)S(1)}, bf16[64,2048]{1,0:T(8,128)(2,1)S(1)}, u32[]{:S(2)}, u32[]{:S(2)}) collective-permute-start(bf16[64,2048]{1,0:T(8,128)(2,1)S(1)} %collective-permute-done.1.refs_0_), channel_id=1, source_target_pairs={{0,32},{1,225},{2,34},{3,227},{4,36},{5,229},{6,38},{7,231},{8,40}... | collective-permute-start | bytes 786440 | tf_op jit(solution)/shard_map/ppermute | solution.py:397
  24.9 3.3 %collective-permute-done.2.refs_1_ = bf16[64,2048]{1,0:T(8,128)(2,1)S(1)} collective-permute-done((bf16[64,2048]{1,0:T(8,128)(2,1)S(1)}, bf16[64,2048]{1,0:T(8,128)(2,1)S(1)}, u32[]{:S(2)}, u32[]{:S(2)}) %collective-permute-start.2) | collective-permute-done | bytes 262176 | tf_op jit(solution)/shard_map/ppermute | solution.py:397
  28.2 0.0 all-to-all-done.mine
  28.2 2.5 %collective-permute-start.3 = (bf16[16,64,512]{2,1,0:T(8,128)(2,1)S(1)}, bf16[16,64,512]{2,1,0:T(8,128)(2,1)S(1)}, u32[]{:S(2)}, u32[]{:S(2)}) collective-permute-start(bf16[16,64,512]{2,1,0:T(8,128)(2,1)S(1)} %all-to-all-done.mine), channel_id=1, source_target_pairs={{0,1},{1,0},{2,3},{3,2},{4,5},{5,4},{6,7},{7,6},{8,9},{9,8},{10,11... | collective-permute-start | bytes 3145736 | tf_op jit(solution)/shard_map/ppermute | solution.py:402
  30.7 3.7 %collective-permute-start.4 = (bf16[64,2048]{1,0:T(8,128)(2,1)S(1)}, bf16[64,2048]{1,0:T(8,128)(2,1)S(1)}, u32[]{:S(2)}, u32[]{:S(2)}) collective-permute-start(bf16[64,2048]{1,0:T(8,128)(2,1)S(1)} %collective-permute-done.2.refs_1_), channel_id=1, source_target_pairs={{0,32},{1,225},{2,34},{3,227},{4,36},{5,229},{6,38},{7,231},{8,40}... | collective-permute-start | bytes 786440 | tf_op jit(solution)/shard_map/ppermute | solution.py:397
  34.5 0.1 pad_add_fusion.here
  34.6 0.1 collective-permute-start.6
  34.7 0.6 collective-permute-start.7
  35.3 3.5 %shard_map.97.hidden = bf16[2048,2048]{1,0:T(8,128)(2,1)S(1)} custom-call(bf16[2048,2048]{1,0:T(8,128)(2,1)} %hidden.1), custom_call_target="tpu_custom_call" | custom-call | bytes 16777216 | tf_op jit(solution)/shard_map/pallas_call | solution.py:406
  38.8 0.0 collective-permute-done.4.refs_2_
  38.8 0.4 collective-permute-start.8
  39.2 1.9 %collective-permute-start.5 = (bf16[32,2048]{1,0:T(8,128)(2,1)S(1)}, bf16[32,2048]{1,0:T(8,128)(2,1)S(1)}, u32[]{:S(2)}, u32[]{:S(2)}) collective-permute-start(bf16[32,2048]{1,0:T(8,128)(2,1)S(1)} %get-tuple-element.77), channel_id=1, source_target_pairs={{0,32},{1,225},{2,34},{3,227},{4,36},{5,229},{6,38},{7,231},{8,40}... | collective-permute-start | bytes 393224 | tf_op jit(solution)/shard_map/ppermute | solution.py:397
  41.1 0.0 collective-permute-done.3.other
  41.1 0.6 collective-permute-start.9
  41.7 3.1 %shard_map.98 = (bf16[2048,256]{1,0:T(8,128)(2,1)S(1)}, bf16[16,128,256]{2,1,0:T(8,128)(2,1)}) custom-call(s32[3]{0:T(128)S(1)} %pad_add_fusion.here, bf16[2048,2048]{1,0:T(8,128)(2,1)S(1)} %shard_map.97.hidden, bf16[16,64,512]{2,1,0:T(8,128)(2,1)S(1)} %all-to-all-done.mine, bf16[16,64,512]{2,1,0:T(8,128)(2,1)S(1)} %collective-permute-done.3.other), custom_call_target="tpu_custom_call" | custom-call | flops 2147483648 | bytes 10485760 | tf_op jit(solution)/shard_map/pallas_call | solution.py:414
  44.8 0.0 collective-permute-done.6.refs_4_
  44.8 0.0 collective-permute-done.7.refs_5_
  44.8 0.0 collective-permute-done.8.refs_6_
  44.8 0.0 collective-permute-done.5.refs_3_
  44.8 3.2 %shard_map.99 = (bf16[2048,2048]{1,0:T(8,128)(2,1)S(1)}, bf16[256,2048]{1,0:T(8,128)(2,1)}, bf16[2048,256]{1,0:T(8,128)(2,1)}, f32[8,16,128]{2,1,0:T(8,128)S(1)}) custom-call(s32[3]{0:T(128)S(1)} %pad_add_fusion.here, bf16[2048,256]{1,0:T(8,128)(2,1)S(1)} %get-tuple-element.43.unit, bf16[64,2048]{1,0:T(8,128)(2,1)S(1)} %get-tuple-element.39.mine.own, ...), custom_call_target="tpu_custom_call" | custom-call | flops 2147483648 | bytes 12582912 | tf_op jit(solution)/shard_map/pallas_call | solution.py:428
  48.0 0.0 collective-permute-done.9.refs_0_
  48.1 1.4 collective-permute-start.10
  49.5 0.1 collective-permute-start.11
  49.6 12.4 %all_to_all.40.parts = f32[8,16,128]{2,1,0:T(8,128)S(1)} all-to-all(f32[8,16,128]{2,1,0:T(8,128)S(1)} %get-tuple-element.47), channel_id=1, replica_groups=mesh['tok'=8,'proto'=32] {'tok'}, dimensions={0} | all-to-all | bytes 131072 | tf_op jit(solution)/shard_map/all_to_all | solution.py:341
  62.0 1.8 %shard_map.100 = bf16[32,16,128]{2,1,0:T(8,128)(2,1)S(1)} custom-call(f32[8,16,128]{2,1,0:T(8,128)S(1)} %all_to_all.40.parts, bf16[2048,2048]{1,0:T(8,128)(2,1)S(1)} %get-tuple-element.48.scores), custom_call_target="tpu_custom_call" | custom-call | flops 8388608 | bytes 8388608 | tf_op jit(solution)/shard_map/pallas_call | solution.py:486
  63.8 0.0 collective-permute-done.11.refs_4_
  63.8 0.0 collective-permute-done.10.refs_1_
  63.8 0.1 collective-permute-start.12
  63.9 2.1 %collective-permute-start.13 = (bf16[32,2048]{1,0:T(8,128)(2,1)S(1)}, bf16[32,2048]{1,0:T(8,128)(2,1)S(1)}, u32[]{:S(2)}, u32[]{:S(2)}) collective-permute-start(bf16[32,2048]{1,0:T(8,128)(2,1)S(1)} %slice.29), channel_id=1, source_target_pairs={{0,1},{1,0},{2,3},{3,2},{4,5},{5,4},{6,7},{7,6},{8,9},{9,8},{10,11... | collective-permute-start | bytes 393224 | tf_op jit(solution)/shard_map/ppermute | solution.py:480
  66.1 14.0 %all_to_all.41.parts = bf16[32,16,128]{2,1,0:T(8,128)(2,1)S(1)} all-to-all(bf16[32,16,128]{2,1,0:T(8,128)(2,1)S(1)} %shard_map.100), channel_id=1, replica_groups=mesh['tok'=8,'proto'=32] {'proto'}, dimensions={0} | all-to-all | bytes 262144 | tf_op jit(solution)/shard_map/all_to_all | solution.py:341
  80.1 2.2 %shard_map.101 = f32[8,16,128]{2,1,0:T(8,128)S(1)} custom-call(bf16[32,16,128]{2,1,0:T(8,128)(2,1)S(1)} %all_to_all.41.parts, bf16[2048,2048]{1,0:T(8,128)(2,1)S(1)} %get-tuple-element.48.scores), custom_call_target="tpu_custom_call" | custom-call | flops 8388608 | bytes 8388608 | tf_op jit(solution)/shard_map/pallas_call | solution.py:488
  82.3 0.0 collective-permute-done.13.refs_5_
  82.3 0.0 collective-permute-done.12.refs_2_
  82.3 0.5 collective-permute-start.15
  82.8 2.4 %collective-permute-start.14 = (bf16[32,2048]{1,0:T(8,128)(2,1)S(1)}, bf16[32,2048]{1,0:T(8,128)(2,1)S(1)}, u32[]{:S(2)}, u32[]{:S(2)}) collective-permute-start(bf16[32,2048]{1,0:T(8,128)(2,1)S(1)} %get-tuple-element.75), channel_id=1, source_target_pairs={{0,32},{1,225},{2,34},{3,227},{4,36},{5,229},{6,38},{7,231},{8,40}... | collective-permute-start | bytes 393224 | tf_op jit(solution)/shard_map/ppermute | solution.py:482
  85.2 9.6 %all_to_all.42.parts = f32[8,16,128]{2,1,0:T(8,128)S(1)} all-to-all(f32[8,16,128]{2,1,0:T(8,128)S(1)} %shard_map.101), channel_id=1, replica_groups=mesh['tok'=8,'proto'=32] {'tok'}, dimensions={0} | all-to-all | bytes 131072 | tf_op jit(solution)/shard_map/all_to_all | solution.py:341
  94.8 0.0 copy-start.1
  94.8 1.8 %shard_map.102 = bf16[32,16,128]{2,1,0:T(8,128)(2,1)S(1)} custom-call(f32[8,16,128]{2,1,0:T(8,128)S(1)} %all_to_all.42.parts, bf16[2048,2048]{1,0:T(8,128)(2,1)S(1)} %get-tuple-element.48.scores), custom_call_target="tpu_custom_call" | custom-call | flops 8388608 | bytes 8388608 | tf_op jit(solution)/shard_map/pallas_call | solution.py:490
  96.6 0.0 collective-permute-done.15.refs_6_
  96.6 0.0 collective-permute-done.14.refs_3_
  96.6 12.6 %all_to_all.43.parts = bf16[32,16,128]{2,1,0:T(8,128)(2,1)S(1)} all-to-all(bf16[32,16,128]{2,1,0:T(8,128)(2,1)S(1)} %shard_map.102), channel_id=1, replica_groups=mesh['tok'=8,'proto'=32] {'proto'}, dimensions={0} | all-to-all | bytes 262144 | tf_op jit(solution)/shard_map/all_to_all | solution.py:341
  109.2 0.0 copy-start.2
  109.2 3.4 %shard_map.103 = (f32[8,16,128]{2,1,0:T(8,128)}, bf16[256,2048]{1,0:T(8,128)(2,1)}) custom-call(s32[3]{0:T(128)S(1)} %pad_add_fusion.here, bf16[32,16,128]{2,1,0:T(8,128)(2,1)S(1)} %all_to_all.43.parts, bf16[2048,2048]{1,0:T(8,128)(2,1)S(1)} %get-tuple-element.48.scores, bf16[64,2048]{1,0:T(8,128)(2,1)S(1)} %get-tuple-element.39.mine.own, ...), custom_call_target="tpu_custom_call" | custom-call | flops 8388608 | bytes 8388608 | tf_op jit(solution)/shard_map/pallas_call | solution.py:492
  112.6 0.0 copy-start
  112.6 4.1 %all-to-all-start.5 = ((f32[8,16,128]{2,1,0:T(8,128)}), f32[8,16,128]{2,1,0:T(8,128)}, u32[]{:S(2)}, u32[]{:S(2)}) async-start(f32[8,16,128]{2,1,0:T(8,128)} %get-tuple-element.62), calls=%async_computation.5 | async-start | bytes 131072 | tf_op jit(solution)/shard_map/all_to_all | solution.py:341
  116.7 0.0 copy-done.1
  116.7 5.4 %shard_map.104 = (f32[256,2048]{1,0:T(8,128)S(1)}, f32[8,2048]{1,0:T(8,128)}, f32[256,384]{1,0:T(8,128)S(1)}, f32[256,256]{1,0:T(8,128)}, f32[256,128]{1,0:T(8,128)}) custom-call(s32[1,256]{1,0:T(1,128)S(1)} %bitcast.10, bf16[256,2048]{1,0:T(8,128)(2,1)} %hidden.2, bf16[2048,256]{1,0:T(8,128)(2,1)} %bitcast.7, bf16[2048,256]{1,0:T(8,128)(2,1)} %get-tuple-element.64.unit, ...), custom_call_target="tpu_custom_call" | custom-call | flops 1342177280 | bytes 8388608 | tf_op jit(solution)/shard_map/pallas_call | solution.py:498
  122.2 1.7 %all-to-all-done.5.parts = f32[8,16,128]{2,1,0:T(8,128)} async-done(((f32[8,16,128]{2,1,0:T(8,128)}), f32[8,16,128]{2,1,0:T(8,128)}, u32[]{:S(2)}, u32[]{:S(2)}) %all-to-all-start.5) | async-done | bytes 65568 | tf_op jit(solution)/shard_map/all_to_all | solution.py:341
  123.9 3.2 %shard_map.105 = f32[256,640]{1,0:T(8,128)S(1)} custom-call(f32[8,16,128]{2,1,0:T(8,128)} %all-to-all-done.5.parts, f32[256,2048]{1,0:T(8,128)S(1)} %get-tuple-element.67.masked, f32[256,384]{1,0:T(8,128)S(1)} %get-tuple-element.68.unit.unit_float, f32[8,2048]{1,0:T(8,128)} %get-tuple-element.69.scale_p, bf16[256,2048]{1,0:T(8,128)(2,1)} %get-tuple-element.66.student.whole, ...), custom_call_target="tpu_custom_call" | custom-call | flops 536870912 | bytes 4194304 | tf_op jit(solution)/shard_map/pallas_call | solution.py:528
  127.1 17.7 %all_to_all.44.parts = f32[32,8,640]{2,1,0:T(8,128)S(1)} all-to-all(f32[32,8,640]{2,1,0:T(8,128)S(1)} %bitcast.9), channel_id=1, replica_groups=mesh['tok'=8,'proto'=32] {'proto'}, dimensions={0} | all-to-all | bytes 1310720 | tf_op jit(solution)/shard_map/all_to_all | solution.py:341
  144.9 0.0 copy-done.2
  144.9 1.2 shard_map.106
  146.1 11.2 %all_to_all.45.parts = bf16[32,16,128]{2,1,0:T(8,128)(2,1)S(1)} all-to-all(bf16[32,16,128]{2,1,0:T(8,128)(2,1)S(1)} %get-tuple-element.73), channel_id=1, replica_groups=mesh['tok'=8,'proto'=32] {'proto'}, dimensions={0} | all-to-all | bytes 262144 | tf_op jit(solution)/shard_map/all_to_all | solution.py:341
  157.3 0.0 copy-done
  157.3 1.4 shard_map.107
  (7 shorter events, 0.1 us)
Async XLA Ops:
  2.6 25.5 %all-to-all-start = ((bf16[16,64,512]{2,1,0:T(8,128)(2,1)}), bf16[16,64,512]{2,1,0:T(8,128)(2,1)S(1)}, u32[]{:S(2)}, u32[]{:S(2)}) async-start(bf16[16,64,512]{2,1,0:T(8,128)(2,1)} %get-tuple-element.38), calls=%async_computation | async-start | bytes 2097152 | tf_op jit(solution)/shard_map/all_to_all | solution.py:341
  10.3 2.2 %collective-permute-start = (bf16[64,2048]{1,0:T(8,128)(2,1)S(1)}, bf16[64,2048]{1,0:T(8,128)(2,1)S(1)}, u32[]{:S(2)}, u32[]{:S(2)}) collective-permute-start(bf16[64,2048]{1,0:T(8,128)(2,1)S(1)} %get-tuple-element.39.mine.own), channel_id=1, source_target_pairs={{0,1},{1,0},{2,3},{3,2},{4,5},{5,4},{6,7},{7,6},{8,9},{9,8},{10,11... | collective-permute-start | bytes 786440 | tf_op jit(solution)/shard_map/ppermute | solution.py:383
  12.5 9.0 %collective-permute-start.1 = (bf16[64,2048]{1,0:T(8,128)(2,1)S(1)}, bf16[64,2048]{1,0:T(8,128)(2,1)S(1)}, u32[]{:S(2)}, u32[]{:S(2)}) collective-permute-start(bf16[64,2048]{1,0:T(8,128)(2,1)S(1)} %get-tuple-element.40), channel_id=1, source_target_pairs={{0,32},{1,225},{2,34},{3,227},{4,36},{5,229},{6,38},{7,231},{8,40}... | collective-permute-start | bytes 786440 | tf_op jit(solution)/shard_map/ppermute | solution.py:397
  21.5 6.7 %collective-permute-start.2 = (bf16[64,2048]{1,0:T(8,128)(2,1)S(1)}, bf16[64,2048]{1,0:T(8,128)(2,1)S(1)}, u32[]{:S(2)}, u32[]{:S(2)}) collective-permute-start(bf16[64,2048]{1,0:T(8,128)(2,1)S(1)} %collective-permute-done.1.refs_0_), channel_id=1, source_target_pairs={{0,32},{1,225},{2,34},{3,227},{4,36},{5,229},{6,38},{7,231},{8,40}... | collective-permute-start | bytes 786440 | tf_op jit(solution)/shard_map/ppermute | solution.py:397
  28.2 12.9 %collective-permute-start.3 = (bf16[16,64,512]{2,1,0:T(8,128)(2,1)S(1)}, bf16[16,64,512]{2,1,0:T(8,128)(2,1)S(1)}, u32[]{:S(2)}, u32[]{:S(2)}) collective-permute-start(bf16[16,64,512]{2,1,0:T(8,128)(2,1)S(1)} %all-to-all-done.mine), channel_id=1, source_target_pairs={{0,1},{1,0},{2,3},{3,2},{4,5},{5,4},{6,7},{7,6},{8,9},{9,8},{10,11... | collective-permute-start | bytes 3145736 | tf_op jit(solution)/shard_map/ppermute | solution.py:402
  30.7 8.0 %collective-permute-start.4 = (bf16[64,2048]{1,0:T(8,128)(2,1)S(1)}, bf16[64,2048]{1,0:T(8,128)(2,1)S(1)}, u32[]{:S(2)}, u32[]{:S(2)}) collective-permute-start(bf16[64,2048]{1,0:T(8,128)(2,1)S(1)} %collective-permute-done.2.refs_1_), channel_id=1, source_target_pairs={{0,32},{1,225},{2,34},{3,227},{4,36},{5,229},{6,38},{7,231},{8,40}... | collective-permute-start | bytes 786440 | tf_op jit(solution)/shard_map/ppermute | solution.py:397
  34.6 10.2 %collective-permute-start.6 = (bf16[32,2048]{1,0:T(8,128)(2,1)S(1)}, bf16[32,2048]{1,0:T(8,128)(2,1)S(1)}, u32[]{:S(2)}, u32[]{:S(2)}) collective-permute-start(bf16[32,2048]{1,0:T(8,128)(2,1)S(1)} %slice.33), channel_id=1, source_target_pairs={{0,1},{1,0},{2,3},{3,2},{4,5},{5,4},{6,7},{7,6},{8,9},{9,8},{10,11... | collective-permute-start | bytes 393224 | tf_op jit(solution)/shard_map/ppermute | solution.py:399
  34.7 10.1 %collective-permute-start.7 = (bf16[32,2048]{1,0:T(8,128)(2,1)S(1)}, bf16[32,2048]{1,0:T(8,128)(2,1)S(1)}, u32[]{:S(2)}, u32[]{:S(2)}) collective-permute-start(bf16[32,2048]{1,0:T(8,128)(2,1)S(1)} %slice.34), channel_id=1, source_target_pairs={{0,1},{1,0},{2,3},{3,2},{4,5},{5,4},{6,7},{7,6},{8,9},{9,8},{10,11... | collective-permute-start | bytes 393224 | tf_op jit(solution)/shard_map/ppermute | solution.py:399
  38.8 6.0 %collective-permute-start.8 = (bf16[32,2048]{1,0:T(8,128)(2,1)S(1)}, bf16[32,2048]{1,0:T(8,128)(2,1)S(1)}, u32[]{:S(2)}, u32[]{:S(2)}) collective-permute-start(bf16[32,2048]{1,0:T(8,128)(2,1)S(1)} %get-tuple-element.76), channel_id=1, source_target_pairs={{0,1},{1,0},{2,3},{3,2},{4,5},{5,4},{6,7},{7,6},{8,9},{9,8},{10,11... | collective-permute-start | bytes 393224 | tf_op jit(solution)/shard_map/ppermute | solution.py:399
  39.2 5.6 %collective-permute-start.5 = (bf16[32,2048]{1,0:T(8,128)(2,1)S(1)}, bf16[32,2048]{1,0:T(8,128)(2,1)S(1)}, u32[]{:S(2)}, u32[]{:S(2)}) collective-permute-start(bf16[32,2048]{1,0:T(8,128)(2,1)S(1)} %get-tuple-element.77), channel_id=1, source_target_pairs={{0,32},{1,225},{2,34},{3,227},{4,36},{5,229},{6,38},{7,231},{8,40}... | collective-permute-start | bytes 393224 | tf_op jit(solution)/shard_map/ppermute | solution.py:397
  41.1 6.9 %collective-permute-start.9 = (bf16[64,2048]{1,0:T(8,128)(2,1)S(1)}, bf16[64,2048]{1,0:T(8,128)(2,1)S(1)}, u32[]{:S(2)}, u32[]{:S(2)}) collective-permute-start(bf16[64,2048]{1,0:T(8,128)(2,1)S(1)} %get-tuple-element.46), channel_id=1, source_target_pairs={{0,32},{1,225},{2,34},{3,227},{4,36},{5,229},{6,38},{7,231},{8,40}... | collective-permute-start | bytes 786440 | tf_op jit(solution)/shard_map/ppermute | solution.py:405
  48.1 15.7 %collective-permute-start.10 = (bf16[64,2048]{1,0:T(8,128)(2,1)S(1)}, bf16[64,2048]{1,0:T(8,128)(2,1)S(1)}, u32[]{:S(2)}, u32[]{:S(2)}) collective-permute-start(bf16[64,2048]{1,0:T(8,128)(2,1)S(1)} %collective-permute-done.9.refs_0_), channel_id=1, source_target_pairs={{0,32},{1,225},{2,34},{3,227},{4,36},{5,229},{6,38},{7,231},{8,40}... | collective-permute-start | bytes 786440 | tf_op jit(solution)/shard_map/ppermute | solution.py:482
  49.5 14.3 %collective-permute-start.11 = (bf16[32,2048]{1,0:T(8,128)(2,1)S(1)}, bf16[32,2048]{1,0:T(8,128)(2,1)S(1)}, u32[]{:S(2)}, u32[]{:S(2)}) collective-permute-start(bf16[32,2048]{1,0:T(8,128)(2,1)S(1)} %slice.28), channel_id=1, source_target_pairs={{0,1},{1,0},{2,3},{3,2},{4,5},{5,4},{6,7},{7,6},{8,9},{9,8},{10,11... | collective-permute-start | bytes 393224 | tf_op jit(solution)/shard_map/ppermute | solution.py:480
  63.8 18.5 %collective-permute-start.12 = (bf16[64,2048]{1,0:T(8,128)(2,1)S(1)}, bf16[64,2048]{1,0:T(8,128)(2,1)S(1)}, u32[]{:S(2)}, u32[]{:S(2)}) collective-permute-start(bf16[64,2048]{1,0:T(8,128)(2,1)S(1)} %collective-permute-done.10.refs_1_), channel_id=1, source_target_pairs={{0,32},{1,225},{2,34},{3,227},{4,36},{5,229},{6,38},{7,231},{8,40}... | collective-permute-start | bytes 786440 | tf_op jit(solution)/shard_map/ppermute | solution.py:482
  63.9 18.4 %collective-permute-start.13 = (bf16[32,2048]{1,0:T(8,128)(2,1)S(1)}, bf16[32,2048]{1,0:T(8,128)(2,1)S(1)}, u32[]{:S(2)}, u32[]{:S(2)}) collective-permute-start(bf16[32,2048]{1,0:T(8,128)(2,1)S(1)} %slice.29), channel_id=1, source_target_pairs={{0,1},{1,0},{2,3},{3,2},{4,5},{5,4},{6,7},{7,6},{8,9},{9,8},{10,11... | collective-permute-start | bytes 393224 | tf_op jit(solution)/shard_map/ppermute | solution.py:480
  82.3 14.3 %collective-permute-start.15 = (bf16[32,2048]{1,0:T(8,128)(2,1)S(1)}, bf16[32,2048]{1,0:T(8,128)(2,1)S(1)}, u32[]{:S(2)}, u32[]{:S(2)}) collective-permute-start(bf16[32,2048]{1,0:T(8,128)(2,1)S(1)} %get-tuple-element.74), channel_id=1, source_target_pairs={{0,1},{1,0},{2,3},{3,2},{4,5},{5,4},{6,7},{7,6},{8,9},{9,8},{10,11... | collective-permute-start | bytes 393224 | tf_op jit(solution)/shard_map/ppermute | solution.py:480
  82.8 13.8 %collective-permute-start.14 = (bf16[32,2048]{1,0:T(8,128)(2,1)S(1)}, bf16[32,2048]{1,0:T(8,128)(2,1)S(1)}, u32[]{:S(2)}, u32[]{:S(2)}) collective-permute-start(bf16[32,2048]{1,0:T(8,128)(2,1)S(1)} %get-tuple-element.75), channel_id=1, source_target_pairs={{0,32},{1,225},{2,34},{3,227},{4,36},{5,229},{6,38},{7,231},{8,40}... | collective-permute-start | bytes 393224 | tf_op jit(solution)/shard_map/ppermute | solution.py:482
  94.8 21.9 %copy-start.1 = (s32[256]{0:T(256)S(1)}, s32[256]{0:T(256)}, u32[]{:S(2)}) copy-start(s32[256]{0:T(256)} %param.14) | copy-start | bytes 3076
  109.2 35.7 %copy-start.2 = (s32[8]{0:T(128)S(1)}, s32[8]{0:T(128)}, u32[]{:S(2)}) copy-start(s32[8]{0:T(128)} %counts.1) | copy-start | bytes 100
  112.6 44.7 %copy-start = (bf16[16,128,256]{2,1,0:T(8,128)(2,1)S(1)}, bf16[16,128,256]{2,1,0:T(8,128)(2,1)}, u32[]{:S(2)}) copy-start(bf16[16,128,256]{2,1,0:T(8,128)(2,1)} %get-tuple-element.63) | copy-start | bytes 3145732
  112.6 11.3 %all-to-all-start.5 = ((f32[8,16,128]{2,1,0:T(8,128)}), f32[8,16,128]{2,1,0:T(8,128)}, u32[]{:S(2)}, u32[]{:S(2)}) async-start(f32[8,16,128]{2,1,0:T(8,128)} %get-tuple-element.62), calls=%async_computation.5 | async-start | bytes 131072 | tf_op jit(solution)/shard_map/all_to_all | solution.py:341

commit v6 on v5

--- a/solution.py
+++ b/solution.py
@@ -257,7 +257,22 @@
 
 
 def goal_kernel(
-    parts, masked, unit, scale_p, whole, grad, total, out, v_scale, v_whole, v_total, halves, sems
+    here,
+    parts,
+    masked,
+    unit,
+    scale_p,
+    whole,
+    grad,
+    total,
+    keep,
+    give,
+    out,
+    v_scale,
+    v_whole,
+    v_total,
+    halves,
+    sems,
 ):
     slots, width = grad.shape
     step = 512
@@ -289,6 +304,13 @@
     rows = [sums[k : k + 1, c : c + 128] for k in range(3) for c in range(0, slots, 128)]
     tile = jnp.concatenate(rows + [jnp.zeros((8 - len(rows), 128), f32)], axis=0)
     out[:, 2 * width :] = jnp.broadcast_to(tile[None], (slots // 8, 8, 128)).reshape(slots, 128)
+    half = slots // 2
+    keep[...] = out[pl.ds(pl.multiple_of(here[1] * half, half), half), :]
+    give[...] = out[pl.ds(pl.multiple_of((1 - here[1]) * half, half), half), :]
+
+
+def add_kernel(first, second, out):
+    out[...] = first[...] + second[...]
 
 
 def slots_kernel(here, counts, parts, unit_float, out, loss):
@@ -300,7 +322,8 @@
     slot = slot + lax.broadcasted_iota(jnp.int32, (2, 128), 1)
     live = jnp.where(slot < count, 1.0, 0.0)
     loss[...] = live * (jnp.log(sums[0:2, :]) - sums[4:6, :] / sums[2:4, :])
-    at = pl.multiple_of(here[2] * share, share)
+    at = here[1] * (unit_float.shape[0] // 2) + lax.div(here[2], 2) * share
+    at = pl.multiple_of(at, share)
     row = lax.div(at, 128)
     pick = lax.broadcasted_iota(jnp.int32, (share, 128), 1) == (
         lax.rem(at, 128) + lax.broadcasted_iota(jnp.int32, (share, 128), 0)
@@ -326,10 +349,12 @@
 def hidden_kernel(parts, head, hidden):
     count, double, half = parts.shape
     share = double // 2
-    wide = parts[...].astype(f32)
-    halves = [
-        wide[:, k * share : (k + 1) * share, :].reshape(count * share, half) for k in range(2)
-    ]
+    wide = parts[...].astype(f32).reshape(count // 2, 2, double, half)
+    halves = []
+    for k in range(2):
+        rows = [wide[:, c, k * share : (k + 1) * share, :] for c in range(2)]
+        rows = [part.reshape(count // 2 * share, half) for part in rows]
+        halves.append(jnp.concatenate(rows, axis=0))
     neck_grad = jnp.concatenate(halves, axis=1).astype(bf16)
     step = 512
     for c in range(head.shape[0] // step):
@@ -525,13 +550,15 @@
         far(whole_student),
     )
 
-    parts = call(
+    lanes = 2 * width + 128
+    keep, give = call(
         goal_kernel,
-        shaped((slots, 2 * width + 128), f32),
-        [VM] * 3 + [HB] * 4,
-        VM,
+        (shaped((slots // 2, lanes), f32),) * 2,
+        [SM] + [VM] * 3 + [HB] * 4,
+        (VM, VM),
         (4 * slots * local * width, 4 * MIB),
         [
+            pltpu.VMEM((slots, lanes), f32),
             pltpu.VMEM((8, local), f32),
             pltpu.VMEM((rows, local), bf16),
             pltpu.VMEM((slots, 128), f32),
@@ -539,6 +566,7 @@
             dma((4,)),
         ],
     )(
+        here,
         exchange(columns, "tok"),
         held(masked),
         held(unit_float),
@@ -547,7 +575,10 @@
         far(grad),
         far(soft_total),
     )
-    parts = exchange(parts.reshape(protos, share, 2 * width + 128), "proto")
+    parts = call(add_kernel, shaped((slots // 2, lanes), f32), [VM, VM], VM, (0, MIB))(
+        keep, lax.ppermute(give, "proto", swap)
+    )
+    parts = exchange(parts.reshape(chips, share, lanes), "proto", groups)
     finals, row_loss = call(
         slots_kernel,
         (shaped((protos, 2 * share, width // 2), bf16), shaped((slots // 128, 128), f32)),

time: 159 us -> 158 us (level)
  blocking collectives: 77.5 us -> 72.7 us
  starting transfers between devices: 38.3 us -> 40 us
    all_to_all x6, blocking collectives: 77.5 us -> 72.7 us  [exchange(): lax.all_to_all(blocks, axis, 0, 0, tiled=True, axis_index_groups=groups)]
    ppermute x0 -> x1, starting transfers between devices: none -> 1.71 us  [shards(): lax.ppermute(give, 'proto', swap)]
    pallas_call x1 -> x2, Pallas kernels: 3.23 us -> 3.32 us  [the longest x1 3.28 us: shards(): call(goal_kernel, (shaped((slots // 2, lanes), f32),) * 2, [SM] + [VM] *...]
  transfers between devices with their start and end apart: 18 -> 19, of which waited for: 4 -> 5; matrix products, arithmetic and copies ran while one was open for 0% -> 0% of each run, Pallas kernels for 13% -> 13%
where the time goes in v6:
time: 158 us; the launch traced here: 157 us
  blocking collectives  72.7 us (46%)
  starting transfers between devices  40 us (25%)
  Pallas kernels  32.4 us (21%)
  waiting for transfers between devices  10.8 us (7%)
    all_to_all x6, blocking collectives, exchange(): lax.all_to_all(blocks, axis, 0, 0, tiled=True, axis_index_groups=groups)  72.7 us
    ppermute x4, starting transfers between devices, shards(): lax.ppermute(sent if hop < hops - 1 else sent[:rows], ('tok', 'proto'), a...  14.7 us
    all_to_all x2, starting transfers between devices, exchange(): lax.all_to_all(blocks, axis, 0, 0, tiled=True, axis_index_groups=groups)  11.7 us
    ppermute x4, waiting for transfers between devices, shards(): lax.ppermute(sent if hop < hops - 1 else sent[:rows], ('tok', 'proto'), a...  6.64 us
    pallas_call x1, Pallas kernels, shards(): call(student_kernel, (pltpu.VMEM((slots, local), f32), pltpu.HBM((8, loca...  5.41 us
    ppermute x3, starting transfers between devices, onward(): late.append(lax.ppermute(sent, ('tok', 'proto'), along))  3.94 us
    pallas_call x2, Pallas kernels, shards(): sums = row_call(exchange(columns, 'tok'), held(scores))  3.6 us
    pallas_call x1, Pallas kernels, shards(): call(stage_kernel, pltpu.VMEM(hidden.shape, bf16), [HB], VM, (0, 16 * MIB...  3.5 us
  transfers between devices with their start and end apart: 19, of which 5 were waited for; matrix products, arithmetic and copies ran while one was open for 0% of the time, Pallas kernels for 13%

profile of v6, /device:TPU:1, one launch (start us, length us, event | category | flops | bytes accessed | tf_op | source)
XLA Modules:
  0.0 157.0 jit_solution(4808412846822935796)
XLA Ops:
  0.6 2.0 %shard_map.95 = (bf16[16,64,512]{2,1,0:T(8,128)(2,1)}, bf16[64,2048]{1,0:T(8,128)(2,1)S(1)}) custom-call(bf16[64,256]{1,0:T(8,128)(2,1)} %teacher.1, bf16[64,256]{1,0:T(8,128)(2,1)} %student.1, bf16[32,2048]{1,0:T(8,128)(2,1)} %first.1, bf16[32,2048]{1,0:T(8,128)(2,1)} %second.1), custom_call_target="tpu_custom_call" | custom-call | bytes 1048576 | tf_op jit(solution)/shard_map/pallas_call | solution.py:399
  2.6 7.6 %all-to-all-start = ((bf16[16,64,512]{2,1,0:T(8,128)(2,1)}), bf16[16,64,512]{2,1,0:T(8,128)(2,1)S(1)}, u32[]{:S(2)}, u32[]{:S(2)}) async-start(bf16[16,64,512]{2,1,0:T(8,128)(2,1)} %get-tuple-element.40), calls=%async_computation | async-start | bytes 2097152 | tf_op jit(solution)/shard_map/all_to_all | solution.py:366
  10.3 1.0 collective-permute-start
  11.3 1.2 collective-permute-done.other
  12.5 5.7 %collective-permute-start.1 = (bf16[64,2048]{1,0:T(8,128)(2,1)S(1)}, bf16[64,2048]{1,0:T(8,128)(2,1)S(1)}, u32[]{:S(2)}, u32[]{:S(2)}) collective-permute-start(bf16[64,2048]{1,0:T(8,128)(2,1)S(1)} %get-tuple-element.42), channel_id=1, source_target_pairs={{0,32},{1,225},{2,34},{3,227},{4,36},{5,229},{6,38},{7,231},{8,40}... | collective-permute-start | bytes 786440 | tf_op jit(solution)/shard_map/ppermute | solution.py:422
  18.1 3.3 %collective-permute-done.1.refs_0_ = bf16[64,2048]{1,0:T(8,128)(2,1)S(1)} collective-permute-done((bf16[64,2048]{1,0:T(8,128)(2,1)S(1)}, bf16[64,2048]{1,0:T(8,128)(2,1)S(1)}, u32[]{:S(2)}, u32[]{:S(2)}) %collective-permute-start.1) | collective-permute-done | bytes 262176 | tf_op jit(solution)/shard_map/ppermute | solution.py:422
  21.5 3.4 %collective-permute-start.2 = (bf16[64,2048]{1,0:T(8,128)(2,1)S(1)}, bf16[64,2048]{1,0:T(8,128)(2,1)S(1)}, u32[]{:S(2)}, u32[]{:S(2)}) collective-permute-start(bf16[64,2048]{1,0:T(8,128)(2,1)S(1)} %collective-permute-done.1.refs_0_), channel_id=1, source_target_pairs={{0,32},{1,225},{2,34},{3,227},{4,36},{5,229},{6,38},{7,231},{8,40}... | collective-permute-start | bytes 786440 | tf_op jit(solution)/shard_map/ppermute | solution.py:422
  24.9 3.3 %collective-permute-done.2.refs_1_ = bf16[64,2048]{1,0:T(8,128)(2,1)S(1)} collective-permute-done((bf16[64,2048]{1,0:T(8,128)(2,1)S(1)}, bf16[64,2048]{1,0:T(8,128)(2,1)S(1)}, u32[]{:S(2)}, u32[]{:S(2)}) %collective-permute-start.2) | collective-permute-done | bytes 262176 | tf_op jit(solution)/shard_map/ppermute | solution.py:422
  28.2 0.0 all-to-all-done.mine
  28.2 2.5 %collective-permute-start.3 = (bf16[16,64,512]{2,1,0:T(8,128)(2,1)S(1)}, bf16[16,64,512]{2,1,0:T(8,128)(2,1)S(1)}, u32[]{:S(2)}, u32[]{:S(2)}) collective-permute-start(bf16[16,64,512]{2,1,0:T(8,128)(2,1)S(1)} %all-to-all-done.mine), channel_id=1, source_target_pairs={{0,1},{1,0},{2,3},{3,2},{4,5},{5,4},{6,7},{7,6},{8,9},{9,8},{10,11... | collective-permute-start | bytes 3145736 | tf_op jit(solution)/shard_map/ppermute | solution.py:427
  30.7 3.7 %collective-permute-start.4 = (bf16[64,2048]{1,0:T(8,128)(2,1)S(1)}, bf16[64,2048]{1,0:T(8,128)(2,1)S(1)}, u32[]{:S(2)}, u32[]{:S(2)}) collective-permute-start(bf16[64,2048]{1,0:T(8,128)(2,1)S(1)} %collective-permute-done.2.refs_1_), channel_id=1, source_target_pairs={{0,32},{1,225},{2,34},{3,227},{4,36},{5,229},{6,38},{7,231},{8,40}... | collective-permute-start | bytes 786440 | tf_op jit(solution)/shard_map/ppermute | solution.py:422
  34.5 0.1 pad_add_fusion.here
  34.6 0.1 collective-permute-start.6
  34.7 0.6 collective-permute-start.7
  35.3 3.5 %shard_map.97.hidden = bf16[2048,2048]{1,0:T(8,128)(2,1)S(1)} custom-call(bf16[2048,2048]{1,0:T(8,128)(2,1)} %hidden.1), custom_call_target="tpu_custom_call" | custom-call | bytes 16777216 | tf_op jit(solution)/shard_map/pallas_call | solution.py:431
  38.8 0.0 collective-permute-done.4.refs_2_
  38.8 0.4 collective-permute-start.8
  39.2 1.9 %collective-permute-start.5 = (bf16[32,2048]{1,0:T(8,128)(2,1)S(1)}, bf16[32,2048]{1,0:T(8,128)(2,1)S(1)}, u32[]{:S(2)}, u32[]{:S(2)}) collective-permute-start(bf16[32,2048]{1,0:T(8,128)(2,1)S(1)} %get-tuple-element.81), channel_id=1, source_target_pairs={{0,32},{1,225},{2,34},{3,227},{4,36},{5,229},{6,38},{7,231},{8,40}... | collective-permute-start | bytes 393224 | tf_op jit(solution)/shard_map/ppermute | solution.py:422
  41.1 0.0 collective-permute-done.3.other
  41.1 0.6 collective-permute-start.9
  41.7 3.1 %shard_map.98 = (bf16[2048,256]{1,0:T(8,128)(2,1)S(1)}, bf16[16,128,256]{2,1,0:T(8,128)(2,1)}) custom-call(s32[3]{0:T(128)S(1)} %pad_add_fusion.here, bf16[2048,2048]{1,0:T(8,128)(2,1)S(1)} %shard_map.97.hidden, bf16[16,64,512]{2,1,0:T(8,128)(2,1)S(1)} %all-to-all-done.mine, bf16[16,64,512]{2,1,0:T(8,128)(2,1)S(1)} %collective-permute-done.3.other), custom_call_target="tpu_custom_call" | custom-call | flops 2147483648 | bytes 10485760 | tf_op jit(solution)/shard_map/pallas_call | solution.py:439
  44.8 0.0 collective-permute-done.6.refs_4_
  44.8 0.0 collective-permute-done.7.refs_5_
  44.8 0.0 collective-permute-done.8.refs_6_
  44.8 0.0 collective-permute-done.5.refs_3_
  44.8 3.2 %shard_map.99 = (bf16[2048,2048]{1,0:T(8,128)(2,1)S(1)}, bf16[256,2048]{1,0:T(8,128)(2,1)}, bf16[2048,256]{1,0:T(8,128)(2,1)}, f32[8,16,128]{2,1,0:T(8,128)S(1)}) custom-call(s32[3]{0:T(128)S(1)} %pad_add_fusion.here, bf16[2048,256]{1,0:T(8,128)(2,1)S(1)} %get-tuple-element.45.unit, bf16[64,2048]{1,0:T(8,128)(2,1)S(1)} %get-tuple-element.41.mine.own, ...), custom_call_target="tpu_custom_call" | custom-call | flops 2147483648 | bytes 12582912 | tf_op jit(solution)/shard_map/pallas_call | solution.py:453
  48.0 0.0 collective-permute-done.9.refs_0_
  48.1 1.4 collective-permute-start.10
  49.5 0.1 collective-permute-start.11
  49.6 12.4 %all_to_all.40.parts = f32[8,16,128]{2,1,0:T(8,128)S(1)} all-to-all(f32[8,16,128]{2,1,0:T(8,128)S(1)} %get-tuple-element.49), channel_id=1, replica_groups=mesh['tok'=8,'proto'=32] {'tok'}, dimensions={0} | all-to-all | bytes 131072 | tf_op jit(solution)/shard_map/all_to_all | solution.py:366
  62.0 1.8 %shard_map.100 = bf16[32,16,128]{2,1,0:T(8,128)(2,1)S(1)} custom-call(f32[8,16,128]{2,1,0:T(8,128)S(1)} %all_to_all.40.parts, bf16[2048,2048]{1,0:T(8,128)(2,1)S(1)} %get-tuple-element.50.scores), custom_call_target="tpu_custom_call" | custom-call | flops 8388608 | bytes 8388608 | tf_op jit(solution)/shard_map/pallas_call | solution.py:511
  63.8 0.0 collective-permute-done.11.refs_4_
  63.8 0.0 collective-permute-done.10.refs_1_
  63.8 0.1 collective-permute-start.12
  63.9 2.1 %collective-permute-start.13 = (bf16[32,2048]{1,0:T(8,128)(2,1)S(1)}, bf16[32,2048]{1,0:T(8,128)(2,1)S(1)}, u32[]{:S(2)}, u32[]{:S(2)}) collective-permute-start(bf16[32,2048]{1,0:T(8,128)(2,1)S(1)} %slice.29), channel_id=1, source_target_pairs={{0,1},{1,0},{2,3},{3,2},{4,5},{5,4},{6,7},{7,6},{8,9},{9,8},{10,11... | collective-permute-start | bytes 393224 | tf_op jit(solution)/shard_map/ppermute | solution.py:505
  66.1 14.0 %all_to_all.41.parts = bf16[32,16,128]{2,1,0:T(8,128)(2,1)S(1)} all-to-all(bf16[32,16,128]{2,1,0:T(8,128)(2,1)S(1)} %shard_map.100), channel_id=1, replica_groups=mesh['tok'=8,'proto'=32] {'proto'}, dimensions={0} | all-to-all | bytes 262144 | tf_op jit(solution)/shard_map/all_to_all | solution.py:366
  80.1 2.2 %shard_map.101 = f32[8,16,128]{2,1,0:T(8,128)S(1)} custom-call(bf16[32,16,128]{2,1,0:T(8,128)(2,1)S(1)} %all_to_all.41.parts, bf16[2048,2048]{1,0:T(8,128)(2,1)S(1)} %get-tuple-element.50.scores), custom_call_target="tpu_custom_call" | custom-call | flops 8388608 | bytes 8388608 | tf_op jit(solution)/shard_map/pallas_call | solution.py:513
  82.3 0.0 collective-permute-done.13.refs_5_
  82.3 0.0 collective-permute-done.12.refs_2_
  82.3 0.5 collective-permute-start.15
  82.8 2.4 %collective-permute-start.14 = (bf16[32,2048]{1,0:T(8,128)(2,1)S(1)}, bf16[32,2048]{1,0:T(8,128)(2,1)S(1)}, u32[]{:S(2)}, u32[]{:S(2)}) collective-permute-start(bf16[32,2048]{1,0:T(8,128)(2,1)S(1)} %get-tuple-element.79), channel_id=1, source_target_pairs={{0,32},{1,225},{2,34},{3,227},{4,36},{5,229},{6,38},{7,231},{8,40}... | collective-permute-start | bytes 393224 | tf_op jit(solution)/shard_map/ppermute | solution.py:507
  85.2 9.6 %all_to_all.42.parts = f32[8,16,128]{2,1,0:T(8,128)S(1)} all-to-all(f32[8,16,128]{2,1,0:T(8,128)S(1)} %shard_map.101), channel_id=1, replica_groups=mesh['tok'=8,'proto'=32] {'tok'}, dimensions={0} | all-to-all | bytes 131072 | tf_op jit(solution)/shard_map/all_to_all | solution.py:366
  94.8 0.0 copy-start.1
  94.8 1.8 %shard_map.102 = bf16[32,16,128]{2,1,0:T(8,128)(2,1)S(1)} custom-call(f32[8,16,128]{2,1,0:T(8,128)S(1)} %all_to_all.42.parts, bf16[2048,2048]{1,0:T(8,128)(2,1)S(1)} %get-tuple-element.50.scores), custom_call_target="tpu_custom_call" | custom-call | flops 8388608 | bytes 8388608 | tf_op jit(solution)/shard_map/pallas_call | solution.py:515
  96.6 0.0 collective-permute-done.15.refs_6_
  96.6 0.0 collective-permute-done.14.refs_3_
  96.6 12.6 %all_to_all.43.parts = bf16[32,16,128]{2,1,0:T(8,128)(2,1)S(1)} all-to-all(bf16[32,16,128]{2,1,0:T(8,128)(2,1)S(1)} %shard_map.102), channel_id=1, replica_groups=mesh['tok'=8,'proto'=32] {'proto'}, dimensions={0} | all-to-all | bytes 262144 | tf_op jit(solution)/shard_map/all_to_all | solution.py:366
  109.2 0.0 copy-start.2
  109.2 3.4 %shard_map.103 = (f32[8,16,128]{2,1,0:T(8,128)}, bf16[256,2048]{1,0:T(8,128)(2,1)}) custom-call(s32[3]{0:T(128)S(1)} %pad_add_fusion.here, bf16[32,16,128]{2,1,0:T(8,128)(2,1)S(1)} %all_to_all.43.parts, bf16[2048,2048]{1,0:T(8,128)(2,1)S(1)} %get-tuple-element.50.scores, bf16[64,2048]{1,0:T(8,128)(2,1)S(1)} %get-tuple-element.41.mine.own, ...), custom_call_target="tpu_custom_call" | custom-call | flops 8388608 | bytes 8388608 | tf_op jit(solution)/shard_map/pallas_call | solution.py:517
  112.6 0.0 copy-start
  112.6 4.1 %all-to-all-start.5 = ((f32[8,16,128]{2,1,0:T(8,128)}), f32[8,16,128]{2,1,0:T(8,128)}, u32[]{:S(2)}, u32[]{:S(2)}) async-start(f32[8,16,128]{2,1,0:T(8,128)} %get-tuple-element.64), calls=%async_computation.5 | async-start | bytes 131072 | tf_op jit(solution)/shard_map/all_to_all | solution.py:366
  116.7 0.0 copy-done.1
  116.7 5.4 %shard_map.104 = (f32[256,2048]{1,0:T(8,128)S(1)}, f32[8,2048]{1,0:T(8,128)}, f32[256,384]{1,0:T(8,128)S(1)}, f32[256,256]{1,0:T(8,128)}, f32[256,128]{1,0:T(8,128)}) custom-call(s32[1,256]{1,0:T(1,128)S(1)} %bitcast.10, bf16[256,2048]{1,0:T(8,128)(2,1)} %hidden.2, bf16[2048,256]{1,0:T(8,128)(2,1)} %bitcast.7, bf16[2048,256]{1,0:T(8,128)(2,1)} %get-tuple-element.66.unit, ...), custom_call_target="tpu_custom_call" | custom-call | flops 1342177280 | bytes 8388608 | tf_op jit(solution)/shard_map/pallas_call | solution.py:523
  122.2 1.7 %all-to-all-done.5.parts = f32[8,16,128]{2,1,0:T(8,128)} async-done(((f32[8,16,128]{2,1,0:T(8,128)}), f32[8,16,128]{2,1,0:T(8,128)}, u32[]{:S(2)}, u32[]{:S(2)}) %all-to-all-start.5) | async-done | bytes 65568 | tf_op jit(solution)/shard_map/all_to_all | solution.py:366
  123.9 3.3 %shard_map.105 = (f32[128,640]{1,0:T(8,128)S(1)}, f32[128,640]{1,0:T(8,128)S(1)}) custom-call(s32[3]{0:T(128)S(1)} %pad_add_fusion.here, f32[8,16,128]{2,1,0:T(8,128)} %all-to-all-done.5.parts, f32[256,2048]{1,0:T(8,128)S(1)} %get-tuple-element.69.masked, f32[256,384]{1,0:T(8,128)S(1)} %get-tuple-element.70.unit.unit_float, ...), custom_call_target="tpu_custom_call" | custom-call | flops 536870912 | bytes 4194304 | tf_op jit(solution)/shard_map/pallas_call | solution.py:554
  127.2 1.7 %collective-permute-start.16 = (f32[128,640]{1,0:T(8,128)S(1)}, f32[128,640]{1,0:T(8,128)S(1)}, u32[]{:S(2)}, u32[]{:S(2)}) collective-permute-start(f32[128,640]{1,0:T(8,128)S(1)} %get-tuple-element.75), channel_id=1, source_target_pairs={{0,1},{1,0},{2,3},{3,2},{4,5},{5,4},{6,7},{7,6},{8,9},{9,8},{10,11... | collective-permute-start | bytes 983048 | tf_op jit(solution)/shard_map/ppermute | solution.py:579
  128.9 1.3 collective-permute-done.16.second
  130.2 10.8 %all_to_all.44.parts = f32[16,8,640]{2,1,0:T(8,128)S(1)} all-to-all(f32[16,8,640]{2,1,0:T(8,128)S(1)} %bitcast.9), channel_id=1, replica_groups={{0,2,4,6,8,10,12,14,16,18,20,22,24,26,28,30},{1,3,5,7,9,11,13,15,17,19,..., dimensions={0} | all-to-all | bytes 655360 | tf_op jit(solution)/shard_map/all_to_all | solution.py:366
  141.0 0.0 copy-done.2
  141.0 1.2 shard_map.107
  142.2 13.4 %all_to_all.45.parts = bf16[32,16,128]{2,1,0:T(8,128)(2,1)S(1)} all-to-all(bf16[32,16,128]{2,1,0:T(8,128)(2,1)S(1)} %get-tuple-element.77), channel_id=1, replica_groups=mesh['tok'=8,'proto'=32] {'proto'}, dimensions={0} | all-to-all | bytes 262144 | tf_op jit(solution)/shard_map/all_to_all | solution.py:366
  155.6 0.0 copy-done
  155.6 1.4 shard_map.108
  (8 shorter events, 0.1 us)
Async XLA Ops:
  2.6 25.5 %all-to-all-start = ((bf16[16,64,512]{2,1,0:T(8,128)(2,1)}), bf16[16,64,512]{2,1,0:T(8,128)(2,1)S(1)}, u32[]{:S(2)}, u32[]{:S(2)}) async-start(bf16[16,64,512]{2,1,0:T(8,128)(2,1)} %get-tuple-element.40), calls=%async_computation | async-start | bytes 2097152 | tf_op jit(solution)/shard_map/all_to_all | solution.py:366
  10.3 2.2 %collective-permute-start = (bf16[64,2048]{1,0:T(8,128)(2,1)S(1)}, bf16[64,2048]{1,0:T(8,128)(2,1)S(1)}, u32[]{:S(2)}, u32[]{:S(2)}) collective-permute-start(bf16[64,2048]{1,0:T(8,128)(2,1)S(1)} %get-tuple-element.41.mine.own), channel_id=1, source_target_pairs={{0,1},{1,0},{2,3},{3,2},{4,5},{5,4},{6,7},{7,6},{8,9},{9,8},{10,11... | collective-permute-start | bytes 786440 | tf_op jit(solution)/shard_map/ppermute | solution.py:408
  12.5 9.0 %collective-permute-start.1 = (bf16[64,2048]{1,0:T(8,128)(2,1)S(1)}, bf16[64,2048]{1,0:T(8,128)(2,1)S(1)}, u32[]{:S(2)}, u32[]{:S(2)}) collective-permute-start(bf16[64,2048]{1,0:T(8,128)(2,1)S(1)} %get-tuple-element.42), channel_id=1, source_target_pairs={{0,32},{1,225},{2,34},{3,227},{4,36},{5,229},{6,38},{7,231},{8,40}... | collective-permute-start | bytes 786440 | tf_op jit(solution)/shard_map/ppermute | solution.py:422
  21.5 6.7 %collective-permute-start.2 = (bf16[64,2048]{1,0:T(8,128)(2,1)S(1)}, bf16[64,2048]{1,0:T(8,128)(2,1)S(1)}, u32[]{:S(2)}, u32[]{:S(2)}) collective-permute-start(bf16[64,2048]{1,0:T(8,128)(2,1)S(1)} %collective-permute-done.1.refs_0_), channel_id=1, source_target_pairs={{0,32},{1,225},{2,34},{3,227},{4,36},{5,229},{6,38},{7,231},{8,40}... | collective-permute-start | bytes 786440 | tf_op jit(solution)/shard_map/ppermute | solution.py:422
  28.2 12.9 %collective-permute-start.3 = (bf16[16,64,512]{2,1,0:T(8,128)(2,1)S(1)}, bf16[16,64,512]{2,1,0:T(8,128)(2,1)S(1)}, u32[]{:S(2)}, u32[]{:S(2)}) collective-permute-start(bf16[16,64,512]{2,1,0:T(8,128)(2,1)S(1)} %all-to-all-done.mine), channel_id=1, source_target_pairs={{0,1},{1,0},{2,3},{3,2},{4,5},{5,4},{6,7},{7,6},{8,9},{9,8},{10,11... | collective-permute-start | bytes 3145736 | tf_op jit(solution)/shard_map/ppermute | solution.py:427
  30.7 8.0 %collective-permute-start.4 = (bf16[64,2048]{1,0:T(8,128)(2,1)S(1)}, bf16[64,2048]{1,0:T(8,128)(2,1)S(1)}, u32[]{:S(2)}, u32[]{:S(2)}) collective-permute-start(bf16[64,2048]{1,0:T(8,128)(2,1)S(1)} %collective-permute-done.2.refs_1_), channel_id=1, source_target_pairs={{0,32},{1,225},{2,34},{3,227},{4,36},{5,229},{6,38},{7,231},{8,40}... | collective-permute-start | bytes 786440 | tf_op jit(solution)/shard_map/ppermute | solution.py:422
  34.6 10.2 %collective-permute-start.6 = (bf16[32,2048]{1,0:T(8,128)(2,1)S(1)}, bf16[32,2048]{1,0:T(8,128)(2,1)S(1)}, u32[]{:S(2)}, u32[]{:S(2)}) collective-permute-start(bf16[32,2048]{1,0:T(8,128)(2,1)S(1)} %slice.33), channel_id=1, source_target_pairs={{0,1},{1,0},{2,3},{3,2},{4,5},{5,4},{6,7},{7,6},{8,9},{9,8},{10,11... | collective-permute-start | bytes 393224 | tf_op jit(solution)/shard_map/ppermute | solution.py:424
  34.7 10.1 %collective-permute-start.7 = (bf16[32,2048]{1,0:T(8,128)(2,1)S(1)}, bf16[32,2048]{1,0:T(8,128)(2,1)S(1)}, u32[]{:S(2)}, u32[]{:S(2)}) collective-permute-start(bf16[32,2048]{1,0:T(8,128)(2,1)S(1)} %slice.34), channel_id=1, source_target_pairs={{0,1},{1,0},{2,3},{3,2},{4,5},{5,4},{6,7},{7,6},{8,9},{9,8},{10,11... | collective-permute-start | bytes 393224 | tf_op jit(solution)/shard_map/ppermute | solution.py:424
  38.8 6.0 %collective-permute-start.8 = (bf16[32,2048]{1,0:T(8,128)(2,1)S(1)}, bf16[32,2048]{1,0:T(8,128)(2,1)S(1)}, u32[]{:S(2)}, u32[]{:S(2)}) collective-permute-start(bf16[32,2048]{1,0:T(8,128)(2,1)S(1)} %get-tuple-element.80), channel_id=1, source_target_pairs={{0,1},{1,0},{2,3},{3,2},{4,5},{5,4},{6,7},{7,6},{8,9},{9,8},{10,11... | collective-permute-start | bytes 393224 | tf_op jit(solution)/shard_map/ppermute | solution.py:424
  39.2 5.6 %collective-permute-start.5 = (bf16[32,2048]{1,0:T(8,128)(2,1)S(1)}, bf16[32,2048]{1,0:T(8,128)(2,1)S(1)}, u32[]{:S(2)}, u32[]{:S(2)}) collective-permute-start(bf16[32,2048]{1,0:T(8,128)(2,1)S(1)} %get-tuple-element.81), channel_id=1, source_target_pairs={{0,32},{1,225},{2,34},{3,227},{4,36},{5,229},{6,38},{7,231},{8,40}... | collective-permute-start | bytes 393224 | tf_op jit(solution)/shard_map/ppermute | solution.py:422
  41.1 6.9 %collective-permute-start.9 = (bf16[64,2048]{1,0:T(8,128)(2,1)S(1)}, bf16[64,2048]{1,0:T(8,128)(2,1)S(1)}, u32[]{:S(2)}, u32[]{:S(2)}) collective-permute-start(bf16[64,2048]{1,0:T(8,128)(2,1)S(1)} %get-tuple-element.48), channel_id=1, source_target_pairs={{0,32},{1,225},{2,34},{3,227},{4,36},{5,229},{6,38},{7,231},{8,40}... | collective-permute-start | bytes 786440 | tf_op jit(solution)/shard_map/ppermute | solution.py:430
  48.1 15.7 %collective-permute-start.10 = (bf16[64,2048]{1,0:T(8,128)(2,1)S(1)}, bf16[64,2048]{1,0:T(8,128)(2,1)S(1)}, u32[]{:S(2)}, u32[]{:S(2)}) collective-permute-start(bf16[64,2048]{1,0:T(8,128)(2,1)S(1)} %collective-permute-done.9.refs_0_), channel_id=1, source_target_pairs={{0,32},{1,225},{2,34},{3,227},{4,36},{5,229},{6,38},{7,231},{8,40}... | collective-permute-start | bytes 786440 | tf_op jit(solution)/shard_map/ppermute | solution.py:507
  49.5 14.3 %collective-permute-start.11 = (bf16[32,2048]{1,0:T(8,128)(2,1)S(1)}, bf16[32,2048]{1,0:T(8,128)(2,1)S(1)}, u32[]{:S(2)}, u32[]{:S(2)}) collective-permute-start(bf16[32,2048]{1,0:T(8,128)(2,1)S(1)} %slice.28), channel_id=1, source_target_pairs={{0,1},{1,0},{2,3},{3,2},{4,5},{5,4},{6,7},{7,6},{8,9},{9,8},{10,11... | collective-permute-start | bytes 393224 | tf_op jit(solution)/shard_map/ppermute | solution.py:505
  63.8 18.5 %collective-permute-start.12 = (bf16[64,2048]{1,0:T(8,128)(2,1)S(1)}, bf16[64,2048]{1,0:T(8,128)(2,1)S(1)}, u32[]{:S(2)}, u32[]{:S(2)}) collective-permute-start(bf16[64,2048]{1,0:T(8,128)(2,1)S(1)} %collective-permute-done.10.refs_1_), channel_id=1, source_target_pairs={{0,32},{1,225},{2,34},{3,227},{4,36},{5,229},{6,38},{7,231},{8,40}... | collective-permute-start | bytes 786440 | tf_op jit(solution)/shard_map/ppermute | solution.py:507
  63.9 18.4 %collective-permute-start.13 = (bf16[32,2048]{1,0:T(8,128)(2,1)S(1)}, bf16[32,2048]{1,0:T(8,128)(2,1)S(1)}, u32[]{:S(2)}, u32[]{:S(2)}) collective-permute-start(bf16[32,2048]{1,0:T(8,128)(2,1)S(1)} %slice.29), channel_id=1, source_target_pairs={{0,1},{1,0},{2,3},{3,2},{4,5},{5,4},{6,7},{7,6},{8,9},{9,8},{10,11... | collective-permute-start | bytes 393224 | tf_op jit(solution)/shard_map/ppermute | solution.py:505
  82.3 14.3 %collective-permute-start.15 = (bf16[32,2048]{1,0:T(8,128)(2,1)S(1)}, bf16[32,2048]{1,0:T(8,128)(2,1)S(1)}, u32[]{:S(2)}, u32[]{:S(2)}) collective-permute-start(bf16[32,2048]{1,0:T(8,128)(2,1)S(1)} %get-tuple-element.78), channel_id=1, source_target_pairs={{0,1},{1,0},{2,3},{3,2},{4,5},{5,4},{6,7},{7,6},{8,9},{9,8},{10,11... | collective-permute-start | bytes 393224 | tf_op jit(solution)/shard_map/ppermute | solution.py:505
  82.8 13.8 %collective-permute-start.14 = (bf16[32,2048]{1,0:T(8,128)(2,1)S(1)}, bf16[32,2048]{1,0:T(8,128)(2,1)S(1)}, u32[]{:S(2)}, u32[]{:S(2)}) collective-permute-start(bf16[32,2048]{1,0:T(8,128)(2,1)S(1)} %get-tuple-element.79), channel_id=1, source_target_pairs={{0,32},{1,225},{2,34},{3,227},{4,36},{5,229},{6,38},{7,231},{8,40}... | collective-permute-start | bytes 393224 | tf_op jit(solution)/shard_map/ppermute | solution.py:507
  94.8 21.9 %copy-start.1 = (s32[256]{0:T(256)S(1)}, s32[256]{0:T(256)}, u32[]{:S(2)}) copy-start(s32[256]{0:T(256)} %param.14) | copy-start | bytes 3076
  109.2 31.8 %copy-start.2 = (s32[8]{0:T(128)S(1)}, s32[8]{0:T(128)}, u32[]{:S(2)}) copy-start(s32[8]{0:T(128)} %counts.1) | copy-start | bytes 100
  112.6 43.0 %copy-start = (bf16[16,128,256]{2,1,0:T(8,128)(2,1)S(1)}, bf16[16,128,256]{2,1,0:T(8,128)(2,1)}, u32[]{:S(2)}) copy-start(bf16[16,128,256]{2,1,0:T(8,128)(2,1)} %get-tuple-element.65) | copy-start | bytes 3145732
  112.6 11.3 %all-to-all-start.5 = ((f32[8,16,128]{2,1,0:T(8,128)}), f32[8,16,128]{2,1,0:T(8,128)}, u32[]{:S(2)}, u32[]{:S(2)}) async-start(f32[8,16,128]{2,1,0:T(8,128)} %get-tuple-element.64), calls=%async_computation.5 | async-start | bytes 131072 | tf_op jit(solution)/shard_map/all_to_all | solution.py:366
  127.2 3.0 %collective-permute-start.16 = (f32[128,640]{1,0:T(8,128)S(1)}, f32[128,640]{1,0:T(8,128)S(1)}, u32[]{:S(2)}, u32[]{:S(2)}) collective-permute-start(f32[128,640]{1,0:T(8,128)S(1)} %get-tuple-element.75), channel_id=1, source_target_pairs={{0,1},{1,0},{2,3},{3,2},{4,5},{5,4},{6,7},{7,6},{8,9},{9,8},{10,11... | collective-permute-start | bytes 983048 | tf_op jit(solution)/shard_map/ppermute | solution.py:579

commit v7 on v6

--- a/solution.py
+++ b/solution.py
@@ -67,15 +67,14 @@
         copy.wait()
 
 
-def heads_kernel(teacher, student, first, second, copies, both, v_teacher, v_student, sems):
+def heads_kernel(teacher, student, first, second, copies, both, v_heads, sems):
     rows, width = first.shape[0], teacher.shape[1]
-    heads = fetch([(teacher, v_teacher), (student, v_student)], sems)
+    heads = fetch([(teacher, v_heads.at[:, :width]), (student, v_heads.at[:, width:])], sems)
     rest = fetch(
         [(first, both.at[pl.ds(0, rows), :]), (second, both.at[pl.ds(rows, rows), :])], sems, 2
     )
     settle(heads)
-    copies[:, :, :width] = jnp.broadcast_to(v_teacher[...][None], copies.shape[:2] + (width,))
-    copies[:, :, width:] = jnp.broadcast_to(v_student[...][None], copies.shape[:2] + (width,))
+    rest += fetch([(v_heads, copies.at[k]) for k in range(copies.shape[0])], sems, 4)
     settle(rest)
 
 
@@ -226,6 +225,9 @@
         sems,
     )
     slots, tokens = v_hidden.shape[0], v_unit.shape[0]
+    wanted = jnp.broadcast_to(index[...].astype(f32), (128, slots)).T[:, 0:1]
+    chosen = wanted == lax.broadcasted_iota(jnp.int32, (slots, tokens), 1).astype(f32)
+    chosen = chosen.astype(f32).astype(bf16)
     settle(copies[:2])
     neck = dot(v_hidden[...], v_head[...])
     scale = lax.rsqrt(jnp.sum(neck * neck, axis=1, keepdims=True) + norm_eps)
@@ -234,10 +236,9 @@
     unit_out[:, :width] = unit_float
     unit_out[:, width:] = jnp.broadcast_to(scale, (unit_float.shape[0], 128))
     student = unit_float.astype(bf16)
-    settle(copies[2:])
-    wanted = jnp.broadcast_to(index[...].astype(f32), (128, slots)).T[:, 0:1]
-    chosen = wanted == lax.broadcasted_iota(jnp.int32, (slots, tokens), 1).astype(f32)
-    picked = dot(chosen.astype(f32).astype(bf16), v_unit[...]).astype(bf16)
+    settle(copies[2:3])
+    picked = dot(chosen, v_unit[...]).astype(bf16)
+    settle(copies[3:])
     fold = LOG2E / teacher_temp
     step = 256
     total_acc = jnp.zeros((slots, 1), f32)
@@ -398,11 +399,11 @@
     groups = [[2 * k + c for k in range(chips)] for c in range(2)]
     copies, both = call(
         heads_kernel,
-        (shaped((chips, depth // protos, 2 * width), bf16), shaped((2 * rows, local), bf16)),
+        (pltpu.HBM((chips, depth // protos, 2 * width), bf16), shaped((2 * rows, local), bf16)),
         [HB] * 4,
-        (VM, VM),
+        (HB, VM),
         (0, MIB),
-        [pltpu.VMEM((depth // protos, width), bf16)] * 2 + [dma((4,))],
+        [pltpu.VMEM((depth // protos, 2 * width), bf16), dma((4 + chips,))],
     )(far(head_teacher), far(head_student), far(proto_teacher), far(proto_student))
     mine = exchange(copies, "proto", groups)
     sibling = lax.ppermute(both, "proto", swap)

time: 158 us -> 157 us (level)
  no operation moved by 1% of the time
where the time goes in v7:
time: 157 us
  blocking collectives  72.7 us (46%)
  starting transfers between devices  40 us (25%)
  Pallas kernels  32.1 us (20%)
  waiting for transfers between devices  11 us (7%)
    all_to_all x6, blocking collectives, exchange(): lax.all_to_all(blocks, axis, 0, 0, tiled=True, axis_index_groups=groups)  72.7 us
    ppermute x4, starting transfers between devices, shards(): lax.ppermute(sent if hop < hops - 1 else sent[:rows], ('tok', 'proto'), a...  14.7 us
    all_to_all x2, starting transfers between devices, exchange(): lax.all_to_all(blocks, axis, 0, 0, tiled=True, axis_index_groups=groups)  11.7 us
    ppermute x4, waiting for transfers between devices, shards(): lax.ppermute(sent if hop < hops - 1 else sent[:rows], ('tok', 'proto'), a...  6.64 us
    pallas_call x1, Pallas kernels, shards(): call(student_kernel, (pltpu.VMEM((slots, local), f32), pltpu.HBM((8, loca...  5.21 us
    ppermute x3, starting transfers between devices, onward(): late.append(lax.ppermute(sent, ('tok', 'proto'), along))  3.94 us
    pallas_call x2, Pallas kernels, shards(): sums = row_call(exchange(columns, 'tok'), held(scores))  3.6 us
    pallas_call x1, Pallas kernels, shards(): call(stage_kernel, pltpu.VMEM(hidden.shape, bf16), [HB], VM, (0, 16 * MIB...  3.5 us
  transfers between devices with their start and end apart: 19, of which 5 were waited for; matrix products, arithmetic and copies ran while one was open for 0% of the time, Pallas kernels for 13%

profile of v7, /device:TPU:1, one launch (start us, length us, event | category | flops | bytes accessed | tf_op | source)
XLA Modules:
  0.0 156.9 jit_solution(17921642927141111224)
XLA Ops:
  0.6 1.9 %shard_map.95 = (bf16[16,64,512]{2,1,0:T(8,128)(2,1)}, bf16[64,2048]{1,0:T(8,128)(2,1)S(1)}) custom-call(bf16[64,256]{1,0:T(8,128)(2,1)} %teacher.1, bf16[64,256]{1,0:T(8,128)(2,1)} %student.1, bf16[32,2048]{1,0:T(8,128)(2,1)} %first.1, bf16[32,2048]{1,0:T(8,128)(2,1)} %second.1), custom_call_target="tpu_custom_call" | custom-call | bytes 1048576 | tf_op jit(solution)/shard_map/pallas_call | solution.py:400
  2.5 7.6 %all-to-all-start = ((bf16[16,64,512]{2,1,0:T(8,128)(2,1)}), bf16[16,64,512]{2,1,0:T(8,128)(2,1)S(1)}, u32[]{:S(2)}, u32[]{:S(2)}) async-start(bf16[16,64,512]{2,1,0:T(8,128)(2,1)} %get-tuple-element.40), calls=%async_computation | async-start | bytes 2097152 | tf_op jit(solution)/shard_map/all_to_all | solution.py:367
  10.1 1.0 collective-permute-start
  11.2 1.2 collective-permute-done.other
  12.4 5.7 %collective-permute-start.1 = (bf16[64,2048]{1,0:T(8,128)(2,1)S(1)}, bf16[64,2048]{1,0:T(8,128)(2,1)S(1)}, u32[]{:S(2)}, u32[]{:S(2)}) collective-permute-start(bf16[64,2048]{1,0:T(8,128)(2,1)S(1)} %get-tuple-element.42), channel_id=1, source_target_pairs={{0,32},{1,225},{2,34},{3,227},{4,36},{5,229},{6,38},{7,231},{8,40}... | collective-permute-start | bytes 786440 | tf_op jit(solution)/shard_map/ppermute | solution.py:423
  18.0 3.3 %collective-permute-done.1.refs_0_ = bf16[64,2048]{1,0:T(8,128)(2,1)S(1)} collective-permute-done((bf16[64,2048]{1,0:T(8,128)(2,1)S(1)}, bf16[64,2048]{1,0:T(8,128)(2,1)S(1)}, u32[]{:S(2)}, u32[]{:S(2)}) %collective-permute-start.1) | collective-permute-done | bytes 262176 | tf_op jit(solution)/shard_map/ppermute | solution.py:423
  21.4 3.4 %collective-permute-start.2 = (bf16[64,2048]{1,0:T(8,128)(2,1)S(1)}, bf16[64,2048]{1,0:T(8,128)(2,1)S(1)}, u32[]{:S(2)}, u32[]{:S(2)}) collective-permute-start(bf16[64,2048]{1,0:T(8,128)(2,1)S(1)} %collective-permute-done.1.refs_0_), channel_id=1, source_target_pairs={{0,32},{1,225},{2,34},{3,227},{4,36},{5,229},{6,38},{7,231},{8,40}... | collective-permute-start | bytes 786440 | tf_op jit(solution)/shard_map/ppermute | solution.py:423
  24.8 3.3 %collective-permute-done.2.refs_1_ = bf16[64,2048]{1,0:T(8,128)(2,1)S(1)} collective-permute-done((bf16[64,2048]{1,0:T(8,128)(2,1)S(1)}, bf16[64,2048]{1,0:T(8,128)(2,1)S(1)}, u32[]{:S(2)}, u32[]{:S(2)}) %collective-permute-start.2) | collective-permute-done | bytes 262176 | tf_op jit(solution)/shard_map/ppermute | solution.py:423
  28.1 0.0 all-to-all-done.mine
  28.1 2.5 %collective-permute-start.3 = (bf16[16,64,512]{2,1,0:T(8,128)(2,1)S(1)}, bf16[16,64,512]{2,1,0:T(8,128)(2,1)S(1)}, u32[]{:S(2)}, u32[]{:S(2)}) collective-permute-start(bf16[16,64,512]{2,1,0:T(8,128)(2,1)S(1)} %all-to-all-done.mine), channel_id=1, source_target_pairs={{0,1},{1,0},{2,3},{3,2},{4,5},{5,4},{6,7},{7,6},{8,9},{9,8},{10,11... | collective-permute-start | bytes 3145736 | tf_op jit(solution)/shard_map/ppermute | solution.py:428
  30.6 3.7 %collective-permute-start.4 = (bf16[64,2048]{1,0:T(8,128)(2,1)S(1)}, bf16[64,2048]{1,0:T(8,128)(2,1)S(1)}, u32[]{:S(2)}, u32[]{:S(2)}) collective-permute-start(bf16[64,2048]{1,0:T(8,128)(2,1)S(1)} %collective-permute-done.2.refs_1_), channel_id=1, source_target_pairs={{0,32},{1,225},{2,34},{3,227},{4,36},{5,229},{6,38},{7,231},{8,40}... | collective-permute-start | bytes 786440 | tf_op jit(solution)/shard_map/ppermute | solution.py:423
  34.4 0.1 pad_add_fusion.here
  34.5 0.1 collective-permute-start.6
  34.6 0.6 collective-permute-start.7
  35.2 3.5 %shard_map.97.hidden = bf16[2048,2048]{1,0:T(8,128)(2,1)S(1)} custom-call(bf16[2048,2048]{1,0:T(8,128)(2,1)} %hidden.1), custom_call_target="tpu_custom_call" | custom-call | bytes 16777216 | tf_op jit(solution)/shard_map/pallas_call | solution.py:432
  38.7 0.0 collective-permute-done.4.refs_2_
  38.7 0.4 collective-permute-start.8
  39.1 1.9 %collective-permute-start.5 = (bf16[32,2048]{1,0:T(8,128)(2,1)S(1)}, bf16[32,2048]{1,0:T(8,128)(2,1)S(1)}, u32[]{:S(2)}, u32[]{:S(2)}) collective-permute-start(bf16[32,2048]{1,0:T(8,128)(2,1)S(1)} %get-tuple-element.81), channel_id=1, source_target_pairs={{0,32},{1,225},{2,34},{3,227},{4,36},{5,229},{6,38},{7,231},{8,40}... | collective-permute-start | bytes 393224 | tf_op jit(solution)/shard_map/ppermute | solution.py:423
  41.0 0.0 collective-permute-done.3.other
  41.0 0.6 collective-permute-start.9
  41.6 3.1 %shard_map.98 = (bf16[2048,256]{1,0:T(8,128)(2,1)S(1)}, bf16[16,128,256]{2,1,0:T(8,128)(2,1)}) custom-call(s32[3]{0:T(128)S(1)} %pad_add_fusion.here, bf16[2048,2048]{1,0:T(8,128)(2,1)S(1)} %shard_map.97.hidden, bf16[16,64,512]{2,1,0:T(8,128)(2,1)S(1)} %all-to-all-done.mine, bf16[16,64,512]{2,1,0:T(8,128)(2,1)S(1)} %collective-permute-done.3.other), custom_call_target="tpu_custom_call" | custom-call | flops 2147483648 | bytes 10485760 | tf_op jit(solution)/shard_map/pallas_call | solution.py:440
  44.7 0.0 collective-permute-done.6.refs_4_
  44.7 0.0 collective-permute-done.7.refs_5_
  44.7 0.0 collective-permute-done.8.refs_6_
  44.7 0.0 collective-permute-done.5.refs_3_
  44.7 3.2 %shard_map.99 = (bf16[2048,2048]{1,0:T(8,128)(2,1)S(1)}, bf16[256,2048]{1,0:T(8,128)(2,1)}, bf16[2048,256]{1,0:T(8,128)(2,1)}, f32[8,16,128]{2,1,0:T(8,128)S(1)}) custom-call(s32[3]{0:T(128)S(1)} %pad_add_fusion.here, bf16[2048,256]{1,0:T(8,128)(2,1)S(1)} %get-tuple-element.45.unit, bf16[64,2048]{1,0:T(8,128)(2,1)S(1)} %get-tuple-element.41.mine.own, ...), custom_call_target="tpu_custom_call" | custom-call | flops 2147483648 | bytes 12582912 | tf_op jit(solution)/shard_map/pallas_call | solution.py:454
  47.9 0.0 collective-permute-done.9.refs_0_
  47.9 1.4 collective-permute-start.10
  49.4 0.1 collective-permute-start.11
  49.5 12.4 %all_to_all.40.parts = f32[8,16,128]{2,1,0:T(8,128)S(1)} all-to-all(f32[8,16,128]{2,1,0:T(8,128)S(1)} %get-tuple-element.49), channel_id=1, replica_groups=mesh['tok'=8,'proto'=32] {'tok'}, dimensions={0} | all-to-all | bytes 131072 | tf_op jit(solution)/shard_map/all_to_all | solution.py:367
  61.8 1.8 %shard_map.100 = bf16[32,16,128]{2,1,0:T(8,128)(2,1)S(1)} custom-call(f32[8,16,128]{2,1,0:T(8,128)S(1)} %all_to_all.40.parts, bf16[2048,2048]{1,0:T(8,128)(2,1)S(1)} %get-tuple-element.50.scores), custom_call_target="tpu_custom_call" | custom-call | flops 8388608 | bytes 8388608 | tf_op jit(solution)/shard_map/pallas_call | solution.py:512
  63.7 0.0 collective-permute-done.11.refs_4_
  63.7 0.0 collective-permute-done.10.refs_1_
  63.7 0.1 collective-permute-start.12
  63.8 2.1 %collective-permute-start.13 = (bf16[32,2048]{1,0:T(8,128)(2,1)S(1)}, bf16[32,2048]{1,0:T(8,128)(2,1)S(1)}, u32[]{:S(2)}, u32[]{:S(2)}) collective-permute-start(bf16[32,2048]{1,0:T(8,128)(2,1)S(1)} %slice.29), channel_id=1, source_target_pairs={{0,1},{1,0},{2,3},{3,2},{4,5},{5,4},{6,7},{7,6},{8,9},{9,8},{10,11... | collective-permute-start | bytes 393224 | tf_op jit(solution)/shard_map/ppermute | solution.py:506
  66.0 14.0 %all_to_all.41.parts = bf16[32,16,128]{2,1,0:T(8,128)(2,1)S(1)} all-to-all(bf16[32,16,128]{2,1,0:T(8,128)(2,1)S(1)} %shard_map.100), channel_id=1, replica_groups=mesh['tok'=8,'proto'=32] {'proto'}, dimensions={0} | all-to-all | bytes 262144 | tf_op jit(solution)/shard_map/all_to_all | solution.py:367
  80.0 2.2 %shard_map.101 = f32[8,16,128]{2,1,0:T(8,128)S(1)} custom-call(bf16[32,16,128]{2,1,0:T(8,128)(2,1)S(1)} %all_to_all.41.parts, bf16[2048,2048]{1,0:T(8,128)(2,1)S(1)} %get-tuple-element.50.scores), custom_call_target="tpu_custom_call" | custom-call | flops 8388608 | bytes 8388608 | tf_op jit(solution)/shard_map/pallas_call | solution.py:514
  82.2 0.0 collective-permute-done.13.refs_5_
  82.2 0.0 collective-permute-done.12.refs_2_
  82.2 0.5 collective-permute-start.15
  82.7 2.4 %collective-permute-start.14 = (bf16[32,2048]{1,0:T(8,128)(2,1)S(1)}, bf16[32,2048]{1,0:T(8,128)(2,1)S(1)}, u32[]{:S(2)}, u32[]{:S(2)}) collective-permute-start(bf16[32,2048]{1,0:T(8,128)(2,1)S(1)} %get-tuple-element.79), channel_id=1, source_target_pairs={{0,32},{1,225},{2,34},{3,227},{4,36},{5,229},{6,38},{7,231},{8,40}... | collective-permute-start | bytes 393224 | tf_op jit(solution)/shard_map/ppermute | solution.py:508
  85.1 9.6 %all_to_all.42.parts = f32[8,16,128]{2,1,0:T(8,128)S(1)} all-to-all(f32[8,16,128]{2,1,0:T(8,128)S(1)} %shard_map.101), channel_id=1, replica_groups=mesh['tok'=8,'proto'=32] {'tok'}, dimensions={0} | all-to-all | bytes 131072 | tf_op jit(solution)/shard_map/all_to_all | solution.py:367
  94.7 0.0 copy-start.1
  94.7 1.8 %shard_map.102 = bf16[32,16,128]{2,1,0:T(8,128)(2,1)S(1)} custom-call(f32[8,16,128]{2,1,0:T(8,128)S(1)} %all_to_all.42.parts, bf16[2048,2048]{1,0:T(8,128)(2,1)S(1)} %get-tuple-element.50.scores), custom_call_target="tpu_custom_call" | custom-call | flops 8388608 | bytes 8388608 | tf_op jit(solution)/shard_map/pallas_call | solution.py:516
  96.5 0.0 collective-permute-done.15.refs_6_
  96.5 0.0 collective-permute-done.14.refs_3_
  96.5 12.6 %all_to_all.43.parts = bf16[32,16,128]{2,1,0:T(8,128)(2,1)S(1)} all-to-all(bf16[32,16,128]{2,1,0:T(8,128)(2,1)S(1)} %shard_map.102), channel_id=1, replica_groups=mesh['tok'=8,'proto'=32] {'proto'}, dimensions={0} | all-to-all | bytes 262144 | tf_op jit(solution)/shard_map/all_to_all | solution.py:367
  109.1 0.0 copy-start.2
  109.1 3.4 %shard_map.103 = (f32[8,16,128]{2,1,0:T(8,128)}, bf16[256,2048]{1,0:T(8,128)(2,1)}) custom-call(s32[3]{0:T(128)S(1)} %pad_add_fusion.here, bf16[32,16,128]{2,1,0:T(8,128)(2,1)S(1)} %all_to_all.43.parts, bf16[2048,2048]{1,0:T(8,128)(2,1)S(1)} %get-tuple-element.50.scores, bf16[64,2048]{1,0:T(8,128)(2,1)S(1)} %get-tuple-element.41.mine.own, ...), custom_call_target="tpu_custom_call" | custom-call | flops 8388608 | bytes 8388608 | tf_op jit(solution)/shard_map/pallas_call | solution.py:518
  112.5 0.0 copy-start
  112.5 4.1 %all-to-all-start.5 = ((f32[8,16,128]{2,1,0:T(8,128)}), f32[8,16,128]{2,1,0:T(8,128)}, u32[]{:S(2)}, u32[]{:S(2)}) async-start(f32[8,16,128]{2,1,0:T(8,128)} %get-tuple-element.64), calls=%async_computation.5 | async-start | bytes 131072 | tf_op jit(solution)/shard_map/all_to_all | solution.py:367
  116.6 0.0 copy-done.1
  116.6 5.2 %shard_map.104 = (f32[256,2048]{1,0:T(8,128)S(1)}, f32[8,2048]{1,0:T(8,128)}, f32[256,384]{1,0:T(8,128)S(1)}, f32[256,256]{1,0:T(8,128)}, f32[256,128]{1,0:T(8,128)}) custom-call(s32[1,256]{1,0:T(1,128)S(1)} %bitcast.10, bf16[256,2048]{1,0:T(8,128)(2,1)} %hidden.2, bf16[2048,256]{1,0:T(8,128)(2,1)} %bitcast.7, bf16[2048,256]{1,0:T(8,128)(2,1)} %get-tuple-element.66.unit, ...), custom_call_target="tpu_custom_call" | custom-call | flops 1342177280 | bytes 8388608 | tf_op jit(solution)/shard_map/pallas_call | solution.py:524
  121.8 1.9 %all-to-all-done.5.parts = f32[8,16,128]{2,1,0:T(8,128)} async-done(((f32[8,16,128]{2,1,0:T(8,128)}), f32[8,16,128]{2,1,0:T(8,128)}, u32[]{:S(2)}, u32[]{:S(2)}) %all-to-all-start.5) | async-done | bytes 65568 | tf_op jit(solution)/shard_map/all_to_all | solution.py:367
  123.8 3.3 %shard_map.105 = (f32[128,640]{1,0:T(8,128)S(1)}, f32[128,640]{1,0:T(8,128)S(1)}) custom-call(s32[3]{0:T(128)S(1)} %pad_add_fusion.here, f32[8,16,128]{2,1,0:T(8,128)} %all-to-all-done.5.parts, f32[256,2048]{1,0:T(8,128)S(1)} %get-tuple-element.69.masked, f32[256,384]{1,0:T(8,128)S(1)} %get-tuple-element.70.unit.unit_float, ...), custom_call_target="tpu_custom_call" | custom-call | flops 536870912 | bytes 4194304 | tf_op jit(solution)/shard_map/pallas_call | solution.py:555
  127.1 1.7 %collective-permute-start.16 = (f32[128,640]{1,0:T(8,128)S(1)}, f32[128,640]{1,0:T(8,128)S(1)}, u32[]{:S(2)}, u32[]{:S(2)}) collective-permute-start(f32[128,640]{1,0:T(8,128)S(1)} %get-tuple-element.75), channel_id=1, source_target_pairs={{0,1},{1,0},{2,3},{3,2},{4,5},{5,4},{6,7},{7,6},{8,9},{9,8},{10,11... | collective-permute-start | bytes 983048 | tf_op jit(solution)/shard_map/ppermute | solution.py:580
  128.8 1.3 collective-permute-done.16.second
  130.1 10.8 %all_to_all.44.parts = f32[16,8,640]{2,1,0:T(8,128)S(1)} all-to-all(f32[16,8,640]{2,1,0:T(8,128)S(1)} %bitcast.9), channel_id=1, replica_groups={{0,2,4,6,8,10,12,14,16,18,20,22,24,26,28,30},{1,3,5,7,9,11,13,15,17,19,..., dimensions={0} | all-to-all | bytes 655360 | tf_op jit(solution)/shard_map/all_to_all | solution.py:367
  140.8 0.0 copy-done.2
  140.8 1.2 shard_map.107
  142.1 13.4 %all_to_all.45.parts = bf16[32,16,128]{2,1,0:T(8,128)(2,1)S(1)} all-to-all(bf16[32,16,128]{2,1,0:T(8,128)(2,1)S(1)} %get-tuple-element.77), channel_id=1, replica_groups=mesh['tok'=8,'proto'=32] {'proto'}, dimensions={0} | all-to-all | bytes 262144 | tf_op jit(solution)/shard_map/all_to_all | solution.py:367
  155.5 0.0 copy-done
  155.5 1.4 shard_map.108
  (8 shorter events, 0.1 us)
Async XLA Ops:
  2.5 25.5 %all-to-all-start = ((bf16[16,64,512]{2,1,0:T(8,128)(2,1)}), bf16[16,64,512]{2,1,0:T(8,128)(2,1)S(1)}, u32[]{:S(2)}, u32[]{:S(2)}) async-start(bf16[16,64,512]{2,1,0:T(8,128)(2,1)} %get-tuple-element.40), calls=%async_computation | async-start | bytes 2097152 | tf_op jit(solution)/shard_map/all_to_all | solution.py:367
  10.1 2.2 %collective-permute-start = (bf16[64,2048]{1,0:T(8,128)(2,1)S(1)}, bf16[64,2048]{1,0:T(8,128)(2,1)S(1)}, u32[]{:S(2)}, u32[]{:S(2)}) collective-permute-start(bf16[64,2048]{1,0:T(8,128)(2,1)S(1)} %get-tuple-element.41.mine.own), channel_id=1, source_target_pairs={{0,1},{1,0},{2,3},{3,2},{4,5},{5,4},{6,7},{7,6},{8,9},{9,8},{10,11... | collective-permute-start | bytes 786440 | tf_op jit(solution)/shard_map/ppermute | solution.py:409
  12.4 9.0 %collective-permute-start.1 = (bf16[64,2048]{1,0:T(8,128)(2,1)S(1)}, bf16[64,2048]{1,0:T(8,128)(2,1)S(1)}, u32[]{:S(2)}, u32[]{:S(2)}) collective-permute-start(bf16[64,2048]{1,0:T(8,128)(2,1)S(1)} %get-tuple-element.42), channel_id=1, source_target_pairs={{0,32},{1,225},{2,34},{3,227},{4,36},{5,229},{6,38},{7,231},{8,40}... | collective-permute-start | bytes 786440 | tf_op jit(solution)/shard_map/ppermute | solution.py:423
  21.4 6.7 %collective-permute-start.2 = (bf16[64,2048]{1,0:T(8,128)(2,1)S(1)}, bf16[64,2048]{1,0:T(8,128)(2,1)S(1)}, u32[]{:S(2)}, u32[]{:S(2)}) collective-permute-start(bf16[64,2048]{1,0:T(8,128)(2,1)S(1)} %collective-permute-done.1.refs_0_), channel_id=1, source_target_pairs={{0,32},{1,225},{2,34},{3,227},{4,36},{5,229},{6,38},{7,231},{8,40}... | collective-permute-start | bytes 786440 | tf_op jit(solution)/shard_map/ppermute | solution.py:423
  28.1 12.9 %collective-permute-start.3 = (bf16[16,64,512]{2,1,0:T(8,128)(2,1)S(1)}, bf16[16,64,512]{2,1,0:T(8,128)(2,1)S(1)}, u32[]{:S(2)}, u32[]{:S(2)}) collective-permute-start(bf16[16,64,512]{2,1,0:T(8,128)(2,1)S(1)} %all-to-all-done.mine), channel_id=1, source_target_pairs={{0,1},{1,0},{2,3},{3,2},{4,5},{5,4},{6,7},{7,6},{8,9},{9,8},{10,11... | collective-permute-start | bytes 3145736 | tf_op jit(solution)/shard_map/ppermute | solution.py:428
  30.6 8.0 %collective-permute-start.4 = (bf16[64,2048]{1,0:T(8,128)(2,1)S(1)}, bf16[64,2048]{1,0:T(8,128)(2,1)S(1)}, u32[]{:S(2)}, u32[]{:S(2)}) collective-permute-start(bf16[64,2048]{1,0:T(8,128)(2,1)S(1)} %collective-permute-done.2.refs_1_), channel_id=1, source_target_pairs={{0,32},{1,225},{2,34},{3,227},{4,36},{5,229},{6,38},{7,231},{8,40}... | collective-permute-start | bytes 786440 | tf_op jit(solution)/shard_map/ppermute | solution.py:423
  34.5 10.2 %collective-permute-start.6 = (bf16[32,2048]{1,0:T(8,128)(2,1)S(1)}, bf16[32,2048]{1,0:T(8,128)(2,1)S(1)}, u32[]{:S(2)}, u32[]{:S(2)}) collective-permute-start(bf16[32,2048]{1,0:T(8,128)(2,1)S(1)} %slice.33), channel_id=1, source_target_pairs={{0,1},{1,0},{2,3},{3,2},{4,5},{5,4},{6,7},{7,6},{8,9},{9,8},{10,11... | collective-permute-start | bytes 393224 | tf_op jit(solution)/shard_map/ppermute | solution.py:425
  34.6 10.1 %collective-permute-start.7 = (bf16[32,2048]{1,0:T(8,128)(2,1)S(1)}, bf16[32,2048]{1,0:T(8,128)(2,1)S(1)}, u32[]{:S(2)}, u32[]{:S(2)}) collective-permute-start(bf16[32,2048]{1,0:T(8,128)(2,1)S(1)} %slice.34), channel_id=1, source_target_pairs={{0,1},{1,0},{2,3},{3,2},{4,5},{5,4},{6,7},{7,6},{8,9},{9,8},{10,11... | collective-permute-start | bytes 393224 | tf_op jit(solution)/shard_map/ppermute | solution.py:425
  38.7 6.0 %collective-permute-start.8 = (bf16[32,2048]{1,0:T(8,128)(2,1)S(1)}, bf16[32,2048]{1,0:T(8,128)(2,1)S(1)}, u32[]{:S(2)}, u32[]{:S(2)}) collective-permute-start(bf16[32,2048]{1,0:T(8,128)(2,1)S(1)} %get-tuple-element.80), channel_id=1, source_target_pairs={{0,1},{1,0},{2,3},{3,2},{4,5},{5,4},{6,7},{7,6},{8,9},{9,8},{10,11... | collective-permute-start | bytes 393224 | tf_op jit(solution)/shard_map/ppermute | solution.py:425
  39.1 5.6 %collective-permute-start.5 = (bf16[32,2048]{1,0:T(8,128)(2,1)S(1)}, bf16[32,2048]{1,0:T(8,128)(2,1)S(1)}, u32[]{:S(2)}, u32[]{:S(2)}) collective-permute-start(bf16[32,2048]{1,0:T(8,128)(2,1)S(1)} %get-tuple-element.81), channel_id=1, source_target_pairs={{0,32},{1,225},{2,34},{3,227},{4,36},{5,229},{6,38},{7,231},{8,40}... | collective-permute-start | bytes 393224 | tf_op jit(solution)/shard_map/ppermute | solution.py:423
  41.0 6.9 %collective-permute-start.9 = (bf16[64,2048]{1,0:T(8,128)(2,1)S(1)}, bf16[64,2048]{1,0:T(8,128)(2,1)S(1)}, u32[]{:S(2)}, u32[]{:S(2)}) collective-permute-start(bf16[64,2048]{1,0:T(8,128)(2,1)S(1)} %get-tuple-element.48), channel_id=1, source_target_pairs={{0,32},{1,225},{2,34},{3,227},{4,36},{5,229},{6,38},{7,231},{8,40}... | collective-permute-start | bytes 786440 | tf_op jit(solution)/shard_map/ppermute | solution.py:431
  47.9 15.7 %collective-permute-start.10 = (bf16[64,2048]{1,0:T(8,128)(2,1)S(1)}, bf16[64,2048]{1,0:T(8,128)(2,1)S(1)}, u32[]{:S(2)}, u32[]{:S(2)}) collective-permute-start(bf16[64,2048]{1,0:T(8,128)(2,1)S(1)} %collective-permute-done.9.refs_0_), channel_id=1, source_target_pairs={{0,32},{1,225},{2,34},{3,227},{4,36},{5,229},{6,38},{7,231},{8,40}... | collective-permute-start | bytes 786440 | tf_op jit(solution)/shard_map/ppermute | solution.py:508
  49.4 14.3 %collective-permute-start.11 = (bf16[32,2048]{1,0:T(8,128)(2,1)S(1)}, bf16[32,2048]{1,0:T(8,128)(2,1)S(1)}, u32[]{:S(2)}, u32[]{:S(2)}) collective-permute-start(bf16[32,2048]{1,0:T(8,128)(2,1)S(1)} %slice.28), channel_id=1, source_target_pairs={{0,1},{1,0},{2,3},{3,2},{4,5},{5,4},{6,7},{7,6},{8,9},{9,8},{10,11... | collective-permute-start | bytes 393224 | tf_op jit(solution)/shard_map/ppermute | solution.py:506
  63.7 18.5 %collective-permute-start.12 = (bf16[64,2048]{1,0:T(8,128)(2,1)S(1)}, bf16[64,2048]{1,0:T(8,128)(2,1)S(1)}, u32[]{:S(2)}, u32[]{:S(2)}) collective-permute-start(bf16[64,2048]{1,0:T(8,128)(2,1)S(1)} %collective-permute-done.10.refs_1_), channel_id=1, source_target_pairs={{0,32},{1,225},{2,34},{3,227},{4,36},{5,229},{6,38},{7,231},{8,40}... | collective-permute-start | bytes 786440 | tf_op jit(solution)/shard_map/ppermute | solution.py:508
  63.8 18.4 %collective-permute-start.13 = (bf16[32,2048]{1,0:T(8,128)(2,1)S(1)}, bf16[32,2048]{1,0:T(8,128)(2,1)S(1)}, u32[]{:S(2)}, u32[]{:S(2)}) collective-permute-start(bf16[32,2048]{1,0:T(8,128)(2,1)S(1)} %slice.29), channel_id=1, source_target_pairs={{0,1},{1,0},{2,3},{3,2},{4,5},{5,4},{6,7},{7,6},{8,9},{9,8},{10,11... | collective-permute-start | bytes 393224 | tf_op jit(solution)/shard_map/ppermute | solution.py:506
  82.2 14.3 %collective-permute-start.15 = (bf16[32,2048]{1,0:T(8,128)(2,1)S(1)}, bf16[32,2048]{1,0:T(8,128)(2,1)S(1)}, u32[]{:S(2)}, u32[]{:S(2)}) collective-permute-start(bf16[32,2048]{1,0:T(8,128)(2,1)S(1)} %get-tuple-element.78), channel_id=1, source_target_pairs={{0,1},{1,0},{2,3},{3,2},{4,5},{5,4},{6,7},{7,6},{8,9},{9,8},{10,11... | collective-permute-start | bytes 393224 | tf_op jit(solution)/shard_map/ppermute | solution.py:506
  82.7 13.8 %collective-permute-start.14 = (bf16[32,2048]{1,0:T(8,128)(2,1)S(1)}, bf16[32,2048]{1,0:T(8,128)(2,1)S(1)}, u32[]{:S(2)}, u32[]{:S(2)}) collective-permute-start(bf16[32,2048]{1,0:T(8,128)(2,1)S(1)} %get-tuple-element.79), channel_id=1, source_target_pairs={{0,32},{1,225},{2,34},{3,227},{4,36},{5,229},{6,38},{7,231},{8,40}... | collective-permute-start | bytes 393224 | tf_op jit(solution)/shard_map/ppermute | solution.py:508
  94.7 21.9 %copy-start.1 = (s32[256]{0:T(256)S(1)}, s32[256]{0:T(256)}, u32[]{:S(2)}) copy-start(s32[256]{0:T(256)} %param.14) | copy-start | bytes 3076
  109.1 31.8 %copy-start.2 = (s32[8]{0:T(128)S(1)}, s32[8]{0:T(128)}, u32[]{:S(2)}) copy-start(s32[8]{0:T(128)} %counts.1) | copy-start | bytes 100
  112.5 43.0 %copy-start = (bf16[16,128,256]{2,1,0:T(8,128)(2,1)S(1)}, bf16[16,128,256]{2,1,0:T(8,128)(2,1)}, u32[]{:S(2)}) copy-start(bf16[16,128,256]{2,1,0:T(8,128)(2,1)} %get-tuple-element.65) | copy-start | bytes 3145732
  112.5 11.3 %all-to-all-start.5 = ((f32[8,16,128]{2,1,0:T(8,128)}), f32[8,16,128]{2,1,0:T(8,128)}, u32[]{:S(2)}, u32[]{:S(2)}) async-start(f32[8,16,128]{2,1,0:T(8,128)} %get-tuple-element.64), calls=%async_computation.5 | async-start | bytes 131072 | tf_op jit(solution)/shard_map/all_to_all | solution.py:367
  127.1 3.0 %collective-permute-start.16 = (f32[128,640]{1,0:T(8,128)S(1)}, f32[128,640]{1,0:T(8,128)S(1)}, u32[]{:S(2)}, u32[]{:S(2)}) collective-permute-start(f32[128,640]{1,0:T(8,128)S(1)} %get-tuple-element.75), channel_id=1, source_target_pairs={{0,1},{1,0},{2,3},{3,2},{4,5},{5,4},{6,7},{7,6},{8,9},{9,8},{10,11... | collective-permute-start | bytes 983048 | tf_op jit(solution)/shard_map/ppermute | solution.py:580

commit v8 on v7

--- a/solution.py
+++ b/solution.py
@@ -157,7 +157,7 @@
             sums[pl.ds(c * count + k, 1), :] = acc[:, k * 128 : (k + 1) * 128]
         return 0
 
-    lax.fori_loop(0, whole.shape[1] // step, over_columns, 0, unroll=4)
+    lax.fori_loop(0, whole.shape[1] // step, over_columns, 0, unroll=True)
     settle(rest)
     columns[...] = jnp.broadcast_to(sums[...][None], columns.shape)
 
@@ -176,7 +176,7 @@
             sums[pl.ds(i * group + r, 1), :] = jnp.sum(acc.T, axis=0, keepdims=True)
         return 0
 
-    lax.fori_loop(0, scores.shape[0] // (group * 128), over_rows, 0, unroll=2)
+    lax.fori_loop(0, scores.shape[0] // (group * 128), over_rows, 0, unroll=True)
     rows[...] = jnp.broadcast_to(sums[...].astype(rows.dtype)[None], rows.shape)
 
 

time: 157 us -> 157 us (level)
  no operation moved by 1% of the time
where the time goes in v8:
time: 157 us
  blocking collectives  72.7 us (46%)
  starting transfers between devices  40.4 us (26%)
  Pallas kernels  31.8 us (20%)
  waiting for transfers between devices  10.8 us (7%)
    all_to_all x6, blocking collectives, exchange(): lax.all_to_all(blocks, axis, 0, 0, tiled=True, axis_index_groups=groups)  72.7 us
    ppermute x4, starting transfers between devices, shards(): lax.ppermute(sent if hop < hops - 1 else sent[:rows], ('tok', 'proto'), a...  14.7 us
    all_to_all x2, starting transfers between devices, exchange(): lax.all_to_all(blocks, axis, 0, 0, tiled=True, axis_index_groups=groups)  11.9 us
    ppermute x4, waiting for transfers between devices, shards(): lax.ppermute(sent if hop < hops - 1 else sent[:rows], ('tok', 'proto'), a...  6.64 us
    pallas_call x1, Pallas kernels, shards(): call(student_kernel, (pltpu.VMEM((slots, local), f32), pltpu.HBM((8, loca...  5.2 us
    ppermute x3, starting transfers between devices, onward(): late.append(lax.ppermute(sent, ('tok', 'proto'), along))  4.12 us
    pallas_call x1, Pallas kernels, shards(): call(stage_kernel, pltpu.VMEM(hidden.shape, bf16), [HB], VM, (0, 16 * MIB...  3.5 us
    pallas_call x2, Pallas kernels, shards(): sums = row_call(exchange(columns, 'tok'), held(scores))  3.45 us
  transfers between devices with their start and end apart: 19, of which 5 were waited for; matrix products, arithmetic and copies ran while one was open for 0% of the time, Pallas kernels for 13%

profile of v8, /device:TPU:1, one launch (start us, length us, event | category | flops | bytes accessed | tf_op | source)
XLA Modules:
  0.0 156.7 jit_solution(11078639148598895527)
XLA Ops:
  0.6 1.9 %shard_map.95 = (bf16[16,64,512]{2,1,0:T(8,128)(2,1)}, bf16[64,2048]{1,0:T(8,128)(2,1)S(1)}) custom-call(bf16[64,256]{1,0:T(8,128)(2,1)} %teacher.1, bf16[64,256]{1,0:T(8,128)(2,1)} %student.1, bf16[32,2048]{1,0:T(8,128)(2,1)} %first.1, bf16[32,2048]{1,0:T(8,128)(2,1)} %second.1), custom_call_target="tpu_custom_call" | custom-call | bytes 1048576 | tf_op jit(solution)/shard_map/pallas_call | solution.py:400
  2.5 7.6 %all-to-all-start = ((bf16[16,64,512]{2,1,0:T(8,128)(2,1)}), bf16[16,64,512]{2,1,0:T(8,128)(2,1)S(1)}, u32[]{:S(2)}, u32[]{:S(2)}) async-start(bf16[16,64,512]{2,1,0:T(8,128)(2,1)} %get-tuple-element.40), calls=%async_computation | async-start | bytes 2097152 | tf_op jit(solution)/shard_map/all_to_all | solution.py:367
  10.1 1.0 collective-permute-start
  11.2 1.2 collective-permute-done.other
  12.4 5.7 %collective-permute-start.1 = (bf16[64,2048]{1,0:T(8,128)(2,1)S(1)}, bf16[64,2048]{1,0:T(8,128)(2,1)S(1)}, u32[]{:S(2)}, u32[]{:S(2)}) collective-permute-start(bf16[64,2048]{1,0:T(8,128)(2,1)S(1)} %get-tuple-element.42), channel_id=1, source_target_pairs={{0,32},{1,225},{2,34},{3,227},{4,36},{5,229},{6,38},{7,231},{8,40}... | collective-permute-start | bytes 786440 | tf_op jit(solution)/shard_map/ppermute | solution.py:423
  18.0 3.3 %collective-permute-done.1.refs_0_ = bf16[64,2048]{1,0:T(8,128)(2,1)S(1)} collective-permute-done((bf16[64,2048]{1,0:T(8,128)(2,1)S(1)}, bf16[64,2048]{1,0:T(8,128)(2,1)S(1)}, u32[]{:S(2)}, u32[]{:S(2)}) %collective-permute-start.1) | collective-permute-done | bytes 262176 | tf_op jit(solution)/shard_map/ppermute | solution.py:423
  21.4 3.4 %collective-permute-start.2 = (bf16[64,2048]{1,0:T(8,128)(2,1)S(1)}, bf16[64,2048]{1,0:T(8,128)(2,1)S(1)}, u32[]{:S(2)}, u32[]{:S(2)}) collective-permute-start(bf16[64,2048]{1,0:T(8,128)(2,1)S(1)} %collective-permute-done.1.refs_0_), channel_id=1, source_target_pairs={{0,32},{1,225},{2,34},{3,227},{4,36},{5,229},{6,38},{7,231},{8,40}... | collective-permute-start | bytes 786440 | tf_op jit(solution)/shard_map/ppermute | solution.py:423
  24.8 3.3 %collective-permute-done.2.refs_1_ = bf16[64,2048]{1,0:T(8,128)(2,1)S(1)} collective-permute-done((bf16[64,2048]{1,0:T(8,128)(2,1)S(1)}, bf16[64,2048]{1,0:T(8,128)(2,1)S(1)}, u32[]{:S(2)}, u32[]{:S(2)}) %collective-permute-start.2) | collective-permute-done | bytes 262176 | tf_op jit(solution)/shard_map/ppermute | solution.py:423
  28.1 0.0 all-to-all-done.mine
  28.1 2.5 %collective-permute-start.3 = (bf16[16,64,512]{2,1,0:T(8,128)(2,1)S(1)}, bf16[16,64,512]{2,1,0:T(8,128)(2,1)S(1)}, u32[]{:S(2)}, u32[]{:S(2)}) collective-permute-start(bf16[16,64,512]{2,1,0:T(8,128)(2,1)S(1)} %all-to-all-done.mine), channel_id=1, source_target_pairs={{0,1},{1,0},{2,3},{3,2},{4,5},{5,4},{6,7},{7,6},{8,9},{9,8},{10,11... | collective-permute-start | bytes 3145736 | tf_op jit(solution)/shard_map/ppermute | solution.py:428
  30.6 3.7 %collective-permute-start.4 = (bf16[64,2048]{1,0:T(8,128)(2,1)S(1)}, bf16[64,2048]{1,0:T(8,128)(2,1)S(1)}, u32[]{:S(2)}, u32[]{:S(2)}) collective-permute-start(bf16[64,2048]{1,0:T(8,128)(2,1)S(1)} %collective-permute-done.2.refs_1_), channel_id=1, source_target_pairs={{0,32},{1,225},{2,34},{3,227},{4,36},{5,229},{6,38},{7,231},{8,40}... | collective-permute-start | bytes 786440 | tf_op jit(solution)/shard_map/ppermute | solution.py:423
  34.4 0.1 pad_add_fusion.here
  34.5 0.1 collective-permute-start.6
  34.6 0.6 collective-permute-start.7
  35.2 3.5 %shard_map.97.hidden = bf16[2048,2048]{1,0:T(8,128)(2,1)S(1)} custom-call(bf16[2048,2048]{1,0:T(8,128)(2,1)} %hidden.1), custom_call_target="tpu_custom_call" | custom-call | bytes 16777216 | tf_op jit(solution)/shard_map/pallas_call | solution.py:432
  38.7 0.0 collective-permute-done.4.refs_2_
  38.7 0.4 collective-permute-start.8
  39.1 1.9 %collective-permute-start.5 = (bf16[32,2048]{1,0:T(8,128)(2,1)S(1)}, bf16[32,2048]{1,0:T(8,128)(2,1)S(1)}, u32[]{:S(2)}, u32[]{:S(2)}) collective-permute-start(bf16[32,2048]{1,0:T(8,128)(2,1)S(1)} %get-tuple-element.81), channel_id=1, source_target_pairs={{0,32},{1,225},{2,34},{3,227},{4,36},{5,229},{6,38},{7,231},{8,40}... | collective-permute-start | bytes 393224 | tf_op jit(solution)/shard_map/ppermute | solution.py:423
  41.0 0.0 collective-permute-done.3.other
  41.0 0.6 collective-permute-start.9
  41.6 3.1 %shard_map.98 = (bf16[2048,256]{1,0:T(8,128)(2,1)S(1)}, bf16[16,128,256]{2,1,0:T(8,128)(2,1)}) custom-call(s32[3]{0:T(128)S(1)} %pad_add_fusion.here, bf16[2048,2048]{1,0:T(8,128)(2,1)S(1)} %shard_map.97.hidden, bf16[16,64,512]{2,1,0:T(8,128)(2,1)S(1)} %all-to-all-done.mine, bf16[16,64,512]{2,1,0:T(8,128)(2,1)S(1)} %collective-permute-done.3.other), custom_call_target="tpu_custom_call" | custom-call | flops 2147483648 | bytes 10485760 | tf_op jit(solution)/shard_map/pallas_call | solution.py:440
  44.7 0.0 collective-permute-done.6.refs_4_
  44.7 0.0 collective-permute-done.7.refs_5_
  44.7 0.0 collective-permute-done.8.refs_6_
  44.7 0.0 collective-permute-done.5.refs_3_
  44.7 3.0 %shard_map.99 = (bf16[2048,2048]{1,0:T(8,128)(2,1)S(1)}, bf16[256,2048]{1,0:T(8,128)(2,1)}, bf16[2048,256]{1,0:T(8,128)(2,1)}, f32[8,16,128]{2,1,0:T(8,128)S(1)}) custom-call(s32[3]{0:T(128)S(1)} %pad_add_fusion.here, bf16[2048,256]{1,0:T(8,128)(2,1)S(1)} %get-tuple-element.45.unit, bf16[64,2048]{1,0:T(8,128)(2,1)S(1)} %get-tuple-element.41.mine.own, ...), custom_call_target="tpu_custom_call" | custom-call | flops 2147483648 | bytes 12582912 | tf_op jit(solution)/shard_map/pallas_call | solution.py:454
  47.7 0.0 collective-permute-done.9.refs_0_
  47.8 1.6 %collective-permute-start.10 = (bf16[64,2048]{1,0:T(8,128)(2,1)S(1)}, bf16[64,2048]{1,0:T(8,128)(2,1)S(1)}, u32[]{:S(2)}, u32[]{:S(2)}) collective-permute-start(bf16[64,2048]{1,0:T(8,128)(2,1)S(1)} %collective-permute-done.9.refs_0_), channel_id=1, source_target_pairs={{0,32},{1,225},{2,34},{3,227},{4,36},{5,229},{6,38},{7,231},{8,40}... | collective-permute-start | bytes 786440 | tf_op jit(solution)/shard_map/ppermute | solution.py:508
  49.4 0.1 collective-permute-start.11
  49.5 12.4 %all_to_all.40.parts = f32[8,16,128]{2,1,0:T(8,128)S(1)} all-to-all(f32[8,16,128]{2,1,0:T(8,128)S(1)} %get-tuple-element.49), channel_id=1, replica_groups=mesh['tok'=8,'proto'=32] {'tok'}, dimensions={0} | all-to-all | bytes 131072 | tf_op jit(solution)/shard_map/all_to_all | solution.py:367
  61.8 1.7 %shard_map.100 = bf16[32,16,128]{2,1,0:T(8,128)(2,1)S(1)} custom-call(f32[8,16,128]{2,1,0:T(8,128)S(1)} %all_to_all.40.parts, bf16[2048,2048]{1,0:T(8,128)(2,1)S(1)} %get-tuple-element.50.scores), custom_call_target="tpu_custom_call" | custom-call | flops 8388608 | bytes 8388608 | tf_op jit(solution)/shard_map/pallas_call | solution.py:512
  63.6 0.0 collective-permute-done.11.refs_4_
  63.6 0.0 collective-permute-done.10.refs_1_
  63.6 0.1 collective-permute-start.12
  63.7 2.1 %collective-permute-start.13 = (bf16[32,2048]{1,0:T(8,128)(2,1)S(1)}, bf16[32,2048]{1,0:T(8,128)(2,1)S(1)}, u32[]{:S(2)}, u32[]{:S(2)}) collective-permute-start(bf16[32,2048]{1,0:T(8,128)(2,1)S(1)} %slice.29), channel_id=1, source_target_pairs={{0,1},{1,0},{2,3},{3,2},{4,5},{5,4},{6,7},{7,6},{8,9},{9,8},{10,11... | collective-permute-start | bytes 393224 | tf_op jit(solution)/shard_map/ppermute | solution.py:506
  65.9 14.0 %all_to_all.41.parts = bf16[32,16,128]{2,1,0:T(8,128)(2,1)S(1)} all-to-all(bf16[32,16,128]{2,1,0:T(8,128)(2,1)S(1)} %shard_map.100), channel_id=1, replica_groups=mesh['tok'=8,'proto'=32] {'proto'}, dimensions={0} | all-to-all | bytes 262144 | tf_op jit(solution)/shard_map/all_to_all | solution.py:367
  79.9 2.2 %shard_map.101 = f32[8,16,128]{2,1,0:T(8,128)S(1)} custom-call(bf16[32,16,128]{2,1,0:T(8,128)(2,1)S(1)} %all_to_all.41.parts, bf16[2048,2048]{1,0:T(8,128)(2,1)S(1)} %get-tuple-element.50.scores), custom_call_target="tpu_custom_call" | custom-call | flops 8388608 | bytes 8388608 | tf_op jit(solution)/shard_map/pallas_call | solution.py:514
  82.1 0.0 collective-permute-done.13.refs_5_
  82.1 0.0 collective-permute-done.12.refs_2_
  82.1 0.5 collective-permute-start.15
  82.6 2.4 %collective-permute-start.14 = (bf16[32,2048]{1,0:T(8,128)(2,1)S(1)}, bf16[32,2048]{1,0:T(8,128)(2,1)S(1)}, u32[]{:S(2)}, u32[]{:S(2)}) collective-permute-start(bf16[32,2048]{1,0:T(8,128)(2,1)S(1)} %get-tuple-element.79), channel_id=1, source_target_pairs={{0,32},{1,225},{2,34},{3,227},{4,36},{5,229},{6,38},{7,231},{8,40}... | collective-permute-start | bytes 393224 | tf_op jit(solution)/shard_map/ppermute | solution.py:508
  85.0 9.6 %all_to_all.42.parts = f32[8,16,128]{2,1,0:T(8,128)S(1)} all-to-all(f32[8,16,128]{2,1,0:T(8,128)S(1)} %shard_map.101), channel_id=1, replica_groups=mesh['tok'=8,'proto'=32] {'tok'}, dimensions={0} | all-to-all | bytes 131072 | tf_op jit(solution)/shard_map/all_to_all | solution.py:367
  94.6 0.0 copy-start.1
  94.6 1.7 %shard_map.102 = bf16[32,16,128]{2,1,0:T(8,128)(2,1)S(1)} custom-call(f32[8,16,128]{2,1,0:T(8,128)S(1)} %all_to_all.42.parts, bf16[2048,2048]{1,0:T(8,128)(2,1)S(1)} %get-tuple-element.50.scores), custom_call_target="tpu_custom_call" | custom-call | flops 8388608 | bytes 8388608 | tf_op jit(solution)/shard_map/pallas_call | solution.py:516
  96.3 0.0 collective-permute-done.15.refs_6_
  96.4 0.0 collective-permute-done.14.refs_3_
  96.4 12.6 %all_to_all.43.parts = bf16[32,16,128]{2,1,0:T(8,128)(2,1)S(1)} all-to-all(bf16[32,16,128]{2,1,0:T(8,128)(2,1)S(1)} %shard_map.102), channel_id=1, replica_groups=mesh['tok'=8,'proto'=32] {'proto'}, dimensions={0} | all-to-all | bytes 262144 | tf_op jit(solution)/shard_map/all_to_all | solution.py:367
  108.9 0.0 copy-start.2
  108.9 3.4 %shard_map.103 = (f32[8,16,128]{2,1,0:T(8,128)}, bf16[256,2048]{1,0:T(8,128)(2,1)}) custom-call(s32[3]{0:T(128)S(1)} %pad_add_fusion.here, bf16[32,16,128]{2,1,0:T(8,128)(2,1)S(1)} %all_to_all.43.parts, bf16[2048,2048]{1,0:T(8,128)(2,1)S(1)} %get-tuple-element.50.scores, bf16[64,2048]{1,0:T(8,128)(2,1)S(1)} %get-tuple-element.41.mine.own, ...), custom_call_target="tpu_custom_call" | custom-call | flops 8388608 | bytes 8388608 | tf_op jit(solution)/shard_map/pallas_call | solution.py:518
  112.3 0.0 copy-start
  112.3 4.3 %all-to-all-start.5 = ((f32[8,16,128]{2,1,0:T(8,128)}), f32[8,16,128]{2,1,0:T(8,128)}, u32[]{:S(2)}, u32[]{:S(2)}) async-start(f32[8,16,128]{2,1,0:T(8,128)} %get-tuple-element.64), calls=%async_computation.5 | async-start | bytes 131072 | tf_op jit(solution)/shard_map/all_to_all | solution.py:367
  116.7 0.0 copy-done.1
  116.7 5.2 %shard_map.104 = (f32[256,2048]{1,0:T(8,128)S(1)}, f32[8,2048]{1,0:T(8,128)}, f32[256,384]{1,0:T(8,128)S(1)}, f32[256,256]{1,0:T(8,128)}, f32[256,128]{1,0:T(8,128)}) custom-call(s32[1,256]{1,0:T(1,128)S(1)} %bitcast.10, bf16[256,2048]{1,0:T(8,128)(2,1)} %hidden.2, bf16[2048,256]{1,0:T(8,128)(2,1)} %bitcast.7, bf16[2048,256]{1,0:T(8,128)(2,1)} %get-tuple-element.66.unit, ...), custom_call_target="tpu_custom_call" | custom-call | flops 1342177280 | bytes 8388608 | tf_op jit(solution)/shard_map/pallas_call | solution.py:524
  121.9 1.7 %all-to-all-done.5.parts = f32[8,16,128]{2,1,0:T(8,128)} async-done(((f32[8,16,128]{2,1,0:T(8,128)}), f32[8,16,128]{2,1,0:T(8,128)}, u32[]{:S(2)}, u32[]{:S(2)}) %all-to-all-start.5) | async-done | bytes 65568 | tf_op jit(solution)/shard_map/all_to_all | solution.py:367
  123.6 3.3 %shard_map.105 = (f32[128,640]{1,0:T(8,128)S(1)}, f32[128,640]{1,0:T(8,128)S(1)}) custom-call(s32[3]{0:T(128)S(1)} %pad_add_fusion.here, f32[8,16,128]{2,1,0:T(8,128)} %all-to-all-done.5.parts, f32[256,2048]{1,0:T(8,128)S(1)} %get-tuple-element.69.masked, f32[256,384]{1,0:T(8,128)S(1)} %get-tuple-element.70.unit.unit_float, ...), custom_call_target="tpu_custom_call" | custom-call | flops 536870912 | bytes 4194304 | tf_op jit(solution)/shard_map/pallas_call | solution.py:555
  126.9 1.7 %collective-permute-start.16 = (f32[128,640]{1,0:T(8,128)S(1)}, f32[128,640]{1,0:T(8,128)S(1)}, u32[]{:S(2)}, u32[]{:S(2)}) collective-permute-start(f32[128,640]{1,0:T(8,128)S(1)} %get-tuple-element.75), channel_id=1, source_target_pairs={{0,1},{1,0},{2,3},{3,2},{4,5},{5,4},{6,7},{7,6},{8,9},{9,8},{10,11... | collective-permute-start | bytes 983048 | tf_op jit(solution)/shard_map/ppermute | solution.py:580
  128.6 1.3 collective-permute-done.16.second
  129.9 10.8 %all_to_all.44.parts = f32[16,8,640]{2,1,0:T(8,128)S(1)} all-to-all(f32[16,8,640]{2,1,0:T(8,128)S(1)} %bitcast.9), channel_id=1, replica_groups={{0,2,4,6,8,10,12,14,16,18,20,22,24,26,28,30},{1,3,5,7,9,11,13,15,17,19,..., dimensions={0} | all-to-all | bytes 655360 | tf_op jit(solution)/shard_map/all_to_all | solution.py:367
  140.7 0.0 copy-done.2
  140.7 1.2 shard_map.107
  141.9 13.4 %all_to_all.45.parts = bf16[32,16,128]{2,1,0:T(8,128)(2,1)S(1)} all-to-all(bf16[32,16,128]{2,1,0:T(8,128)(2,1)S(1)} %get-tuple-element.77), channel_id=1, replica_groups=mesh['tok'=8,'proto'=32] {'proto'}, dimensions={0} | all-to-all | bytes 262144 | tf_op jit(solution)/shard_map/all_to_all | solution.py:367
  155.3 0.0 copy-done
  155.3 1.4 shard_map.108
  (8 shorter events, 0.1 us)
Async XLA Ops:
  2.5 25.5 %all-to-all-start = ((bf16[16,64,512]{2,1,0:T(8,128)(2,1)}), bf16[16,64,512]{2,1,0:T(8,128)(2,1)S(1)}, u32[]{:S(2)}, u32[]{:S(2)}) async-start(bf16[16,64,512]{2,1,0:T(8,128)(2,1)} %get-tuple-element.40), calls=%async_computation | async-start | bytes 2097152 | tf_op jit(solution)/shard_map/all_to_all | solution.py:367
  10.1 2.2 %collective-permute-start = (bf16[64,2048]{1,0:T(8,128)(2,1)S(1)}, bf16[64,2048]{1,0:T(8,128)(2,1)S(1)}, u32[]{:S(2)}, u32[]{:S(2)}) collective-permute-start(bf16[64,2048]{1,0:T(8,128)(2,1)S(1)} %get-tuple-element.41.mine.own), channel_id=1, source_target_pairs={{0,1},{1,0},{2,3},{3,2},{4,5},{5,4},{6,7},{7,6},{8,9},{9,8},{10,11... | collective-permute-start | bytes 786440 | tf_op jit(solution)/shard_map/ppermute | solution.py:409
  12.4 9.0 %collective-permute-start.1 = (bf16[64,2048]{1,0:T(8,128)(2,1)S(1)}, bf16[64,2048]{1,0:T(8,128)(2,1)S(1)}, u32[]{:S(2)}, u32[]{:S(2)}) collective-permute-start(bf16[64,2048]{1,0:T(8,128)(2,1)S(1)} %get-tuple-element.42), channel_id=1, source_target_pairs={{0,32},{1,225},{2,34},{3,227},{4,36},{5,229},{6,38},{7,231},{8,40}... | collective-permute-start | bytes 786440 | tf_op jit(solution)/shard_map/ppermute | solution.py:423
  21.4 6.7 %collective-permute-start.2 = (bf16[64,2048]{1,0:T(8,128)(2,1)S(1)}, bf16[64,2048]{1,0:T(8,128)(2,1)S(1)}, u32[]{:S(2)}, u32[]{:S(2)}) collective-permute-start(bf16[64,2048]{1,0:T(8,128)(2,1)S(1)} %collective-permute-done.1.refs_0_), channel_id=1, source_target_pairs={{0,32},{1,225},{2,34},{3,227},{4,36},{5,229},{6,38},{7,231},{8,40}... | collective-permute-start | bytes 786440 | tf_op jit(solution)/shard_map/ppermute | solution.py:423
  28.1 12.9 %collective-permute-start.3 = (bf16[16,64,512]{2,1,0:T(8,128)(2,1)S(1)}, bf16[16,64,512]{2,1,0:T(8,128)(2,1)S(1)}, u32[]{:S(2)}, u32[]{:S(2)}) collective-permute-start(bf16[16,64,512]{2,1,0:T(8,128)(2,1)S(1)} %all-to-all-done.mine), channel_id=1, source_target_pairs={{0,1},{1,0},{2,3},{3,2},{4,5},{5,4},{6,7},{7,6},{8,9},{9,8},{10,11... | collective-permute-start | bytes 3145736 | tf_op jit(solution)/shard_map/ppermute | solution.py:428
  30.6 8.0 %collective-permute-start.4 = (bf16[64,2048]{1,0:T(8,128)(2,1)S(1)}, bf16[64,2048]{1,0:T(8,128)(2,1)S(1)}, u32[]{:S(2)}, u32[]{:S(2)}) collective-permute-start(bf16[64,2048]{1,0:T(8,128)(2,1)S(1)} %collective-permute-done.2.refs_1_), channel_id=1, source_target_pairs={{0,32},{1,225},{2,34},{3,227},{4,36},{5,229},{6,38},{7,231},{8,40}... | collective-permute-start | bytes 786440 | tf_op jit(solution)/shard_map/ppermute | solution.py:423
  34.5 10.2 %collective-permute-start.6 = (bf16[32,2048]{1,0:T(8,128)(2,1)S(1)}, bf16[32,2048]{1,0:T(8,128)(2,1)S(1)}, u32[]{:S(2)}, u32[]{:S(2)}) collective-permute-start(bf16[32,2048]{1,0:T(8,128)(2,1)S(1)} %slice.33), channel_id=1, source_target_pairs={{0,1},{1,0},{2,3},{3,2},{4,5},{5,4},{6,7},{7,6},{8,9},{9,8},{10,11... | collective-permute-start | bytes 393224 | tf_op jit(solution)/shard_map/ppermute | solution.py:425
  34.6 10.1 %collective-permute-start.7 = (bf16[32,2048]{1,0:T(8,128)(2,1)S(1)}, bf16[32,2048]{1,0:T(8,128)(2,1)S(1)}, u32[]{:S(2)}, u32[]{:S(2)}) collective-permute-start(bf16[32,2048]{1,0:T(8,128)(2,1)S(1)} %slice.34), channel_id=1, source_target_pairs={{0,1},{1,0},{2,3},{3,2},{4,5},{5,4},{6,7},{7,6},{8,9},{9,8},{10,11... | collective-permute-start | bytes 393224 | tf_op jit(solution)/shard_map/ppermute | solution.py:425
  38.7 6.0 %collective-permute-start.8 = (bf16[32,2048]{1,0:T(8,128)(2,1)S(1)}, bf16[32,2048]{1,0:T(8,128)(2,1)S(1)}, u32[]{:S(2)}, u32[]{:S(2)}) collective-permute-start(bf16[32,2048]{1,0:T(8,128)(2,1)S(1)} %get-tuple-element.80), channel_id=1, source_target_pairs={{0,1},{1,0},{2,3},{3,2},{4,5},{5,4},{6,7},{7,6},{8,9},{9,8},{10,11... | collective-permute-start | bytes 393224 | tf_op jit(solution)/shard_map/ppermute | solution.py:425
  39.1 5.6 %collective-permute-start.5 = (bf16[32,2048]{1,0:T(8,128)(2,1)S(1)}, bf16[32,2048]{1,0:T(8,128)(2,1)S(1)}, u32[]{:S(2)}, u32[]{:S(2)}) collective-permute-start(bf16[32,2048]{1,0:T(8,128)(2,1)S(1)} %get-tuple-element.81), channel_id=1, source_target_pairs={{0,32},{1,225},{2,34},{3,227},{4,36},{5,229},{6,38},{7,231},{8,40}... | collective-permute-start | bytes 393224 | tf_op jit(solution)/shard_map/ppermute | solution.py:423
  41.0 6.7 %collective-permute-start.9 = (bf16[64,2048]{1,0:T(8,128)(2,1)S(1)}, bf16[64,2048]{1,0:T(8,128)(2,1)S(1)}, u32[]{:S(2)}, u32[]{:S(2)}) collective-permute-start(bf16[64,2048]{1,0:T(8,128)(2,1)S(1)} %get-tuple-element.48), channel_id=1, source_target_pairs={{0,32},{1,225},{2,34},{3,227},{4,36},{5,229},{6,38},{7,231},{8,40}... | collective-permute-start | bytes 786440 | tf_op jit(solution)/shard_map/ppermute | solution.py:431
  47.8 15.8 %collective-permute-start.10 = (bf16[64,2048]{1,0:T(8,128)(2,1)S(1)}, bf16[64,2048]{1,0:T(8,128)(2,1)S(1)}, u32[]{:S(2)}, u32[]{:S(2)}) collective-permute-start(bf16[64,2048]{1,0:T(8,128)(2,1)S(1)} %collective-permute-done.9.refs_0_), channel_id=1, source_target_pairs={{0,32},{1,225},{2,34},{3,227},{4,36},{5,229},{6,38},{7,231},{8,40}... | collective-permute-start | bytes 786440 | tf_op jit(solution)/shard_map/ppermute | solution.py:508
  49.4 14.2 %collective-permute-start.11 = (bf16[32,2048]{1,0:T(8,128)(2,1)S(1)}, bf16[32,2048]{1,0:T(8,128)(2,1)S(1)}, u32[]{:S(2)}, u32[]{:S(2)}) collective-permute-start(bf16[32,2048]{1,0:T(8,128)(2,1)S(1)} %slice.28), channel_id=1, source_target_pairs={{0,1},{1,0},{2,3},{3,2},{4,5},{5,4},{6,7},{7,6},{8,9},{9,8},{10,11... | collective-permute-start | bytes 393224 | tf_op jit(solution)/shard_map/ppermute | solution.py:506
  63.6 18.5 %collective-permute-start.12 = (bf16[64,2048]{1,0:T(8,128)(2,1)S(1)}, bf16[64,2048]{1,0:T(8,128)(2,1)S(1)}, u32[]{:S(2)}, u32[]{:S(2)}) collective-permute-start(bf16[64,2048]{1,0:T(8,128)(2,1)S(1)} %collective-permute-done.10.refs_1_), channel_id=1, source_target_pairs={{0,32},{1,225},{2,34},{3,227},{4,36},{5,229},{6,38},{7,231},{8,40}... | collective-permute-start | bytes 786440 | tf_op jit(solution)/shard_map/ppermute | solution.py:508
  63.7 18.4 %collective-permute-start.13 = (bf16[32,2048]{1,0:T(8,128)(2,1)S(1)}, bf16[32,2048]{1,0:T(8,128)(2,1)S(1)}, u32[]{:S(2)}, u32[]{:S(2)}) collective-permute-start(bf16[32,2048]{1,0:T(8,128)(2,1)S(1)} %slice.29), channel_id=1, source_target_pairs={{0,1},{1,0},{2,3},{3,2},{4,5},{5,4},{6,7},{7,6},{8,9},{9,8},{10,11... | collective-permute-start | bytes 393224 | tf_op jit(solution)/shard_map/ppermute | solution.py:506
  82.1 14.2 %collective-permute-start.15 = (bf16[32,2048]{1,0:T(8,128)(2,1)S(1)}, bf16[32,2048]{1,0:T(8,128)(2,1)S(1)}, u32[]{:S(2)}, u32[]{:S(2)}) collective-permute-start(bf16[32,2048]{1,0:T(8,128)(2,1)S(1)} %get-tuple-element.78), channel_id=1, source_target_pairs={{0,1},{1,0},{2,3},{3,2},{4,5},{5,4},{6,7},{7,6},{8,9},{9,8},{10,11... | collective-permute-start | bytes 393224 | tf_op jit(solution)/shard_map/ppermute | solution.py:506
  82.6 13.7 %collective-permute-start.14 = (bf16[32,2048]{1,0:T(8,128)(2,1)S(1)}, bf16[32,2048]{1,0:T(8,128)(2,1)S(1)}, u32[]{:S(2)}, u32[]{:S(2)}) collective-permute-start(bf16[32,2048]{1,0:T(8,128)(2,1)S(1)} %get-tuple-element.79), channel_id=1, source_target_pairs={{0,32},{1,225},{2,34},{3,227},{4,36},{5,229},{6,38},{7,231},{8,40}... | collective-permute-start | bytes 393224 | tf_op jit(solution)/shard_map/ppermute | solution.py:508
  94.6 22.1 %copy-start.1 = (s32[256]{0:T(256)S(1)}, s32[256]{0:T(256)}, u32[]{:S(2)}) copy-start(s32[256]{0:T(256)} %param.14) | copy-start | bytes 3076
  108.9 31.8 %copy-start.2 = (s32[8]{0:T(128)S(1)}, s32[8]{0:T(128)}, u32[]{:S(2)}) copy-start(s32[8]{0:T(128)} %counts.1) | copy-start | bytes 100
  112.3 43.0 %copy-start = (bf16[16,128,256]{2,1,0:T(8,128)(2,1)S(1)}, bf16[16,128,256]{2,1,0:T(8,128)(2,1)}, u32[]{:S(2)}) copy-start(bf16[16,128,256]{2,1,0:T(8,128)(2,1)} %get-tuple-element.65) | copy-start | bytes 3145732
  112.3 11.3 %all-to-all-start.5 = ((f32[8,16,128]{2,1,0:T(8,128)}), f32[8,16,128]{2,1,0:T(8,128)}, u32[]{:S(2)}, u32[]{:S(2)}) async-start(f32[8,16,128]{2,1,0:T(8,128)} %get-tuple-element.64), calls=%async_computation.5 | async-start | bytes 131072 | tf_op jit(solution)/shard_map/all_to_all | solution.py:367
  126.9 3.0 %collective-permute-start.16 = (f32[128,640]{1,0:T(8,128)S(1)}, f32[128,640]{1,0:T(8,128)S(1)}, u32[]{:S(2)}, u32[]{:S(2)}) collective-permute-start(f32[128,640]{1,0:T(8,128)S(1)} %get-tuple-element.75), channel_id=1, source_target_pairs={{0,1},{1,0},{2,3},{3,2},{4,5},{5,4},{6,7},{7,6},{8,9},{9,8},{10,11... | collective-permute-start | bytes 983048 | tf_op jit(solution)/shard_map/ppermute | solution.py:580
